TPU v7x, 256 devices: a whole 4x4x8 slice. The times are simulated.
256 devices in a mesh: blk: 8 (over y, x_hi), rep: 32 (over x_lo, z, core).
Axes of the slice: x: 4 (x_hi: 2, x_lo: 2; x = x_hi * 2 + x_lo), y: 4, z: 8, core: 2. Of those that a mesh axis runs over, the one named last changes fastest.
Arguments:
- node_feats: bfloat16 [98304, 128], P(('blk', 'rep')), may hold values from -6 to 6
- block_vals: bfloat16 [8, 32, 8, 40, 128, 128], P('blk', 'rep'), may hold values from 0.00049972534 to 0.049804688
- block_rows: int32 [8, 32, 8, 40], P('blk', 'rep'), may hold values from 0 to 95
- block_cols: int32 [8, 32, 8, 40], P('blk', 'rep'), may hold values from 0 to 2
- block_count: int32 [8, 32, 8], P('blk', 'rep'), may hold values from 1 to 40, as said below
- weight: bfloat16 [128, 256], replicated, may hold values from -0.5 to 0.5
Outputs:
- layer_out: bfloat16 [98304, 256], P(('blk', 'rep'))
Inputs may be any that keep to these rules, and one draw needn't show every extreme that they name: Only the first block_count[b, r, j] slots of list (b, r, j) are live; the values, rows and columns of later slots are ignored. The largest count 40 is reached in every draw.
All inputs are finite; a program needn't handle non-finite values.
Results may differ from a plain program's by a relative error of at most 0.0011.
Values may be sent and summed in bfloat16 or wider, within the bound.
No kernel may reach another device: no remote copies, remote signals or barrier semaphores. Data moves between devices by JAX's collectives and lax.ppermute only.
A program may use at most 128 MiB of HBM per device.

v0:
```python
import functools

import jax
import jax.numpy as jnp
from jax import lax
from jax.experimental import pallas as pl
from jax.experimental.pallas import tpu as pltpu
from jax.sharding import PartitionSpec as P

BS = 128
F = 128
H = 256
SLOTS = 40
LISTS = 8
PIECE_BLK = 3
PIECE_ROWS = PIECE_BLK * BS
HALF = PIECE_ROWS // 2
PANEL_BLK = 96
GROUP = 8
GROUPS = SLOTS // GROUP
TOP = 32766.0
MIB = 1 << 20

FIRST, SECOND = (0, 2), (2, 1)


def message_rows(blocks):
    return blocks * BS + 16


SMEM = pl.BlockSpec(memory_space=pltpu.SMEM)
VMEM = pl.BlockSpec(memory_space=pltpu.VMEM)
ANY = pl.BlockSpec(memory_space=pl.ANY)


def call(kernel, name, out_shape, in_specs, out_specs, args, us, mib=24, **more):
    return pl.pallas_call(
        kernel,
        out_shape=out_shape,
        in_specs=in_specs,
        out_specs=out_specs,
        compiler_params=pltpu.CompilerParams(vmem_limit_bytes=mib * MIB),
        cost_estimate=pl.CostEstimate(flops=0, bytes_accessed=int(us * 3.0e6), transcendentals=0),
        name=name,
        **more,
    )(*args)


def groups_of(count):
    return lax.div(jnp.clip(count, 0, SLOTS) + (GROUP - 1), GROUP)


def add_list(panel, piece, vals, count_ref, rows_ref, cols_ref, j, before=None):
    count = count_ref[0, j]

    @pl.loop(0, groups_of(count))
    def _(g):
        if before is not None:
            before(g)
        for half in range(2):
            products, rows = [], []
            for u in range(half * GROUP // 2, (half + 1) * GROUP // 2):
                q = g * GROUP + u
                live = q < count
                rows.append(jnp.where(live, rows_ref[j, q], PANEL_BLK))
                col = jnp.where(live, cols_ref[j, q], 0)
                products.append(
                    jnp.dot(
                        vals[j * SLOTS + q],
                        piece[pl.ds(pl.multiple_of(col * BS, BS), BS), :],
                        preferred_element_type=jnp.float32,
                    )
                )
            for row, product in zip(rows, products):
                panel[row] += product


def piece_of(place_ref, shift, flip):
    x_hi = place_ref[1]
    return lax.rem(place_ref[0] + shift, 4) * 2 + (1 - x_hi if flip else x_hi)


def first_products(place_ref, count_ref, rows_ref, cols_ref, own_ref, vals_ref, panel, vals, sems):
    def copy(j, g):
        base = pl.multiple_of(j * SLOTS + g * GROUP, GROUP)
        return pltpu.make_async_copy(
            vals_ref.at[pl.ds(base, GROUP)], vals.at[pl.ds(base, GROUP)], sems.at[j * GROUPS + g]
        )

    mine = piece_of(place_ref, 0, False)

    @pl.loop(0, LISTS)
    def _(k):
        j = lax.rem(mine + k, LISTS)

        @pl.loop(0, groups_of(count_ref[0, j]))
        def _(g):
            copy(j, g).start()

    @pl.loop(0, PANEL_BLK)
    def _(k):
        panel[k] = jnp.zeros((BS, F), jnp.float32)

    add_list(panel, own_ref, vals, count_ref, rows_ref, cols_ref, mine, lambda g: copy(mine, g).wait())

    @pl.loop(1, LISTS)
    def _(k):
        j = lax.rem(mine + k, LISTS)

        @pl.loop(0, groups_of(count_ref[0, j]))
        def _(g):
            copy(j, g).wait()


def more_products(pieces, split, *refs):
    place_ref, count_ref, rows_ref, cols_ref = refs[:4]
    vals = refs[5]
    panel = refs[6 + len(pieces) + 2 * len(split)]
    for (shift, flip), piece in zip(pieces, refs[6:]):
        add_list(panel, piece, vals, count_ref, rows_ref, cols_ref, piece_of(place_ref, shift, flip))
    if split:
        whole = refs[-1]
        rest = refs[6 + len(pieces) :]
        for i, (shift, flip) in enumerate(split):
            whole[:HALF, :] = rest[2 * i][...]
            whole[HALF:, :] = rest[2 * i + 1][...]
            add_list(panel, whole, vals, count_ref, rows_ref, cols_ref, piece_of(place_ref, shift, flip))


def quantize(block):
    peak = jnp.maximum(jnp.max(jnp.abs(block), axis=0, keepdims=True), 1e-32)
    exponent = jnp.ceil(jnp.log2(peak) + 0.001)
    scaled = block * (jnp.exp2(-exponent) * TOP)
    return jnp.round(scaled).astype(jnp.int32).astype(jnp.int16), exponent


def write_message(out_ref, index, blocks):
    count = len(blocks)
    row = lax.broadcasted_iota(jnp.int32, (16, F), 0)
    tail = jnp.zeros((16, F), jnp.float32)
    for i, block in enumerate(blocks):
        whole, exponent = quantize(block)
        out_ref[index, i * BS : (i + 1) * BS, :] = whole
        tail = jnp.where(row == i, exponent, tail)
    out_ref[index, count * BS : count * BS + 16, :] = tail.astype(jnp.int32).astype(jnp.int16)


def read_message(ref, index, count):
    tail = ref[index, count * BS : count * BS + 16, :].astype(jnp.int32).astype(jnp.float32)
    size = jnp.exp2(tail) * (1.0 / TOP)
    blocks = []
    for i in range(count):
        whole = ref[index, i * BS : (i + 1) * BS, :].astype(jnp.int32).astype(jnp.float32)
        blocks.append(whole * size[i : i + 1, :])
    return blocks


def add(first, *others):
    for other in others:
        first = [a + b for a, b in zip(first, other)]
    return first


class Here:
    def __init__(self, place_ref, panel=None):
        self.core, self.x, self.z = place_ref[2], place_ref[3], place_ref[4]
        self.panel = panel

    def x_of(self, other):
        return 1 - self.x if other else self.x

    def z_of(self, shift):
        return lax.rem(self.z + shift + 8, 8)

    def partial(self, other_x, z, part, other_core=False):
        core = 1 - self.core if other_core else self.core
        owner = self.x_of(other_x) * 16 + z * 2 + core
        return [self.panel[owner * PIECE_BLK + part[0] + i] for i in range(part[1])]


def core_messages(part, other_x, place_ref, panel, out_ref):
    here = Here(place_ref, panel)
    for k, other in enumerate(other_x):

        @pl.loop(0, 8)
        def _(z):
            write_message(out_ref, k * 8 + z, here.partial(other, z, part, other_core=True))


def last_products(pieces, split, *refs):
    more_products(pieces, split, *refs[:-2], refs[-1])
    core_messages(FIRST, (True,), refs[0], refs[-3], refs[-2])


def x_messages(place_ref, panel, rc_ref, out_ref):
    here = Here(place_ref, panel)

    @pl.loop(0, 8)
    def _(z):
        write_message(out_ref, z, add(here.partial(True, z, FIRST), read_message(rc_ref, z, FIRST[1])))


def base_value(part, here, rc_ref, rx_ref, other, z):
    if part == FIRST:
        return add(
            here.partial(other, z, part), read_message(rc_ref, z, part[1]), read_message(rx_ref, z, part[1])
        )
    return add(here.partial(other, z, part), read_message(rc_ref, other * 8 + z, part[1]))


def sides(part):
    return (0,) if part == FIRST else (0, 1)


def z_start(part, place_ref, panel, rc_ref, rx_ref, down_ref, up_ref):
    here = Here(place_ref, panel)
    for other in sides(part):
        for k, shift in enumerate((-4, -2)):
            write_message(
                down_ref, 2 * other + k, base_value(part, here, rc_ref, rx_ref, other, here.z_of(shift))
            )
        write_message(up_ref, other, base_value(part, here, rc_ref, rx_ref, other, here.z_of(2)))


def z_middle(part, place_ref, panel, rc_ref, rx_ref, down_ref, up_ref, three_ref, one_ref, back_ref, far_ref):
    here = Here(place_ref, panel)
    count = part[1]
    for other in sides(part):
        value = functools.partial(base_value, part, here, rc_ref, rx_ref, other)
        write_message(
            three_ref, other, add(value(here.z_of(-3)), read_message(down_ref, 2 * other, count))
        )
        write_message(far_ref, other, value(here.z_of(3)))
        write_message(
            one_ref, other, add(value(here.z_of(-1)), read_message(down_ref, 2 * other + 1, count))
        )
        write_message(back_ref, other, add(value(here.z_of(1)), read_message(up_ref, other, count)))


def z_end(place_ref, panel, rc_ref, *refs):
    here = Here(place_ref, panel)
    value = base_value(SECOND, here, rc_ref, None, 1, here.z)
    write_message(refs[4], 0, add(value, *[read_message(ref, 1, SECOND[1]) for ref in refs[:4]]))


def layer(place_ref, panel, rc1_ref, rx1_ref, rc2_ref, rx2_ref, *refs):
    here = Here(place_ref, panel)
    weight_ref, out_ref = refs[8], refs[9]
    first = base_value(FIRST, here, rc1_ref, rx1_ref, 0, here.z)
    first = add(first, *[read_message(ref, 0, FIRST[1]) for ref in refs[:4]])
    second = base_value(SECOND, here, rc2_ref, None, 0, here.z)
    second = add(second, read_message(rx2_ref, 0, 1), *[read_message(ref, 0, SECOND[1]) for ref in refs[4:8]])
    weight = weight_ref[...]
    for i, block in enumerate(first + second):
        high = block.astype(jnp.bfloat16)
        rest = block - high.astype(jnp.float32)
        middle = rest.astype(jnp.bfloat16)
        low = (rest - middle.astype(jnp.float32)).astype(jnp.bfloat16)
        result = jnp.dot(low, weight, preferred_element_type=jnp.float32)
        result += jnp.dot(middle, weight, preferred_element_type=jnp.float32)
        result += jnp.dot(high, weight, preferred_element_type=jnp.float32)
        out_ref[i * BS : (i + 1) * BS, :] = jnp.maximum(result, 0.0).astype(jnp.bfloat16)


def messages(count, part):
    return jax.ShapeDtypeStruct((count, message_rows(part[1]), F), jnp.int16)


def send_blk(array, dy, flip=0):
    pairs = [(y * 2 + h, ((y + dy) % 4) * 2 + (h ^ flip)) for y in range(4) for h in range(2)]
    return lax.ppermute(array, "blk", pairs)


def send_rep(array, dx, dz, dc):
    pairs = [
        (x * 16 + z * 2 + c, (x ^ dx) * 16 + ((z + dz) % 8) * 2 + (c ^ dc))
        for x in range(2) for z in range(8) for c in range(2)
    ]
    return lax.ppermute(array, "rep", pairs)


def sum_along_z(part, name, place, panel, rc, rx, also=None):
    count = len(sides(part))
    have = (rc,) if rx is None else (rc, rx)

    def fill(kernel):
        if rx is not None:
            return functools.partial(kernel, part)
        return lambda place_ref, panel_ref, rc_ref, *refs: kernel(part, place_ref, panel_ref, rc_ref, None, *refs)

    down, up = call(
        fill(z_start), name + "_start", (messages(2 * count, part), messages(count, part)),
        [SMEM] + [VMEM] * (1 + len(have)), (VMEM, VMEM), (place, panel, *have), 0.6,
    )
    down, up = send_rep(down, 0, -1, 0), send_rep(up, 0, 1, 0)
    down, also = lax.optimization_barrier((down, also))
    three, one, back, far = call(
        fill(z_middle), name + "_middle", (messages(count, part),) * 4,
        [SMEM] + [VMEM] * (3 + len(have)), (VMEM,) * 4, (place, panel, *have, down, up), 0.6,
    )
    arrived = send_rep(three, 0, -3, 0), send_rep(far, 0, 3, 0), send_rep(one, 0, -1, 0), send_rep(back, 0, 1, 0)
    return arrived, also


def local(node_feats, block_vals, block_rows, block_cols, block_count, weight):
    blk = lax.axis_index("blk")
    rep = lax.axis_index("rep")
    place = jnp.stack([blk // 2, blk % 2, rep % 2, rep // 16, (rep // 2) % 8]).astype(jnp.int32)
    lists = (place, block_count.reshape(1, LISTS), block_rows.reshape(LISTS, SLOTS), block_cols.reshape(LISTS, SLOTS))
    panel_type = jax.ShapeDtypeStruct((PANEL_BLK + 1, BS, F), jnp.float32)
    vals_type = jax.ShapeDtypeStruct((LISTS * SLOTS, BS, BS), jnp.bfloat16)
    piece_buffer = pltpu.VMEM((PIECE_ROWS, F), jnp.bfloat16)

    own = node_feats
    flipped, below, above = send_blk(own, 0, 1), send_blk(own, 1), send_blk(own, -1)
    panel, vals = call(
        first_products, "products_own", (panel_type, vals_type), [SMEM] * 4 + [VMEM, ANY], (VMEM, VMEM),
        (*lists, own, block_vals.reshape(LISTS * SLOTS, BS, BS)), 5, 40,
        scratch_shapes=[pltpu.SemaphoreType.DMA((LISTS * GROUPS,))],
    )

    def add_pieces(panel, name, which, arrays, split=(), kernel=more_products, extra=()):
        return call(
            functools.partial(kernel, which, split), name, (panel_type, *extra),
            [SMEM] * 4 + [VMEM] * (2 + len(arrays)), (VMEM,) * (1 + len(extra)), (*lists, panel, vals, *arrays), 3, 40,
            input_output_aliases={4: 0},
            scratch_shapes=[piece_buffer] if split else [],
        )

    panel, flipped, below, above = lax.optimization_barrier((panel, flipped, below, above))
    below_flipped, above_flipped = send_blk(flipped, 1), send_blk(flipped, -1)
    far = send_blk(below[:HALF], 1), send_blk(above[HALF:], -1)
    (panel,) = add_pieces(
        panel, "products_near", ((0, True), (3, False), (1, False)), (flipped, below, above)
    )
    panel, below_flipped, above_flipped = lax.optimization_barrier((panel, below_flipped, above_flipped))
    far_flipped = send_blk(below_flipped[:HALF], 1), send_blk(above_flipped[HALF:], -1)
    (panel,) = add_pieces(
        panel, "products_near_flipped", ((3, True), (1, True)), (below_flipped, above_flipped, *far), ((2, False),)
    )
    panel, to_core = add_pieces(
        panel, "products_far", (), far_flipped, ((2, True),), last_products, (messages(8, FIRST),)
    )

    def to_other_core(name, part, other_x):
        return call(
            functools.partial(core_messages, part, other_x), name, messages(8 * len(other_x), part),
            [SMEM, VMEM], VMEM, (place, panel), 0.6,
        )

    rc_cross = send_rep(to_core, 0, 0, 1)
    rc_second = send_rep(to_other_core("core_second", SECOND, (False, True)), 0, 0, 1)
    rc_first = send_rep(to_other_core("core_first", FIRST, (False,)), 0, 0, 1)
    to_x = call(x_messages, "x_first", messages(8, FIRST), [SMEM, VMEM, VMEM], VMEM, (place, panel, rc_cross), 0.6)
    rx_first = send_rep(to_x, 1, 0, 0)
    second, rc_first = sum_along_z(SECOND, "second", place, panel, rc_second, None, rc_first)
    to_x = call(
        z_end, "x_second", messages(1, SECOND), [SMEM] + [VMEM] * 6, VMEM, (place, panel, rc_second, *second), 0.6
    )
    panel, to_x = lax.optimization_barrier((panel, to_x))
    rx_second = send_rep(to_x, 1, 0, 0)
    first, _ = sum_along_z(FIRST, "first", place, panel, rc_first, rx_first)
    return call(
        layer, "layer", jax.ShapeDtypeStruct((PIECE_ROWS, H), jnp.bfloat16), [SMEM] + [VMEM] * 14, VMEM,
        (place, panel, rc_first, rx_first, rc_second, rx_second, *first, *second, weight), 1.5,
    )


def solution(mesh):
    return jax.shard_map(
        local,
        mesh=mesh,
        in_specs=(
            P(("blk", "rep"), None),
            P("blk", "rep", None, None, None, None),
            P("blk", "rep", None, None),
            P("blk", "rep", None, None),
            P("blk", "rep", None),
            P(),
        ),
        out_specs=P(("blk", "rep"), None),
        check_vma=False,
    )
```

profile of v0, /device:TPU:2, one launch (start us, length us, event | category | flops | bytes accessed | tf_op | source)
XLA Modules:
  0.0 93.9 jit_solution(9069663243938423376)
XLA Ops:
  0.0 2.1 %collective-permute-start = (bf16[384,128]{1,0:T(8,128)(2,1)}, bf16[384,128]{1,0:T(8,128)(2,1)S(1)}, u32[]{:S(2)}, u32[]{:S(2)}) collective-permute-start(bf16[384,128]{1,0:T(8,128)(2,1)} %own_ref.1), channel_id=1, source_target_pairs={{0,32},{32,0},{64,96},{96,64},{128,160},{160,128},{192,224},{224,1... | collective-permute-start | bytes 294920 | tf_op jit(solution)/shard_map/ppermute | solution.py:271
  2.1 3.0 %collective-permute-start.2 = (bf16[384,128]{1,0:T(8,128)(2,1)}, bf16[384,128]{1,0:T(8,128)(2,1)S(1)}, u32[]{:S(2)}, u32[]{:S(2)}) collective-permute-start(bf16[384,128]{1,0:T(8,128)(2,1)} %own_ref.1), channel_id=1, source_target_pairs={{0,192},{32,224},{64,0},{96,32},{128,64},{160,96},{192,128},{224,1... | collective-permute-start | bytes 294920 | tf_op jit(solution)/shard_map/ppermute | solution.py:271
  8.2 7.2 %products_own.1 = (f32[97,128,128]{2,1,0:T(8,128)S(1)}, bf16[320,128,128]{2,1,0:T(8,128)(2,1)}) custom-call(s32[5]{0:T(128)S(1)} %stack.23.place_ref.refs_0_, s32[1,8]{1,0:T(1,128)S(1)} %bitcast.17, s32[8,40]{1,0:T(8,128)S(1)} %bitcast.9, s32[8,40]{1,0:T(8,128)S(1)} %bitcast.13, bf16[384,128]{1,0:T(8,128)(2,1)S(1)} %copy-done, bf16[320,128,128]{2,1,0:T(8,128)(2,1)} %bitcast.21), custom_call_target="tpu_custom_call" | custom-call | bytes 15000000 | tf_op jit(solution)/shard_map/products_own/pallas_call | solution.py:37
  15.4 3.5 %collective-permute-start.4 = (bf16[384,128]{1,0:T(8,128)(2,1)S(1)}, bf16[384,128]{1,0:T(8,128)(2,1)S(1)}, u32[]{:S(2)}, u32[]{:S(2)}) collective-permute-start(bf16[384,128]{1,0:T(8,128)(2,1)S(1)} %collective-permute-done.refs_6_), channel_id=1, source_target_pairs={{0,192},{32,224},{64,0},{96,32},{128,64},{160,96},{192,128},{224,1... | collective-permute-start | bytes 294920 | tf_op jit(solution)/shard_map/ppermute | solution.py:271
  19.0 3.3 %collective-permute-start.6 = (bf16[192,128]{1,0:T(8,128)(2,1)S(1)}, bf16[192,128]{1,0:T(8,128)(2,1)S(1)}, u32[]{:S(2)}, u32[]{:S(2)}) collective-permute-start(bf16[192,128]{1,0:T(8,128)(2,1)S(1)} %slice.13), channel_id=1, source_target_pairs={{0,192},{32,224},{64,0},{96,32},{128,64},{160,96},{192,128},{224,1... | collective-permute-start | bytes 147464 | tf_op jit(solution)/shard_map/ppermute | solution.py:271
  22.3 5.0 %products_near.1.refs_4_ = f32[97,128,128]{2,1,0:T(8,128)S(1)} custom-call(s32[5]{0:T(128)S(1)} %stack.23.place_ref.refs_0_, s32[1,8]{1,0:T(1,128)S(1)} %bitcast.18, s32[8,40]{1,0:T(8,128)S(1)} %bitcast.10, s32[8,40]{1,0:T(8,128)S(1)} %bitcast.14, f32[97,128,128]{2,1,0:T(8,128)S(1)} %get-tuple-element.33.refs_4_, ...), custom_call_target="tpu_custom_call", output_to_operand_aliasing={{}: (4, {})} | custom-call | bytes 9000000 | tf_op jit(solution)/shard_map/products_near/pallas_call | solution.py:37
  27.4 3.2 %collective-permute-start.8 = (bf16[192,128]{1,0:T(8,128)(2,1)S(1)}, bf16[192,128]{1,0:T(8,128)(2,1)S(1)}, u32[]{:S(2)}, u32[]{:S(2)}) collective-permute-start(bf16[192,128]{1,0:T(8,128)(2,1)S(1)} %slice.15), channel_id=1, source_target_pairs={{0,192},{32,224},{64,0},{96,32},{128,64},{160,96},{192,128},{224,1... | collective-permute-start | bytes 147464 | tf_op jit(solution)/shard_map/ppermute | solution.py:271
  30.6 5.9 %products_near_flipped.1.refs_4_ = f32[97,128,128]{2,1,0:T(8,128)S(1)} custom-call(s32[5]{0:T(128)S(1)} %stack.23.place_ref.refs_0_, s32[1,8]{1,0:T(1,128)S(1)} %bitcast.19, s32[8,40]{1,0:T(8,128)S(1)} %bitcast.11, s32[8,40]{1,0:T(8,128)S(1)} %bitcast.15, f32[97,128,128]{2,1,0:T(8,128)S(1)} %products_near.1.refs_4_, ...), custom_call_target="tpu_custom_call", output_to_operand_aliasing={{}: (4, {})} | custom-call | bytes 9000000 | tf_op jit(solution)/shard_map/products_near_flipped/pallas_call | solution.py:37
  36.6 4.9 %products_far.1 = (f32[97,128,128]{2,1,0:T(8,128)S(1)}, s16[8,272,128]{2,1,0:T(8,128)(2,1)S(1)}) custom-call(s32[5]{0:T(128)S(1)} %stack.23.place_ref.refs_0_, s32[1,8]{1,0:T(1,128)S(1)} %bitcast.20, s32[8,40]{1,0:T(8,128)S(1)} %bitcast.12, s32[8,40]{1,0:T(8,128)S(1)} %bitcast.16, ...), custom_call_target="tpu_custom_call", output_to_operand_aliasing={{0}: (4, {})} | custom-call | bytes 9000000 | tf_op jit(solution)/shard_map/products_far/pallas_call | solution.py:37
  46.2 7.1 %collective-permute-start.10 = (s16[4,144,128]{2,1,0:T(8,128)(2,1)S(1)}, s16[4,144,128]{2,1,0:T(8,128)(2,1)S(1)}, u32[]{:S(2)}, u32[]{:S(2)}) collective-permute-start(s16[4,144,128]{2,1,0:T(8,128)(2,1)S(1)} %get-tuple-element.42), channel_id=1, source_target_pairs={{0,14},{1,15},{2,0},{3,1},{4,2},{5,3},{6,4},{7,5},{8,6},{9,7},{10,... | collective-permute-start | bytes 442376 | tf_op jit(solution)/shard_map/ppermute | solution.py:279
  53.4 3.5 %collective-permute-done.10.refs_0_ = s16[4,144,128]{2,1,0:T(8,128)(2,1)S(1)} collective-permute-done((s16[4,144,128]{2,1,0:T(8,128)(2,1)S(1)}, s16[4,144,128]{2,1,0:T(8,128)(2,1)S(1)}, u32[]{:S(2)}, u32[]{:S(2)}) %collective-permute-start.10) | collective-permute-done | bytes 147488 | tf_op jit(solution)/shard_map/ppermute | solution.py:279
  56.8 2.1 %collective-permute-done.12.refs_1_ = s16[2,144,128]{2,1,0:T(8,128)(2,1)S(1)} collective-permute-done((s16[2,144,128]{2,1,0:T(8,128)(2,1)S(1)}, s16[2,144,128]{2,1,0:T(8,128)(2,1)S(1)}, u32[]{:S(2)}, u32[]{:S(2)}) %collective-permute-start.12) | collective-permute-done | bytes 73760 | tf_op jit(solution)/shard_map/ppermute | solution.py:279
  59.7 2.8 %collective-permute-start.13 = (s16[2,144,128]{2,1,0:T(8,128)(2,1)S(1)}, s16[2,144,128]{2,1,0:T(8,128)(2,1)S(1)}, u32[]{:S(2)}, u32[]{:S(2)}) collective-permute-start(s16[2,144,128]{2,1,0:T(8,128)(2,1)S(1)} %get-tuple-element.45), channel_id=1, source_target_pairs={{0,10},{1,11},{2,12},{3,13},{4,14},{5,15},{6,0},{7,1},{8,2},{9,3},... | collective-permute-start | bytes 221192 | tf_op jit(solution)/shard_map/ppermute | solution.py:279
  63.6 2.8 %collective-permute-start.15 = (s16[2,144,128]{2,1,0:T(8,128)(2,1)S(1)}, s16[2,144,128]{2,1,0:T(8,128)(2,1)S(1)}, u32[]{:S(2)}, u32[]{:S(2)}) collective-permute-start(s16[2,144,128]{2,1,0:T(8,128)(2,1)S(1)} %get-tuple-element.47), channel_id=1, source_target_pairs={{0,14},{1,15},{2,0},{3,1},{4,2},{5,3},{6,4},{7,5},{8,6},{9,7},{10,... | collective-permute-start | bytes 221192 | tf_op jit(solution)/shard_map/ppermute | solution.py:279
  66.4 1.4 %collective-permute-done.13.refs_0_.refs_4_ = s16[2,144,128]{2,1,0:T(8,128)(2,1)S(1)} collective-permute-done((s16[2,144,128]{2,1,0:T(8,128)(2,1)S(1)}, s16[2,144,128]{2,1,0:T(8,128)(2,1)S(1)}, u32[]{:S(2)}, u32[]{:S(2)}) %collective-permute-start.13) | collective-permute-done | bytes 73760 | tf_op jit(solution)/shard_map/ppermute | solution.py:279
  67.8 3.4 %collective-permute-done.14.refs_1_.refs_5_ = s16[2,144,128]{2,1,0:T(8,128)(2,1)S(1)} collective-permute-done((s16[2,144,128]{2,1,0:T(8,128)(2,1)S(1)}, s16[2,144,128]{2,1,0:T(8,128)(2,1)S(1)}, u32[]{:S(2)}, u32[]{:S(2)}) %collective-permute-start.14) | collective-permute-done | bytes 73760 | tf_op jit(solution)/shard_map/ppermute | solution.py:279
  71.2 1.3 %collective-permute-done.16.refs_3_.refs_7_ = s16[2,144,128]{2,1,0:T(8,128)(2,1)S(1)} collective-permute-done((s16[2,144,128]{2,1,0:T(8,128)(2,1)S(1)}, s16[2,144,128]{2,1,0:T(8,128)(2,1)S(1)}, u32[]{:S(2)}, u32[]{:S(2)}) %collective-permute-start.16) | collective-permute-done | bytes 73760 | tf_op jit(solution)/shard_map/ppermute | solution.py:279
  74.3 1.7 %collective-permute-start.21 = (s16[1,272,128]{2,1,0:T(8,128)(2,1)S(1)}, s16[1,272,128]{2,1,0:T(8,128)(2,1)S(1)}, u32[]{:S(2)}, u32[]{:S(2)}) collective-permute-start(s16[1,272,128]{2,1,0:T(8,128)(2,1)S(1)} %get-tuple-element.54), channel_id=1, source_target_pairs={{0,2},{1,3},{2,4},{3,5},{4,6},{5,7},{6,8},{7,9},{8,10},{9,11},{10,... | collective-permute-start | bytes 208904 | tf_op jit(solution)/shard_map/ppermute | solution.py:279
  76.0 3.2 %collective-permute-done.20.down_ref = s16[2,272,128]{2,1,0:T(8,128)(2,1)S(1)} collective-permute-done((s16[2,272,128]{2,1,0:T(8,128)(2,1)S(1)}, s16[2,272,128]{2,1,0:T(8,128)(2,1)S(1)}, u32[]{:S(2)}, u32[]{:S(2)}) %collective-permute-start.20) | collective-permute-done | bytes 139296 | tf_op jit(solution)/shard_map/ppermute | solution.py:279
  81.3 3.2 %collective-permute-start.23 = (s16[1,272,128]{2,1,0:T(8,128)(2,1)S(1)}, s16[1,272,128]{2,1,0:T(8,128)(2,1)S(1)}, u32[]{:S(2)}, u32[]{:S(2)}) collective-permute-start(s16[1,272,128]{2,1,0:T(8,128)(2,1)S(1)} %get-tuple-element.56), channel_id=1, source_target_pairs={{0,6},{1,7},{2,8},{3,9},{4,10},{5,11},{6,12},{7,13},{8,14},{9,15},... | collective-permute-start | bytes 208904 | tf_op jit(solution)/shard_map/ppermute | solution.py:279
  84.6 2.1 %collective-permute-start.24 = (s16[1,272,128]{2,1,0:T(8,128)(2,1)S(1)}, s16[1,272,128]{2,1,0:T(8,128)(2,1)S(1)}, u32[]{:S(2)}, u32[]{:S(2)}) collective-permute-start(s16[1,272,128]{2,1,0:T(8,128)(2,1)S(1)} %get-tuple-element.57), channel_id=1, source_target_pairs={{0,14},{1,15},{2,0},{3,1},{4,2},{5,3},{6,4},{7,5},{8,6},{9,7},{10,... | collective-permute-start | bytes 208904 | tf_op jit(solution)/shard_map/ppermute | solution.py:279
  87.7 2.9 %collective-permute-done.19.rx2_ref = s16[1,144,128]{2,1,0:T(8,128)(2,1)S(1)} collective-permute-done((s16[1,144,128]{2,1,0:T(8,128)(2,1)S(1)}, s16[1,144,128]{2,1,0:T(8,128)(2,1)S(1)}, u32[]{:S(2)}, u32[]{:S(2)}) %collective-permute-start.19) | collective-permute-done | bytes 36896 | tf_op jit(solution)/shard_map/ppermute | solution.py:279
  90.7 1.5 %collective-permute-done.25.refs_3_ = s16[1,272,128]{2,1,0:T(8,128)(2,1)S(1)} collective-permute-done((s16[1,272,128]{2,1,0:T(8,128)(2,1)S(1)}, s16[1,272,128]{2,1,0:T(8,128)(2,1)S(1)}, u32[]{:S(2)}, u32[]{:S(2)}) %collective-permute-start.25) | collective-permute-done | bytes 69664 | tf_op jit(solution)/shard_map/ppermute | solution.py:279
  92.2 1.6 %layer.1 = bf16[384,256]{1,0:T(8,128)(2,1)} custom-call(s32[5]{0:T(128)S(1)} %stack.23.place_ref.refs_0_, f32[97,128,128]{2,1,0:T(8,128)S(1)} %get-tuple-element.49.panel.panel_ref, s16[8,272,128]{2,1,0:T(8,128)(2,1)S(1)} %collective-permute-done.11.rc_ref.rc1_ref, s16[8,272,128]{2,1,0:T(8,128)(2,1)S(1)} %collective-permute-done.18.rx_ref.rx1_ref, ...), custom_call_target="tpu_custom_call" | custom-call | bytes 4500000 | tf_op jit(solution)/shard_map/layer/pallas_call | solution.py:37
  (56 shorter events, 14.8 us)
Async XLA Ops:
  0.0 15.4 %collective-permute-start = (bf16[384,128]{1,0:T(8,128)(2,1)}, bf16[384,128]{1,0:T(8,128)(2,1)S(1)}, u32[]{:S(2)}, u32[]{:S(2)}) collective-permute-start(bf16[384,128]{1,0:T(8,128)(2,1)} %own_ref.1), channel_id=1, source_target_pairs={{0,32},{32,0},{64,96},{96,64},{128,160},{160,128},{192,224},{224,1... | collective-permute-start | bytes 294920 | tf_op jit(solution)/shard_map/ppermute | solution.py:271
  2.1 13.3 %collective-permute-start.2 = (bf16[384,128]{1,0:T(8,128)(2,1)}, bf16[384,128]{1,0:T(8,128)(2,1)S(1)}, u32[]{:S(2)}, u32[]{:S(2)}) collective-permute-start(bf16[384,128]{1,0:T(8,128)(2,1)} %own_ref.1), channel_id=1, source_target_pairs={{0,192},{32,224},{64,0},{96,32},{128,64},{160,96},{192,128},{224,1... | collective-permute-start | bytes 294920 | tf_op jit(solution)/shard_map/ppermute | solution.py:271
  5.1 10.3 %collective-permute-start.1 = (bf16[384,128]{1,0:T(8,128)(2,1)}, bf16[384,128]{1,0:T(8,128)(2,1)S(1)}, u32[]{:S(2)}, u32[]{:S(2)}) collective-permute-start(bf16[384,128]{1,0:T(8,128)(2,1)} %own_ref.1), channel_id=1, source_target_pairs={{0,64},{32,96},{64,128},{96,160},{128,192},{160,224},{192,0},{224,... | collective-permute-start | bytes 294920 | tf_op jit(solution)/shard_map/ppermute | solution.py:271
  15.4 11.9 %collective-permute-start.4 = (bf16[384,128]{1,0:T(8,128)(2,1)S(1)}, bf16[384,128]{1,0:T(8,128)(2,1)S(1)}, u32[]{:S(2)}, u32[]{:S(2)}) collective-permute-start(bf16[384,128]{1,0:T(8,128)(2,1)S(1)} %collective-permute-done.refs_6_), channel_id=1, source_target_pairs={{0,192},{32,224},{64,0},{96,32},{128,64},{160,96},{192,128},{224,1... | collective-permute-start | bytes 294920 | tf_op jit(solution)/shard_map/ppermute | solution.py:271
  18.9 8.4 %collective-permute-start.3 = (bf16[384,128]{1,0:T(8,128)(2,1)S(1)}, bf16[384,128]{1,0:T(8,128)(2,1)S(1)}, u32[]{:S(2)}, u32[]{:S(2)}) collective-permute-start(bf16[384,128]{1,0:T(8,128)(2,1)S(1)} %collective-permute-done.refs_6_), channel_id=1, source_target_pairs={{0,64},{32,96},{64,128},{96,160},{128,192},{160,224},{192,0},{224,... | collective-permute-start | bytes 294920 | tf_op jit(solution)/shard_map/ppermute | solution.py:271
  18.9 11.8 %collective-permute-start.5 = (bf16[192,128]{1,0:T(8,128)(2,1)S(1)}, bf16[192,128]{1,0:T(8,128)(2,1)S(1)}, u32[]{:S(2)}, u32[]{:S(2)}) collective-permute-start(bf16[192,128]{1,0:T(8,128)(2,1)S(1)} %slice.12), channel_id=1, source_target_pairs={{0,64},{32,96},{64,128},{96,160},{128,192},{160,224},{192,0},{224,... | collective-permute-start | bytes 147464 | tf_op jit(solution)/shard_map/ppermute | solution.py:271
  19.0 11.7 %collective-permute-start.6 = (bf16[192,128]{1,0:T(8,128)(2,1)S(1)}, bf16[192,128]{1,0:T(8,128)(2,1)S(1)}, u32[]{:S(2)}, u32[]{:S(2)}) collective-permute-start(bf16[192,128]{1,0:T(8,128)(2,1)S(1)} %slice.13), channel_id=1, source_target_pairs={{0,192},{32,224},{64,0},{96,32},{128,64},{160,96},{192,128},{224,1... | collective-permute-start | bytes 147464 | tf_op jit(solution)/shard_map/ppermute | solution.py:271
  27.3 9.2 %collective-permute-start.7 = (bf16[192,128]{1,0:T(8,128)(2,1)S(1)}, bf16[192,128]{1,0:T(8,128)(2,1)S(1)}, u32[]{:S(2)}, u32[]{:S(2)}) collective-permute-start(bf16[192,128]{1,0:T(8,128)(2,1)S(1)} %slice.14), channel_id=1, source_target_pairs={{0,64},{32,96},{64,128},{96,160},{128,192},{160,224},{192,0},{224,... | collective-permute-start | bytes 147464 | tf_op jit(solution)/shard_map/ppermute | solution.py:271
  27.4 9.2 %collective-permute-start.8 = (bf16[192,128]{1,0:T(8,128)(2,1)S(1)}, bf16[192,128]{1,0:T(8,128)(2,1)S(1)}, u32[]{:S(2)}, u32[]{:S(2)}) collective-permute-start(bf16[192,128]{1,0:T(8,128)(2,1)S(1)} %slice.15), channel_id=1, source_target_pairs={{0,192},{32,224},{64,0},{96,32},{128,64},{160,96},{192,128},{224,1... | collective-permute-start | bytes 147464 | tf_op jit(solution)/shard_map/ppermute | solution.py:271
  44.3 9.1 %collective-permute-start.11 = (s16[8,272,128]{2,1,0:T(8,128)(2,1)S(1)}, s16[8,272,128]{2,1,0:T(8,128)(2,1)S(1)}, u32[]{:S(2)}, u32[]{:S(2)}) collective-permute-start(s16[8,272,128]{2,1,0:T(8,128)(2,1)S(1)} %core_first.1), channel_id=1, source_target_pairs={{0,1},{1,0},{2,3},{3,2},{4,5},{5,4},{6,7},{7,6},{8,9},{9,8},{10,11... | collective-permute-start | bytes 1671176 | tf_op jit(solution)/shard_map/ppermute | solution.py:279
  45.4 27.7 %collective-permute-start.18 = (s16[8,272,128]{2,1,0:T(8,128)(2,1)S(1)}, s16[8,272,128]{2,1,0:T(8,128)(2,1)S(1)}, u32[]{:S(2)}, u32[]{:S(2)}) collective-permute-start(s16[8,272,128]{2,1,0:T(8,128)(2,1)S(1)} %x_first.1), channel_id=1, source_target_pairs={{0,16},{1,17},{2,18},{3,19},{4,20},{5,21},{6,22},{7,23},{8,24},{9,... | collective-permute-start | bytes 1671176 | tf_op jit(solution)/shard_map/ppermute | solution.py:279
  46.2 10.6 %collective-permute-start.10 = (s16[4,144,128]{2,1,0:T(8,128)(2,1)S(1)}, s16[4,144,128]{2,1,0:T(8,128)(2,1)S(1)}, u32[]{:S(2)}, u32[]{:S(2)}) collective-permute-start(s16[4,144,128]{2,1,0:T(8,128)(2,1)S(1)} %get-tuple-element.42), channel_id=1, source_target_pairs={{0,14},{1,15},{2,0},{3,1},{4,2},{5,3},{6,4},{7,5},{8,6},{9,7},{10,... | collective-permute-start | bytes 442376 | tf_op jit(solution)/shard_map/ppermute | solution.py:279
  53.4 5.6 %collective-permute-start.12 = (s16[2,144,128]{2,1,0:T(8,128)(2,1)S(1)}, s16[2,144,128]{2,1,0:T(8,128)(2,1)S(1)}, u32[]{:S(2)}, u32[]{:S(2)}) collective-permute-start(s16[2,144,128]{2,1,0:T(8,128)(2,1)S(1)} %get-tuple-element.44), channel_id=1, source_target_pairs={{0,2},{1,3},{2,4},{3,5},{4,6},{5,7},{6,8},{7,9},{8,10},{9,11},{10,... | collective-permute-start | bytes 221192 | tf_op jit(solution)/shard_map/ppermute | solution.py:279
  59.7 8.1 %collective-permute-start.13 = (s16[2,144,128]{2,1,0:T(8,128)(2,1)S(1)}, s16[2,144,128]{2,1,0:T(8,128)(2,1)S(1)}, u32[]{:S(2)}, u32[]{:S(2)}) collective-permute-start(s16[2,144,128]{2,1,0:T(8,128)(2,1)S(1)} %get-tuple-element.45), channel_id=1, source_target_pairs={{0,10},{1,11},{2,12},{3,13},{4,14},{5,15},{6,0},{7,1},{8,2},{9,3},... | collective-permute-start | bytes 221192 | tf_op jit(solution)/shard_map/ppermute | solution.py:279
  62.5 8.7 %collective-permute-start.14 = (s16[2,144,128]{2,1,0:T(8,128)(2,1)S(1)}, s16[2,144,128]{2,1,0:T(8,128)(2,1)S(1)}, u32[]{:S(2)}, u32[]{:S(2)}) collective-permute-start(s16[2,144,128]{2,1,0:T(8,128)(2,1)S(1)} %get-tuple-element.46), channel_id=1, source_target_pairs={{0,6},{1,7},{2,8},{3,9},{4,10},{5,11},{6,12},{7,13},{8,14},{9,15},... | collective-permute-start | bytes 221192 | tf_op jit(solution)/shard_map/ppermute | solution.py:279
  63.6 7.6 %collective-permute-start.15 = (s16[2,144,128]{2,1,0:T(8,128)(2,1)S(1)}, s16[2,144,128]{2,1,0:T(8,128)(2,1)S(1)}, u32[]{:S(2)}, u32[]{:S(2)}) collective-permute-start(s16[2,144,128]{2,1,0:T(8,128)(2,1)S(1)} %get-tuple-element.47), channel_id=1, source_target_pairs={{0,14},{1,15},{2,0},{3,1},{4,2},{5,3},{6,4},{7,5},{8,6},{9,7},{10,... | collective-permute-start | bytes 221192 | tf_op jit(solution)/shard_map/ppermute | solution.py:279
  66.4 6.1 %collective-permute-start.16 = (s16[2,144,128]{2,1,0:T(8,128)(2,1)S(1)}, s16[2,144,128]{2,1,0:T(8,128)(2,1)S(1)}, u32[]{:S(2)}, u32[]{:S(2)}) collective-permute-start(s16[2,144,128]{2,1,0:T(8,128)(2,1)S(1)} %get-tuple-element.48), channel_id=1, source_target_pairs={{0,2},{1,3},{2,4},{3,5},{4,6},{5,7},{6,8},{7,9},{8,10},{9,11},{10,... | collective-permute-start | bytes 221192 | tf_op jit(solution)/shard_map/ppermute | solution.py:279
  73.9 5.3 %collective-permute-start.20 = (s16[2,272,128]{2,1,0:T(8,128)(2,1)S(1)}, s16[2,272,128]{2,1,0:T(8,128)(2,1)S(1)}, u32[]{:S(2)}, u32[]{:S(2)}) collective-permute-start(s16[2,272,128]{2,1,0:T(8,128)(2,1)S(1)} %get-tuple-element.53), channel_id=1, source_target_pairs={{0,14},{1,15},{2,0},{3,1},{4,2},{5,3},{6,4},{7,5},{8,6},{9,7},{10,... | collective-permute-start | bytes 417800 | tf_op jit(solution)/shard_map/ppermute | solution.py:279
  74.3 5.5 %collective-permute-start.21 = (s16[1,272,128]{2,1,0:T(8,128)(2,1)S(1)}, s16[1,272,128]{2,1,0:T(8,128)(2,1)S(1)}, u32[]{:S(2)}, u32[]{:S(2)}) collective-permute-start(s16[1,272,128]{2,1,0:T(8,128)(2,1)S(1)} %get-tuple-element.54), channel_id=1, source_target_pairs={{0,2},{1,3},{2,4},{3,5},{4,6},{5,7},{6,8},{7,9},{8,10},{9,11},{10,... | collective-permute-start | bytes 208904 | tf_op jit(solution)/shard_map/ppermute | solution.py:279
  80.7 10.0 %collective-permute-start.22 = (s16[1,272,128]{2,1,0:T(8,128)(2,1)S(1)}, s16[1,272,128]{2,1,0:T(8,128)(2,1)S(1)}, u32[]{:S(2)}, u32[]{:S(2)}) collective-permute-start(s16[1,272,128]{2,1,0:T(8,128)(2,1)S(1)} %get-tuple-element.55), channel_id=1, source_target_pairs={{0,10},{1,11},{2,12},{3,13},{4,14},{5,15},{6,0},{7,1},{8,2},{9,3},... | collective-permute-start | bytes 208904 | tf_op jit(solution)/shard_map/ppermute | solution.py:279
  81.3 9.3 %collective-permute-start.23 = (s16[1,272,128]{2,1,0:T(8,128)(2,1)S(1)}, s16[1,272,128]{2,1,0:T(8,128)(2,1)S(1)}, u32[]{:S(2)}, u32[]{:S(2)}) collective-permute-start(s16[1,272,128]{2,1,0:T(8,128)(2,1)S(1)} %get-tuple-element.56), channel_id=1, source_target_pairs={{0,6},{1,7},{2,8},{3,9},{4,10},{5,11},{6,12},{7,13},{8,14},{9,15},... | collective-permute-start | bytes 208904 | tf_op jit(solution)/shard_map/ppermute | solution.py:279
  84.6 6.1 %collective-permute-start.24 = (s16[1,272,128]{2,1,0:T(8,128)(2,1)S(1)}, s16[1,272,128]{2,1,0:T(8,128)(2,1)S(1)}, u32[]{:S(2)}, u32[]{:S(2)}) collective-permute-start(s16[1,272,128]{2,1,0:T(8,128)(2,1)S(1)} %get-tuple-element.57), channel_id=1, source_target_pairs={{0,14},{1,15},{2,0},{3,1},{4,2},{5,3},{6,4},{7,5},{8,6},{9,7},{10,... | collective-permute-start | bytes 208904 | tf_op jit(solution)/shard_map/ppermute | solution.py:279
  86.7 5.5 %collective-permute-start.25 = (s16[1,272,128]{2,1,0:T(8,128)(2,1)S(1)}, s16[1,272,128]{2,1,0:T(8,128)(2,1)S(1)}, u32[]{:S(2)}, u32[]{:S(2)}) collective-permute-start(s16[1,272,128]{2,1,0:T(8,128)(2,1)S(1)} %get-tuple-element.58), channel_id=1, source_target_pairs={{0,2},{1,3},{2,4},{3,5},{4,6},{5,7},{6,8},{7,9},{8,10},{9,11},{10,... | collective-permute-start | bytes 208904 | tf_op jit(solution)/shard_map/ppermute | solution.py:279
  86.7 4.0 %collective-permute-start.19 = (s16[1,144,128]{2,1,0:T(8,128)(2,1)S(1)}, s16[1,144,128]{2,1,0:T(8,128)(2,1)S(1)}, u32[]{:S(2)}, u32[]{:S(2)}) collective-permute-start(s16[1,144,128]{2,1,0:T(8,128)(2,1)S(1)} %x_second.1), channel_id=1, source_target_pairs={{0,16},{1,17},{2,18},{3,19},{4,20},{5,21},{6,22},{7,23},{8,24},{9,... | collective-permute-start | bytes 110600 | tf_op jit(solution)/shard_map/ppermute | solution.py:279
  (7 other events, 27.7 us)
where the time goes:
time: 94 us; the launch traced here: 93.9 us
  starting transfers between devices  39.1 us (42%)
  Pallas kernels  31.4 us (33%)
  waiting for transfers between devices  20 us (21%)
  local copies, waits for them, and re-layouts  3.05 us (3%)
    pallas_call x13, Pallas kernels, call(): pl.pallas_call(kernel, out_shape=out_shape, in_specs=in_specs, out_specs=...  31.4 us
    ppermute x17, starting transfers between devices, send_rep(): return lax.ppermute(array, 'rep', pairs)  23.9 us
    ppermute x17, waiting for transfers between devices, send_rep(): return lax.ppermute(array, 'rep', pairs)  20 us
    ppermute x9, starting transfers between devices, send_blk(): return lax.ppermute(array, 'blk', pairs)  15.3 us
    unnamed x10, local copies, waits for them, and re-layouts  2.95 us
  transfers between devices with their start and end apart: 26, of which 9 were waited for; matrix products, arithmetic and copies ran while one was open for 0% of the time, Pallas kernels for 25%

commit v1 on v0

v1 whole, which is shorter than its diff:
```python
import functools

import jax
import jax.numpy as jnp
from jax import lax
from jax.experimental import pallas as pl
from jax.experimental.pallas import tpu as pltpu
from jax.sharding import PartitionSpec as P

BS = 128
F = 128
H = 256
SLOTS = 40
LISTS = 8
PIECE_BLK = 3
PIECE_ROWS = PIECE_BLK * BS
HALF = PIECE_ROWS // 2
PANEL_BLK = 96
GROUP = 8
GROUPS = SLOTS // GROUP
TOP = 32766.0
MIB = 1 << 20

FIRST, SECOND = (0, 2), (2, 1)


def message_rows(blocks):
    return blocks * BS + 16


SMEM = pl.BlockSpec(memory_space=pltpu.SMEM)
VMEM = pl.BlockSpec(memory_space=pltpu.VMEM)
ANY = pl.BlockSpec(memory_space=pl.ANY)


def call(kernel, name, out_shape, in_specs, out_specs, args, us, mib=24, **more):
    return pl.pallas_call(
        kernel,
        out_shape=out_shape,
        in_specs=in_specs,
        out_specs=out_specs,
        compiler_params=pltpu.CompilerParams(vmem_limit_bytes=mib * MIB),
        cost_estimate=pl.CostEstimate(flops=0, bytes_accessed=int(us * 3.0e6), transcendentals=0),
        name=name,
        **more,
    )(*args)


def groups_of(count):
    return lax.div(jnp.clip(count, 0, SLOTS) + (GROUP - 1), GROUP)


def fetch(vals_ref, vals, sems, count_ref, j, k):
    def each(action):
        @pl.loop(0, groups_of(count_ref[0, j]))
        def _(g):
            action(
                pltpu.make_async_copy(
                    vals_ref.at[pl.ds(pl.multiple_of(j * SLOTS + g * GROUP, GROUP), GROUP)],
                    vals.at[pl.ds(pl.multiple_of(k * SLOTS + g * GROUP, GROUP), GROUP)],
                    sems.at[k * GROUPS + g],
                )
            )

    return each


def add_list(panel, piece, vals, count_ref, lists_ref, j, k, wait=None):
    count = count_ref[0, j]

    @pl.loop(0, groups_of(count))
    def _(g):
        if wait is not None:
            wait(g)
        products, rows = [], []
        for u in range(GROUP):
            q = g * GROUP + u
            entry = jnp.where(q < count, lists_ref[j, q], PANEL_BLK * 4)
            rows.append(entry >> 2)
            products.append(
                jnp.dot(
                    vals[k * SLOTS + q],
                    piece[pl.ds(pl.multiple_of((entry & 3) * BS, BS), BS), :],
                    preferred_element_type=jnp.float32,
                )
            )
        for row, product in zip(rows, products):
            panel[row] += product


def group_wait(vals_ref, vals, sems, j, k):
    def wait(g):
        pltpu.make_async_copy(
            vals_ref.at[pl.ds(pl.multiple_of(j * SLOTS + g * GROUP, GROUP), GROUP)],
            vals.at[pl.ds(pl.multiple_of(k * SLOTS + g * GROUP, GROUP), GROUP)],
            sems.at[k * GROUPS + g],
        ).wait()

    return wait


def piece_of(place_ref, shift, flip):
    x_hi = place_ref[1]
    return lax.rem(place_ref[0] + shift, 4) * 2 + (1 - x_hi if flip else x_hi)


def first_products(place_ref, count_ref, lists_ref, own_ref, vals_ref, panel, own, vals, sems, own_sem):
    mine = piece_of(place_ref, 0, False)
    own_copy = pltpu.make_async_copy(own_ref, own, own_sem)
    own_copy.start()
    fetch(vals_ref, vals, sems, count_ref, mine, 0)(lambda copy: copy.start())

    @pl.loop(0, PANEL_BLK // 4)
    def _(k):
        for u in range(4):
            panel[k * 4 + u] = jnp.zeros((BS, F), jnp.float32)

    own_copy.wait()
    add_list(panel, own, vals, count_ref, lists_ref, mine, 0, group_wait(vals_ref, vals, sems, mine, 0))


def more_products(pieces, split, ahead, *refs):
    place_ref, count_ref, lists_ref, _, vals_ref = refs[:5]
    inputs = 5 + len(pieces) + 2 * len(split)
    arrays, outputs = refs[5:inputs], refs[inputs:]
    panel = outputs[0]
    vals, sems, whole = outputs[-3:]
    todo = [piece_of(place_ref, *which) for which in pieces + split]
    for k, j in enumerate(todo):
        fetch(vals_ref, vals, sems, count_ref, j, k)(lambda copy: copy.start())
    if ahead:
        next_vals, next_sems = outputs[1], outputs[2]
        later = fetch(vals_ref, next_vals, next_sems, count_ref, piece_of(place_ref, *ahead), 0)
        later(lambda copy: copy.start())
    for k, j in enumerate(todo):
        piece = whole
        if k < len(pieces):
            piece = arrays[k]
        else:
            first = len(pieces) + 2 * (k - len(pieces))
            whole[:HALF, :] = arrays[first][...]
            whole[HALF:, :] = arrays[first + 1][...]
        add_list(panel, piece, vals, count_ref, lists_ref, j, k, group_wait(vals_ref, vals, sems, j, k))
    if ahead:
        later(lambda copy: copy.wait())


def quantize(block):
    peak = jnp.maximum(jnp.max(jnp.abs(block), axis=0, keepdims=True), 1e-32)
    exponent = jnp.ceil(jnp.log2(peak) + 0.001)
    scaled = block * (jnp.exp2(-exponent) * TOP)
    return jnp.round(scaled).astype(jnp.int32).astype(jnp.int16), exponent


def write_message(out_ref, index, blocks):
    count = len(blocks)
    row = lax.broadcasted_iota(jnp.int32, (16, F), 0)
    tail = jnp.zeros((16, F), jnp.float32)
    for i, block in enumerate(blocks):
        whole, exponent = quantize(block)
        out_ref[index, i * BS : (i + 1) * BS, :] = whole
        tail = jnp.where(row == i, exponent, tail)
    out_ref[index, count * BS : count * BS + 16, :] = tail.astype(jnp.int32).astype(jnp.int16)


def read_message(ref, index, count):
    tail = ref[index, count * BS : count * BS + 16, :].astype(jnp.int32).astype(jnp.float32)
    size = jnp.exp2(tail) * (1.0 / TOP)
    blocks = []
    for i in range(count):
        whole = ref[index, i * BS : (i + 1) * BS, :].astype(jnp.int32).astype(jnp.float32)
        blocks.append(whole * size[i : i + 1, :])
    return blocks


def add(first, *others):
    for other in others:
        first = [a + b for a, b in zip(first, other)]
    return first


class Here:
    def __init__(self, place_ref, panel=None):
        self.core, self.x, self.z = place_ref[2], place_ref[3], place_ref[4]
        self.panel = panel

    def x_of(self, other):
        return 1 - self.x if other else self.x

    def z_of(self, shift):
        return lax.rem(self.z + shift + 8, 8)

    def partial(self, other_x, z, part, other_core=False):
        core = 1 - self.core if other_core else self.core
        owner = self.x_of(other_x) * 16 + z * 2 + core
        return [self.panel[owner * PIECE_BLK + part[0] + i] for i in range(part[1])]


def core_messages(part, other_x, place_ref, panel, out_ref):
    here = Here(place_ref, panel)
    for k, other in enumerate(other_x):

        @pl.loop(0, 8)
        def _(z):
            write_message(out_ref, k * 8 + z, here.partial(other, z, part, other_core=True))


def last_products(which, place_ref, count_ref, lists_ref, _, vals, top_ref, bottom_ref, panel, out_ref, whole):
    whole[:HALF, :] = top_ref[...]
    whole[HALF:, :] = bottom_ref[...]
    add_list(panel, whole, vals, count_ref, lists_ref, piece_of(place_ref, *which), 0)
    core_messages(FIRST, (True,), place_ref, panel, out_ref)


def x_messages(place_ref, panel, rc_ref, out_ref):
    here = Here(place_ref, panel)

    @pl.loop(0, 8)
    def _(z):
        write_message(out_ref, z, add(here.partial(True, z, FIRST), read_message(rc_ref, z, FIRST[1])))


def base_value(part, here, rc_ref, rx_ref, other, z):
    if part == FIRST:
        return add(
            here.partial(other, z, part), read_message(rc_ref, z, part[1]), read_message(rx_ref, z, part[1])
        )
    return add(here.partial(other, z, part), read_message(rc_ref, other * 8 + z, part[1]))


def sides(part):
    return (0,) if part == FIRST else (0, 1)


def z_start(part, place_ref, panel, rc_ref, rx_ref, down_ref, up_ref, two_ref, far_ref):
    here = Here(place_ref, panel)
    for other in sides(part):
        for out_ref, index, shift in (
            (down_ref, 2 * other, -4), (down_ref, 2 * other + 1, -1), (up_ref, other, 2),
            (two_ref, other, -2), (far_ref, other, 3),
        ):
            write_message(out_ref, index, base_value(part, here, rc_ref, rx_ref, other, here.z_of(shift)))


def z_middle(part, place_ref, panel, rc_ref, rx_ref, down_ref, up_ref, three_ref, one_ref):
    here = Here(place_ref, panel)
    count = part[1]
    for other in sides(part):
        value = functools.partial(base_value, part, here, rc_ref, rx_ref, other)
        write_message(three_ref, other, add(value(here.z_of(-3)), read_message(down_ref, 2 * other, count)))
        write_message(one_ref, other, add(value(here.z_of(1)), read_message(up_ref, other, count)))


def arrivals(part, other, down_ref, *refs):
    return [read_message(down_ref, 2 * other + 1, part[1])] + [read_message(ref, other, part[1]) for ref in refs]


def z_end(place_ref, panel, rc_ref, *refs):
    here = Here(place_ref, panel)
    value = base_value(SECOND, here, rc_ref, None, 1, here.z)
    write_message(refs[5], 0, add(value, *arrivals(SECOND, 1, *refs[:5])))


def layer(place_ref, panel, rc1_ref, rx1_ref, rc2_ref, rx2_ref, *refs):
    here = Here(place_ref, panel)
    weight_ref, out_ref = refs[10], refs[11]
    first = base_value(FIRST, here, rc1_ref, rx1_ref, 0, here.z)
    first = add(first, *arrivals(FIRST, 0, *refs[:5]))
    second = base_value(SECOND, here, rc2_ref, None, 0, here.z)
    second = add(second, read_message(rx2_ref, 0, 1), *arrivals(SECOND, 0, *refs[5:10]))
    weight = weight_ref[...]
    for i, block in enumerate(first + second):
        high = block.astype(jnp.bfloat16)
        rest = block - high.astype(jnp.float32)
        middle = rest.astype(jnp.bfloat16)
        low = (rest - middle.astype(jnp.float32)).astype(jnp.bfloat16)
        result = jnp.dot(low, weight, preferred_element_type=jnp.float32)
        result += jnp.dot(middle, weight, preferred_element_type=jnp.float32)
        result += jnp.dot(high, weight, preferred_element_type=jnp.float32)
        out_ref[i * BS : (i + 1) * BS, :] = jnp.maximum(result, 0.0).astype(jnp.bfloat16)


def messages(count, part):
    return jax.ShapeDtypeStruct((count, message_rows(part[1]), F), jnp.int16)


def send_blk(array, dy, flip=0):
    pairs = [(y * 2 + h, ((y + dy) % 4) * 2 + (h ^ flip)) for y in range(4) for h in range(2)]
    return lax.ppermute(array, "blk", pairs)


def send_rep(array, dx, dz, dc):
    pairs = [
        (x * 16 + z * 2 + c, (x ^ dx) * 16 + ((z + dz) % 8) * 2 + (c ^ dc))
        for x in range(2) for z in range(8) for c in range(2)
    ]
    return lax.ppermute(array, "rep", pairs)


def sum_along_z(part, name, place, panel, rc, rx, also=None):
    count = len(sides(part))
    have = (rc,) if rx is None else (rc, rx)

    def fill(kernel):
        if rx is not None:
            return functools.partial(kernel, part)
        return lambda place_ref, panel_ref, rc_ref, *refs: kernel(part, place_ref, panel_ref, rc_ref, None, *refs)

    down, up, two, far = call(
        fill(z_start), name + "_start", (messages(2 * count, part),) + (messages(count, part),) * 3,
        [SMEM] + [VMEM] * (1 + len(have)), (VMEM,) * 4, (place, panel, *have), 0.6,
    )
    down, up = send_rep(down, 0, -1, 0), send_rep(up, 0, 1, 0)
    two, far = send_rep(two, 0, -2, 0), send_rep(far, 0, 3, 0)
    down, also = lax.optimization_barrier((down, also))
    three, one = call(
        fill(z_middle), name + "_middle", (messages(count, part),) * 2,
        [SMEM] + [VMEM] * (3 + len(have)), (VMEM,) * 2, (place, panel, *have, down, up), 0.6,
    )
    return (down, two, far, send_rep(three, 0, -3, 0), send_rep(one, 0, 1, 0)), also


def local(node_feats, block_vals, block_rows, block_cols, block_count, weight):
    blk = lax.axis_index("blk")
    rep = lax.axis_index("rep")
    place = jnp.stack([blk // 2, blk % 2, rep % 2, rep // 16, (rep // 2) % 8]).astype(jnp.int32)
    slots = block_rows.reshape(LISTS, SLOTS) * 4 + block_cols.reshape(LISTS, SLOTS)
    lists = (place, block_count.reshape(1, LISTS), slots)
    vals = block_vals.reshape(LISTS * SLOTS, BS, BS)
    panel_type = jax.ShapeDtypeStruct((PANEL_BLK + 1, BS, F), jnp.float32)
    list_type = jax.ShapeDtypeStruct((SLOTS, BS, BS), jnp.bfloat16)
    piece_buffer = pltpu.VMEM((PIECE_ROWS, F), jnp.bfloat16)

    def list_buffers(count):
        return [pltpu.VMEM((count * SLOTS, BS, BS), jnp.bfloat16), pltpu.SemaphoreType.DMA((count * GROUPS,))]

    own = node_feats
    flipped, below, above = send_blk(own, 0, 1), send_blk(own, 1), send_blk(own, -1)
    panel = call(
        first_products, "products_own", panel_type, [SMEM] * 3 + [ANY] * 2, VMEM, (*lists, own, vals), 3, 41,
        scratch_shapes=[piece_buffer, *list_buffers(1), pltpu.SemaphoreType.DMA],
    )
    panel, flipped, below, above = lax.optimization_barrier((panel, flipped, below, above))
    below_flipped, above_flipped = send_blk(flipped, 1), send_blk(flipped, -1)
    far = send_blk(below[:HALF], 1), send_blk(above[HALF:], -1)
    panel = call(
        functools.partial(more_products, ((0, True), (3, False), (1, False)), (), None), "products_near", panel_type,
        [SMEM] * 3 + [VMEM, ANY] + [VMEM] * 3, VMEM, (*lists, panel, vals, flipped, below, above), 4, 41,
        input_output_aliases={3: 0},
        scratch_shapes=[*list_buffers(3), piece_buffer],
    )
    panel, below_flipped, above_flipped, far = lax.optimization_barrier((panel, below_flipped, above_flipped, far))
    far_flipped = send_blk(below_flipped[:HALF], 1), send_blk(above_flipped[HALF:], -1)
    panel, last_vals = call(
        functools.partial(more_products, ((3, True), (1, True)), ((2, False),), (2, True)),
        "products_near_flipped", (panel_type, list_type),
        [SMEM] * 3 + [VMEM, ANY] + [VMEM] * 4, (VMEM,) * 2,
        (*lists, panel, vals, below_flipped, above_flipped, *far), 3, 41,
        input_output_aliases={3: 0},
        scratch_shapes=[pltpu.SemaphoreType.DMA((GROUPS,)), *list_buffers(3), piece_buffer],
    )
    panel, to_core = call(
        functools.partial(last_products, (2, True)), "products_far", (panel_type, messages(8, FIRST)),
        [SMEM] * 3 + [VMEM] * 4, (VMEM,) * 2, (*lists, panel, last_vals, *far_flipped), 3, 40,
        input_output_aliases={3: 0},
        scratch_shapes=[piece_buffer],
    )

    def to_other_core(name, part, other_x):
        return call(
            functools.partial(core_messages, part, other_x), name, messages(8 * len(other_x), part),
            [SMEM, VMEM], VMEM, (place, panel), 0.6,
        )

    rc_cross = send_rep(to_core, 0, 0, 1)
    rc_second = send_rep(to_other_core("core_second", SECOND, (False, True)), 0, 0, 1)
    rc_first = send_rep(to_other_core("core_first", FIRST, (False,)), 0, 0, 1)
    to_x = call(x_messages, "x_first", messages(8, FIRST), [SMEM, VMEM, VMEM], VMEM, (place, panel, rc_cross), 0.6)
    rx_first = send_rep(to_x, 1, 0, 0)
    second, rc_first = sum_along_z(SECOND, "second", place, panel, rc_second, None, rc_first)
    to_x = call(
        z_end, "x_second", messages(1, SECOND), [SMEM] + [VMEM] * 7, VMEM, (place, panel, rc_second, *second), 0.6
    )
    panel, to_x = lax.optimization_barrier((panel, to_x))
    rx_second = send_rep(to_x, 1, 0, 0)
    first, _ = sum_along_z(FIRST, "first", place, panel, rc_first, rx_first)
    return call(
        layer, "layer", jax.ShapeDtypeStruct((PIECE_ROWS, H), jnp.bfloat16), [SMEM] + [VMEM] * 16, VMEM,
        (place, panel, rc_first, rx_first, rc_second, rx_second, *first, *second, weight), 1.5,
    )


def solution(mesh):
    return jax.shard_map(
        local,
        mesh=mesh,
        in_specs=(
            P(("blk", "rep"), None),
            P("blk", "rep", None, None, None, None),
            P("blk", "rep", None, None),
            P("blk", "rep", None, None),
            P("blk", "rep", None),
            P(),
        ),
        out_specs=P(("blk", "rep"), None),
        check_vma=False,
    )
```

time: 94 us -> 76.5 us (0.81)
  Pallas kernels: 31.4 us -> 17.6 us
  waiting for transfers between devices: 20 us -> 15.7 us
  starting transfers between devices: 39.1 us -> 40.6 us
  local copies, waits for them, and re-layouts: 3.05 us -> 1.66 us
    pallas_call x13, Pallas kernels: 31.4 us -> 17.6 us  [call(): pl.pallas_call(kernel, out_shape=out_shape, in_specs=in_specs, out_specs=...]
    ppermute x17, waiting for transfers between devices: 20 us -> 11.5 us  [send_rep(): return lax.ppermute(array, 'rep', pairs)]
    ppermute x9, waiting for transfers between devices: 0.02 us -> 4.22 us  [send_blk(): return lax.ppermute(array, 'blk', pairs)]
    ppermute x17, starting transfers between devices: 23.9 us -> 27.7 us  [send_rep(): return lax.ppermute(array, 'rep', pairs)]
    ppermute x9, starting transfers between devices: 15.3 us -> 12.9 us  [send_blk(): return lax.ppermute(array, 'blk', pairs)]
    unnamed x10 -> x6, local copies, waits for them, and re-layouts: 2.95 us -> 1.55 us
  transfers between devices with their start and end apart: 26 -> 26, of which waited for: 9 -> 11; matrix products, arithmetic and copies ran while one was open for 0% -> 1% of each run, Pallas kernels for 25% -> 18%
where the time goes in v1:
time: 76.5 us; the launch traced here: 76.4 us
  starting transfers between devices  40.6 us (53%)
  Pallas kernels  17.6 us (23%)
  waiting for transfers between devices  15.7 us (21%)
  local copies, waits for them, and re-layouts  1.66 us (2%)
    ppermute x17, starting transfers between devices, send_rep(): return lax.ppermute(array, 'rep', pairs)  27.7 us
    pallas_call x13, Pallas kernels, call(): pl.pallas_call(kernel, out_shape=out_shape, in_specs=in_specs, out_specs=...  17.6 us
    ppermute x9, starting transfers between devices, send_blk(): return lax.ppermute(array, 'blk', pairs)  12.9 us
    ppermute x17, waiting for transfers between devices, send_rep(): return lax.ppermute(array, 'rep', pairs)  11.5 us
    ppermute x9, waiting for transfers between devices, send_blk(): return lax.ppermute(array, 'blk', pairs)  4.22 us
    unnamed x6, local copies, waits for them, and re-layouts  1.55 us
  transfers between devices with their start and end apart: 26, of which 11 were waited for; matrix products, arithmetic and copies ran while one was open for 1% of the time, Pallas kernels for 18%

profile of v1, /device:TPU:2, one launch (start us, length us, event | category | flops | bytes accessed | tf_op | source)
XLA Modules:
  0.0 76.4 jit_solution(13576890876285864750)
XLA Ops:
  0.0 2.1 %collective-permute-start = (bf16[384,128]{1,0:T(8,128)(2,1)}, bf16[384,128]{1,0:T(8,128)(2,1)S(1)}, u32[]{:S(2)}, u32[]{:S(2)}) collective-permute-start(bf16[384,128]{1,0:T(8,128)(2,1)} %own_ref.1), channel_id=1, source_target_pairs={{0,32},{32,0},{64,96},{96,64},{128,160},{160,128},{192,224},{224,1... | collective-permute-start | bytes 294920 | tf_op jit(solution)/shard_map/ppermute | solution.py:289
  2.1 3.0 %collective-permute-start.2 = (bf16[384,128]{1,0:T(8,128)(2,1)}, bf16[384,128]{1,0:T(8,128)(2,1)S(1)}, u32[]{:S(2)}, u32[]{:S(2)}) collective-permute-start(bf16[384,128]{1,0:T(8,128)(2,1)} %own_ref.1), channel_id=1, source_target_pairs={{0,192},{32,224},{64,0},{96,32},{128,64},{160,96},{192,128},{224,1... | collective-permute-start | bytes 294920 | tf_op jit(solution)/shard_map/ppermute | solution.py:289
  7.5 2.2 %products_own.1.refs_3_ = f32[97,128,128]{2,1,0:T(8,128)S(1)} custom-call(s32[5]{0:T(128)S(1)} %stack.23.place_ref.refs_0_, s32[1,8]{1,0:T(1,128)S(1)} %bitcast.9, s32[8,40]{1,0:T(8,128)S(1)} %add_bitcast_fusion.lists_ref.refs_2_, bf16[384,128]{1,0:T(8,128)(2,1)S(1)} %copy-done, bf16[320,128,128]{2,1,0:T(8,128)(2,1)} %bitcast.13), custom_call_target="tpu_custom_call" | custom-call | bytes 9000000 | tf_op jit(solution)/shard_map/products_own/pallas_call | solution.py:37
  9.7 1.4 %collective-permute-done.1.refs_6_ = bf16[384,128]{1,0:T(8,128)(2,1)S(1)} collective-permute-done((bf16[384,128]{1,0:T(8,128)(2,1)}, bf16[384,128]{1,0:T(8,128)(2,1)S(1)}, u32[]{:S(2)}, u32[]{:S(2)}) %collective-permute-start.1) | collective-permute-done | bytes 98336 | tf_op jit(solution)/shard_map/ppermute | solution.py:289
  11.2 1.6 %collective-permute-start.4 = (bf16[384,128]{1,0:T(8,128)(2,1)S(1)}, bf16[384,128]{1,0:T(8,128)(2,1)S(1)}, u32[]{:S(2)}, u32[]{:S(2)}) collective-permute-start(bf16[384,128]{1,0:T(8,128)(2,1)S(1)} %collective-permute-done.refs_5_), channel_id=1, source_target_pairs={{0,192},{32,224},{64,0},{96,32},{128,64},{160,96},{192,128},{224,1... | collective-permute-start | bytes 294920 | tf_op jit(solution)/shard_map/ppermute | solution.py:289
  13.3 3.2 %collective-permute-start.6 = (bf16[192,128]{1,0:T(8,128)(2,1)S(1)}, bf16[192,128]{1,0:T(8,128)(2,1)S(1)}, u32[]{:S(2)}, u32[]{:S(2)}) collective-permute-start(bf16[192,128]{1,0:T(8,128)(2,1)S(1)} %slice.13), channel_id=1, source_target_pairs={{0,192},{32,224},{64,0},{96,32},{128,64},{160,96},{192,128},{224,1... | collective-permute-start | bytes 147464 | tf_op jit(solution)/shard_map/ppermute | solution.py:289
  16.5 2.9 %products_near.1.refs_3_ = f32[97,128,128]{2,1,0:T(8,128)S(1)} custom-call(s32[5]{0:T(128)S(1)} %stack.23.place_ref.refs_0_, s32[1,8]{1,0:T(1,128)S(1)} %bitcast.10, s32[8,40]{1,0:T(8,128)S(1)} %add_bitcast_fusion.lists_ref.refs_2_, f32[97,128,128]{2,1,0:T(8,128)S(1)} %products_own.1.refs_3_, ...), custom_call_target="tpu_custom_call", output_to_operand_aliasing={{}: (3, {})} | custom-call | bytes 12000000 | tf_op jit(solution)/shard_map/products_near/pallas_call | solution.py:37
  19.5 2.4 %collective-permute-start.8 = (bf16[192,128]{1,0:T(8,128)(2,1)S(1)}, bf16[192,128]{1,0:T(8,128)(2,1)S(1)}, u32[]{:S(2)}, u32[]{:S(2)}) collective-permute-start(bf16[192,128]{1,0:T(8,128)(2,1)S(1)} %slice.15), channel_id=1, source_target_pairs={{0,192},{32,224},{64,0},{96,32},{128,64},{160,96},{192,128},{224,1... | collective-permute-start | bytes 147464 | tf_op jit(solution)/shard_map/ppermute | solution.py:289
  21.9 2.5 %products_near_flipped.1 = (f32[97,128,128]{2,1,0:T(8,128)S(1)}, bf16[40,128,128]{2,1,0:T(8,128)(2,1)S(1)}) custom-call(s32[5]{0:T(128)S(1)} %stack.23.place_ref.refs_0_, s32[1,8]{1,0:T(1,128)S(1)} %bitcast.11, s32[8,40]{1,0:T(8,128)S(1)} %add_bitcast_fusion.lists_ref.refs_2_, ...), custom_call_target="tpu_custom_call", output_to_operand_aliasing={{0}: (3, {})} | custom-call | bytes 9000000 | tf_op jit(solution)/shard_map/products_near_flipped/pallas_call | solution.py:37
  24.5 2.8 %collective-permute-done.7.top_ref = bf16[192,128]{1,0:T(8,128)(2,1)S(1)} collective-permute-done((bf16[192,128]{1,0:T(8,128)(2,1)S(1)}, bf16[192,128]{1,0:T(8,128)(2,1)S(1)}, u32[]{:S(2)}, u32[]{:S(2)}) %collective-permute-start.7) | collective-permute-done | bytes 49184 | tf_op jit(solution)/shard_map/ppermute | solution.py:289
  27.2 1.5 %products_far.1 = (f32[97,128,128]{2,1,0:T(8,128)S(1)}, s16[8,272,128]{2,1,0:T(8,128)(2,1)S(1)}) custom-call(s32[5]{0:T(128)S(1)} %stack.23.place_ref.refs_0_, s32[1,8]{1,0:T(1,128)S(1)} %bitcast.12, s32[8,40]{1,0:T(8,128)S(1)} %add_bitcast_fusion.lists_ref.refs_2_, f32[97,128,128]{2,1,0:T(8,128)S(1)} %get-tuple-element.43._, ...), custom_call_target="tpu_custom_call", output_to_operand_aliasing={{0}: (3, {})} | custom-call | bytes 9000000 | tf_op jit(solution)/shard_map/products_far/pallas_call | solution.py:37
  32.7 2.2 %collective-permute-start.18 = (s16[8,272,128]{2,1,0:T(8,128)(2,1)S(1)}, s16[8,272,128]{2,1,0:T(8,128)(2,1)S(1)}, u32[]{:S(2)}, u32[]{:S(2)}) collective-permute-start(s16[8,272,128]{2,1,0:T(8,128)(2,1)S(1)} %x_first.1), channel_id=1, source_target_pairs={{0,16},{1,17},{2,18},{3,19},{4,20},{5,21},{6,22},{7,23},{8,24},{9,... | collective-permute-start | bytes 1671176 | tf_op jit(solution)/shard_map/ppermute | solution.py:297
  35.7 5.6 %collective-permute-start.10 = (s16[4,144,128]{2,1,0:T(8,128)(2,1)S(1)}, s16[4,144,128]{2,1,0:T(8,128)(2,1)S(1)}, u32[]{:S(2)}, u32[]{:S(2)}) collective-permute-start(s16[4,144,128]{2,1,0:T(8,128)(2,1)S(1)} %get-tuple-element.46), channel_id=1, source_target_pairs={{0,14},{1,15},{2,0},{3,1},{4,2},{5,3},{6,4},{7,5},{8,6},{9,7},{10,... | collective-permute-start | bytes 442376 | tf_op jit(solution)/shard_map/ppermute | solution.py:297
  41.4 2.1 %collective-permute-start.12 = (s16[2,144,128]{2,1,0:T(8,128)(2,1)S(1)}, s16[2,144,128]{2,1,0:T(8,128)(2,1)S(1)}, u32[]{:S(2)}, u32[]{:S(2)}) collective-permute-start(s16[2,144,128]{2,1,0:T(8,128)(2,1)S(1)} %get-tuple-element.48), channel_id=1, source_target_pairs={{0,12},{1,13},{2,14},{3,15},{4,0},{5,1},{6,2},{7,3},{8,4},{9,5},{1... | collective-permute-start | bytes 221192 | tf_op jit(solution)/shard_map/ppermute | solution.py:297
  43.4 2.2 %collective-permute-done.10.refs_0_.refs_5_ = s16[4,144,128]{2,1,0:T(8,128)(2,1)S(1)} collective-permute-done((s16[4,144,128]{2,1,0:T(8,128)(2,1)S(1)}, s16[4,144,128]{2,1,0:T(8,128)(2,1)S(1)}, u32[]{:S(2)}, u32[]{:S(2)}) %collective-permute-start.10) | collective-permute-done | bytes 147488 | tf_op jit(solution)/shard_map/ppermute | solution.py:297
  47.6 2.1 %collective-permute-start.15 = (s16[2,144,128]{2,1,0:T(8,128)(2,1)S(1)}, s16[2,144,128]{2,1,0:T(8,128)(2,1)S(1)}, u32[]{:S(2)}, u32[]{:S(2)}) collective-permute-start(s16[2,144,128]{2,1,0:T(8,128)(2,1)S(1)} %get-tuple-element.51), channel_id=1, source_target_pairs={{0,10},{1,11},{2,12},{3,13},{4,14},{5,15},{6,0},{7,1},{8,2},{9,3},... | collective-permute-start | bytes 221192 | tf_op jit(solution)/shard_map/ppermute | solution.py:297
  49.7 2.2 %collective-permute-start.16 = (s16[2,144,128]{2,1,0:T(8,128)(2,1)S(1)}, s16[2,144,128]{2,1,0:T(8,128)(2,1)S(1)}, u32[]{:S(2)}, u32[]{:S(2)}) collective-permute-start(s16[2,144,128]{2,1,0:T(8,128)(2,1)S(1)} %get-tuple-element.52), channel_id=1, source_target_pairs={{0,2},{1,3},{2,4},{3,5},{4,6},{5,7},{6,8},{7,9},{8,10},{9,11},{10,... | collective-permute-start | bytes 221192 | tf_op jit(solution)/shard_map/ppermute | solution.py:297
  56.8 3.2 %collective-permute-start.20 = (s16[2,272,128]{2,1,0:T(8,128)(2,1)S(1)}, s16[2,272,128]{2,1,0:T(8,128)(2,1)S(1)}, u32[]{:S(2)}, u32[]{:S(2)}) collective-permute-start(s16[2,272,128]{2,1,0:T(8,128)(2,1)S(1)} %get-tuple-element.57), channel_id=1, source_target_pairs={{0,14},{1,15},{2,0},{3,1},{4,2},{5,3},{6,4},{7,5},{8,6},{9,7},{10,... | collective-permute-start | bytes 417800 | tf_op jit(solution)/shard_map/ppermute | solution.py:297
  60.0 3.4 %collective-permute-start.21 = (s16[1,272,128]{2,1,0:T(8,128)(2,1)S(1)}, s16[1,272,128]{2,1,0:T(8,128)(2,1)S(1)}, u32[]{:S(2)}, u32[]{:S(2)}) collective-permute-start(s16[1,272,128]{2,1,0:T(8,128)(2,1)S(1)} %get-tuple-element.58), channel_id=1, source_target_pairs={{0,12},{1,13},{2,14},{3,15},{4,0},{5,1},{6,2},{7,3},{8,4},{9,5},{1... | collective-permute-start | bytes 208904 | tf_op jit(solution)/shard_map/ppermute | solution.py:297
  63.5 2.4 %collective-permute-done.23.up_ref = s16[1,272,128]{2,1,0:T(8,128)(2,1)S(1)} collective-permute-done((s16[1,272,128]{2,1,0:T(8,128)(2,1)S(1)}, s16[1,272,128]{2,1,0:T(8,128)(2,1)S(1)}, u32[]{:S(2)}, u32[]{:S(2)}) %collective-permute-start.23) | collective-permute-done | bytes 69664 | tf_op jit(solution)/shard_map/ppermute | solution.py:297
  66.6 2.7 %collective-permute-start.24 = (s16[1,272,128]{2,1,0:T(8,128)(2,1)S(1)}, s16[1,272,128]{2,1,0:T(8,128)(2,1)S(1)}, u32[]{:S(2)}, u32[]{:S(2)}) collective-permute-start(s16[1,272,128]{2,1,0:T(8,128)(2,1)S(1)} %get-tuple-element.61), channel_id=1, source_target_pairs={{0,10},{1,11},{2,12},{3,13},{4,14},{5,15},{6,0},{7,1},{8,2},{9,3},... | collective-permute-start | bytes 208904 | tf_op jit(solution)/shard_map/ppermute | solution.py:297
  70.5 2.1 %collective-permute-start.19 = (s16[1,144,128]{2,1,0:T(8,128)(2,1)S(1)}, s16[1,144,128]{2,1,0:T(8,128)(2,1)S(1)}, u32[]{:S(2)}, u32[]{:S(2)}) collective-permute-start(s16[1,144,128]{2,1,0:T(8,128)(2,1)S(1)} %x_second.1), channel_id=1, source_target_pairs={{0,16},{1,17},{2,18},{3,19},{4,20},{5,21},{6,22},{7,23},{8,24},{9,... | collective-permute-start | bytes 110600 | tf_op jit(solution)/shard_map/ppermute | solution.py:297
  72.6 1.9 %collective-permute-done.19.rx2_ref = s16[1,144,128]{2,1,0:T(8,128)(2,1)S(1)} collective-permute-done((s16[1,144,128]{2,1,0:T(8,128)(2,1)S(1)}, s16[1,144,128]{2,1,0:T(8,128)(2,1)S(1)}, u32[]{:S(2)}, u32[]{:S(2)}) %collective-permute-start.19) | collective-permute-done | bytes 36896 | tf_op jit(solution)/shard_map/ppermute | solution.py:297
  74.8 1.7 %layer.1 = bf16[384,256]{1,0:T(8,128)(2,1)} custom-call(s32[5]{0:T(128)S(1)} %stack.23.place_ref.refs_0_, f32[97,128,128]{2,1,0:T(8,128)S(1)} %get-tuple-element.53.panel.panel_ref, s16[8,272,128]{2,1,0:T(8,128)(2,1)S(1)} %collective-permute-done.11.rc_ref.rc1_ref, s16[8,272,128]{2,1,0:T(8,128)(2,1)S(1)} %collective-permute-done.18.rx_ref.rx1_ref, ...), custom_call_target="tpu_custom_call" | custom-call | bytes 4500000 | tf_op jit(solution)/shard_map/layer/pallas_call | solution.py:37
  (53 shorter events, 16.7 us)
Async XLA Ops:
  0.0 9.7 %collective-permute-start = (bf16[384,128]{1,0:T(8,128)(2,1)}, bf16[384,128]{1,0:T(8,128)(2,1)S(1)}, u32[]{:S(2)}, u32[]{:S(2)}) collective-permute-start(bf16[384,128]{1,0:T(8,128)(2,1)} %own_ref.1), channel_id=1, source_target_pairs={{0,32},{32,0},{64,96},{96,64},{128,160},{160,128},{192,224},{224,1... | collective-permute-start | bytes 294920 | tf_op jit(solution)/shard_map/ppermute | solution.py:289
  2.1 7.6 %collective-permute-start.2 = (bf16[384,128]{1,0:T(8,128)(2,1)}, bf16[384,128]{1,0:T(8,128)(2,1)S(1)}, u32[]{:S(2)}, u32[]{:S(2)}) collective-permute-start(bf16[384,128]{1,0:T(8,128)(2,1)} %own_ref.1), channel_id=1, source_target_pairs={{0,192},{32,224},{64,0},{96,32},{128,64},{160,96},{192,128},{224,1... | collective-permute-start | bytes 294920 | tf_op jit(solution)/shard_map/ppermute | solution.py:289
  5.1 6.0 %collective-permute-start.1 = (bf16[384,128]{1,0:T(8,128)(2,1)}, bf16[384,128]{1,0:T(8,128)(2,1)S(1)}, u32[]{:S(2)}, u32[]{:S(2)}) collective-permute-start(bf16[384,128]{1,0:T(8,128)(2,1)} %own_ref.1), channel_id=1, source_target_pairs={{0,64},{32,96},{64,128},{96,160},{128,192},{160,224},{192,0},{224,... | collective-permute-start | bytes 294920 | tf_op jit(solution)/shard_map/ppermute | solution.py:289
  11.2 8.3 %collective-permute-start.4 = (bf16[384,128]{1,0:T(8,128)(2,1)S(1)}, bf16[384,128]{1,0:T(8,128)(2,1)S(1)}, u32[]{:S(2)}, u32[]{:S(2)}) collective-permute-start(bf16[384,128]{1,0:T(8,128)(2,1)S(1)} %collective-permute-done.refs_5_), channel_id=1, source_target_pairs={{0,192},{32,224},{64,0},{96,32},{128,64},{160,96},{192,128},{224,1... | collective-permute-start | bytes 294920 | tf_op jit(solution)/shard_map/ppermute | solution.py:289
  12.8 6.7 %collective-permute-start.3 = (bf16[384,128]{1,0:T(8,128)(2,1)S(1)}, bf16[384,128]{1,0:T(8,128)(2,1)S(1)}, u32[]{:S(2)}, u32[]{:S(2)}) collective-permute-start(bf16[384,128]{1,0:T(8,128)(2,1)S(1)} %collective-permute-done.refs_5_), channel_id=1, source_target_pairs={{0,64},{32,96},{64,128},{96,160},{128,192},{160,224},{192,0},{224,... | collective-permute-start | bytes 294920 | tf_op jit(solution)/shard_map/ppermute | solution.py:289
  13.2 6.2 %collective-permute-start.5 = (bf16[192,128]{1,0:T(8,128)(2,1)S(1)}, bf16[192,128]{1,0:T(8,128)(2,1)S(1)}, u32[]{:S(2)}, u32[]{:S(2)}) collective-permute-start(bf16[192,128]{1,0:T(8,128)(2,1)S(1)} %slice.12), channel_id=1, source_target_pairs={{0,64},{32,96},{64,128},{96,160},{128,192},{160,224},{192,0},{224,... | collective-permute-start | bytes 147464 | tf_op jit(solution)/shard_map/ppermute | solution.py:289
  13.3 6.2 %collective-permute-start.6 = (bf16[192,128]{1,0:T(8,128)(2,1)S(1)}, bf16[192,128]{1,0:T(8,128)(2,1)S(1)}, u32[]{:S(2)}, u32[]{:S(2)}) collective-permute-start(bf16[192,128]{1,0:T(8,128)(2,1)S(1)} %slice.13), channel_id=1, source_target_pairs={{0,192},{32,224},{64,0},{96,32},{128,64},{160,96},{192,128},{224,1... | collective-permute-start | bytes 147464 | tf_op jit(solution)/shard_map/ppermute | solution.py:289
  19.5 5.0 %collective-permute-start.8 = (bf16[192,128]{1,0:T(8,128)(2,1)S(1)}, bf16[192,128]{1,0:T(8,128)(2,1)S(1)}, u32[]{:S(2)}, u32[]{:S(2)}) collective-permute-start(bf16[192,128]{1,0:T(8,128)(2,1)S(1)} %slice.15), channel_id=1, source_target_pairs={{0,192},{32,224},{64,0},{96,32},{128,64},{160,96},{192,128},{224,1... | collective-permute-start | bytes 147464 | tf_op jit(solution)/shard_map/ppermute | solution.py:289
  21.9 5.3 %collective-permute-start.7 = (bf16[192,128]{1,0:T(8,128)(2,1)S(1)}, bf16[192,128]{1,0:T(8,128)(2,1)S(1)}, u32[]{:S(2)}, u32[]{:S(2)}) collective-permute-start(bf16[192,128]{1,0:T(8,128)(2,1)S(1)} %slice.14), channel_id=1, source_target_pairs={{0,64},{32,96},{64,128},{96,160},{128,192},{160,224},{192,0},{224,... | collective-permute-start | bytes 147464 | tf_op jit(solution)/shard_map/ppermute | solution.py:289
  30.1 4.9 %collective-permute-start.9 = (s16[16,144,128]{2,1,0:T(8,128)(2,1)S(1)}, s16[16,144,128]{2,1,0:T(8,128)(2,1)S(1)}, u32[]{:S(2)}, u32[]{:S(2)}) collective-permute-start(s16[16,144,128]{2,1,0:T(8,128)(2,1)S(1)} %core_second.1), channel_id=1, source_target_pairs={{0,1},{1,0},{2,3},{3,2},{4,5},{5,4},{6,7},{7,6},{8,9},{9,8},{10,11... | collective-permute-start | bytes 1769480 | tf_op jit(solution)/shard_map/ppermute | solution.py:297
  31.6 11.9 %collective-permute-start.11 = (s16[8,272,128]{2,1,0:T(8,128)(2,1)S(1)}, s16[8,272,128]{2,1,0:T(8,128)(2,1)S(1)}, u32[]{:S(2)}, u32[]{:S(2)}) collective-permute-start(s16[8,272,128]{2,1,0:T(8,128)(2,1)S(1)} %core_first.1), channel_id=1, source_target_pairs={{0,1},{1,0},{2,3},{3,2},{4,5},{5,4},{6,7},{7,6},{8,9},{9,8},{10,11... | collective-permute-start | bytes 1671176 | tf_op jit(solution)/shard_map/ppermute | solution.py:297
  32.7 23.2 %collective-permute-start.18 = (s16[8,272,128]{2,1,0:T(8,128)(2,1)S(1)}, s16[8,272,128]{2,1,0:T(8,128)(2,1)S(1)}, u32[]{:S(2)}, u32[]{:S(2)}) collective-permute-start(s16[8,272,128]{2,1,0:T(8,128)(2,1)S(1)} %x_first.1), channel_id=1, source_target_pairs={{0,16},{1,17},{2,18},{3,19},{4,20},{5,21},{6,22},{7,23},{8,24},{9,... | collective-permute-start | bytes 1671176 | tf_op jit(solution)/shard_map/ppermute | solution.py:297
  35.7 9.9 %collective-permute-start.10 = (s16[4,144,128]{2,1,0:T(8,128)(2,1)S(1)}, s16[4,144,128]{2,1,0:T(8,128)(2,1)S(1)}, u32[]{:S(2)}, u32[]{:S(2)}) collective-permute-start(s16[4,144,128]{2,1,0:T(8,128)(2,1)S(1)} %get-tuple-element.46), channel_id=1, source_target_pairs={{0,14},{1,15},{2,0},{3,1},{4,2},{5,3},{6,4},{7,5},{8,6},{9,7},{10,... | collective-permute-start | bytes 442376 | tf_op jit(solution)/shard_map/ppermute | solution.py:297
  41.4 5.6 %collective-permute-start.14 = (s16[2,144,128]{2,1,0:T(8,128)(2,1)S(1)}, s16[2,144,128]{2,1,0:T(8,128)(2,1)S(1)}, u32[]{:S(2)}, u32[]{:S(2)}) collective-permute-start(s16[2,144,128]{2,1,0:T(8,128)(2,1)S(1)} %get-tuple-element.50), channel_id=1, source_target_pairs={{0,2},{1,3},{2,4},{3,5},{4,6},{5,7},{6,8},{7,9},{8,10},{9,11},{10,... | collective-permute-start | bytes 221192 | tf_op jit(solution)/shard_map/ppermute | solution.py:297
  41.4 10.5 %collective-permute-start.12 = (s16[2,144,128]{2,1,0:T(8,128)(2,1)S(1)}, s16[2,144,128]{2,1,0:T(8,128)(2,1)S(1)}, u32[]{:S(2)}, u32[]{:S(2)}) collective-permute-start(s16[2,144,128]{2,1,0:T(8,128)(2,1)S(1)} %get-tuple-element.48), channel_id=1, source_target_pairs={{0,12},{1,13},{2,14},{3,15},{4,0},{5,1},{6,2},{7,3},{8,4},{9,5},{1... | collective-permute-start | bytes 221192 | tf_op jit(solution)/shard_map/ppermute | solution.py:297
  43.4 9.5 %collective-permute-start.13 = (s16[2,144,128]{2,1,0:T(8,128)(2,1)S(1)}, s16[2,144,128]{2,1,0:T(8,128)(2,1)S(1)}, u32[]{:S(2)}, u32[]{:S(2)}) collective-permute-start(s16[2,144,128]{2,1,0:T(8,128)(2,1)S(1)} %get-tuple-element.49), channel_id=1, source_target_pairs={{0,6},{1,7},{2,8},{3,9},{4,10},{5,11},{6,12},{7,13},{8,14},{9,15},... | collective-permute-start | bytes 221192 | tf_op jit(solution)/shard_map/ppermute | solution.py:297
  47.6 6.7 %collective-permute-start.15 = (s16[2,144,128]{2,1,0:T(8,128)(2,1)S(1)}, s16[2,144,128]{2,1,0:T(8,128)(2,1)S(1)}, u32[]{:S(2)}, u32[]{:S(2)}) collective-permute-start(s16[2,144,128]{2,1,0:T(8,128)(2,1)S(1)} %get-tuple-element.51), channel_id=1, source_target_pairs={{0,10},{1,11},{2,12},{3,13},{4,14},{5,15},{6,0},{7,1},{8,2},{9,3},... | collective-permute-start | bytes 221192 | tf_op jit(solution)/shard_map/ppermute | solution.py:297
  49.7 5.6 %collective-permute-start.16 = (s16[2,144,128]{2,1,0:T(8,128)(2,1)S(1)}, s16[2,144,128]{2,1,0:T(8,128)(2,1)S(1)}, u32[]{:S(2)}, u32[]{:S(2)}) collective-permute-start(s16[2,144,128]{2,1,0:T(8,128)(2,1)S(1)} %get-tuple-element.52), channel_id=1, source_target_pairs={{0,2},{1,3},{2,4},{3,5},{4,6},{5,7},{6,8},{7,9},{8,10},{9,11},{10,... | collective-permute-start | bytes 221192 | tf_op jit(solution)/shard_map/ppermute | solution.py:297
  56.8 6.7 %collective-permute-start.20 = (s16[2,272,128]{2,1,0:T(8,128)(2,1)S(1)}, s16[2,272,128]{2,1,0:T(8,128)(2,1)S(1)}, u32[]{:S(2)}, u32[]{:S(2)}) collective-permute-start(s16[2,272,128]{2,1,0:T(8,128)(2,1)S(1)} %get-tuple-element.57), channel_id=1, source_target_pairs={{0,14},{1,15},{2,0},{3,1},{4,2},{5,3},{6,4},{7,5},{8,6},{9,7},{10,... | collective-permute-start | bytes 417800 | tf_op jit(solution)/shard_map/ppermute | solution.py:297
  60.0 5.9 %collective-permute-start.23 = (s16[1,272,128]{2,1,0:T(8,128)(2,1)S(1)}, s16[1,272,128]{2,1,0:T(8,128)(2,1)S(1)}, u32[]{:S(2)}, u32[]{:S(2)}) collective-permute-start(s16[1,272,128]{2,1,0:T(8,128)(2,1)S(1)} %get-tuple-element.60), channel_id=1, source_target_pairs={{0,2},{1,3},{2,4},{3,5},{4,6},{5,7},{6,8},{7,9},{8,10},{9,11},{10,... | collective-permute-start | bytes 208904 | tf_op jit(solution)/shard_map/ppermute | solution.py:297
  60.0 14.6 %collective-permute-start.21 = (s16[1,272,128]{2,1,0:T(8,128)(2,1)S(1)}, s16[1,272,128]{2,1,0:T(8,128)(2,1)S(1)}, u32[]{:S(2)}, u32[]{:S(2)}) collective-permute-start(s16[1,272,128]{2,1,0:T(8,128)(2,1)S(1)} %get-tuple-element.58), channel_id=1, source_target_pairs={{0,12},{1,13},{2,14},{3,15},{4,0},{5,1},{6,2},{7,3},{8,4},{9,5},{1... | collective-permute-start | bytes 208904 | tf_op jit(solution)/shard_map/ppermute | solution.py:297
  63.4 11.2 %collective-permute-start.22 = (s16[1,272,128]{2,1,0:T(8,128)(2,1)S(1)}, s16[1,272,128]{2,1,0:T(8,128)(2,1)S(1)}, u32[]{:S(2)}, u32[]{:S(2)}) collective-permute-start(s16[1,272,128]{2,1,0:T(8,128)(2,1)S(1)} %get-tuple-element.59), channel_id=1, source_target_pairs={{0,6},{1,7},{2,8},{3,9},{4,10},{5,11},{6,12},{7,13},{8,14},{9,15},... | collective-permute-start | bytes 208904 | tf_op jit(solution)/shard_map/ppermute | solution.py:297
  66.6 8.0 %collective-permute-start.24 = (s16[1,272,128]{2,1,0:T(8,128)(2,1)S(1)}, s16[1,272,128]{2,1,0:T(8,128)(2,1)S(1)}, u32[]{:S(2)}, u32[]{:S(2)}) collective-permute-start(s16[1,272,128]{2,1,0:T(8,128)(2,1)S(1)} %get-tuple-element.61), channel_id=1, source_target_pairs={{0,10},{1,11},{2,12},{3,13},{4,14},{5,15},{6,0},{7,1},{8,2},{9,3},... | collective-permute-start | bytes 208904 | tf_op jit(solution)/shard_map/ppermute | solution.py:297
  69.2 5.5 %collective-permute-start.25 = (s16[1,272,128]{2,1,0:T(8,128)(2,1)S(1)}, s16[1,272,128]{2,1,0:T(8,128)(2,1)S(1)}, u32[]{:S(2)}, u32[]{:S(2)}) collective-permute-start(s16[1,272,128]{2,1,0:T(8,128)(2,1)S(1)} %get-tuple-element.62), channel_id=1, source_target_pairs={{0,2},{1,3},{2,4},{3,5},{4,6},{5,7},{6,8},{7,9},{8,10},{9,11},{10,... | collective-permute-start | bytes 208904 | tf_op jit(solution)/shard_map/ppermute | solution.py:297
  (5 other events, 27.4 us)

commit v2 on v1

--- a/solution.py
+++ b/solution.py
@@ -119,30 +119,26 @@
     add_list(panel, own, vals, count_ref, lists_ref, mine, 0, group_wait(vals_ref, vals, sems, mine, 0))
 
 
-def more_products(pieces, split, ahead, *refs):
-    place_ref, count_ref, lists_ref, _, vals_ref = refs[:5]
-    inputs = 5 + len(pieces) + 2 * len(split)
-    arrays, outputs = refs[5:inputs], refs[inputs:]
-    panel = outputs[0]
-    vals, sems, whole = outputs[-3:]
-    todo = [piece_of(place_ref, *which) for which in pieces + split]
+def more_products(pieces, ahead, place_ref, count_ref, lists_ref, _, vals_ref, *refs):
+    inputs = 1 + max(array for _, (array, _) in pieces)
+    pairs, (panel, *outputs) = refs[:inputs], refs[inputs:]
+    vals, sems = outputs[-2:]
+    todo = [piece_of(place_ref, *which) for which, _ in pieces]
     for k, j in enumerate(todo):
         fetch(vals_ref, vals, sems, count_ref, j, k)(lambda copy: copy.start())
-    if ahead:
-        next_vals, next_sems = outputs[1], outputs[2]
-        later = fetch(vals_ref, next_vals, next_sems, count_ref, piece_of(place_ref, *ahead), 0)
-        later(lambda copy: copy.start())
-    for k, j in enumerate(todo):
-        piece = whole
-        if k < len(pieces):
-            piece = arrays[k]
-        else:
-            first = len(pieces) + 2 * (k - len(pieces))
-            whole[:HALF, :] = arrays[first][...]
-            whole[HALF:, :] = arrays[first + 1][...]
-        add_list(panel, piece, vals, count_ref, lists_ref, j, k, group_wait(vals_ref, vals, sems, j, k))
-    if ahead:
-        later(lambda copy: copy.wait())
+    later = [
+        fetch(vals_ref, outputs[0], outputs[1], count_ref, piece_of(place_ref, *which), k)
+        for k, which in enumerate(ahead)
+    ]
+    for each in later:
+        each(lambda copy: copy.start())
+    for k, (j, (_, (array, half))) in enumerate(zip(todo, pieces)):
+        add_list(
+            panel, pairs[array].at[half], vals, count_ref, lists_ref, j, k,
+            group_wait(vals_ref, vals, sems, j, k),
+        )
+    for each in later:
+        each(lambda copy: copy.wait())
 
 
 def quantize(block):
@@ -205,11 +201,16 @@
             write_message(out_ref, k * 8 + z, here.partial(other, z, part, other_core=True))
 
 
-def last_products(which, place_ref, count_ref, lists_ref, _, vals, top_ref, bottom_ref, panel, out_ref, whole):
-    whole[:HALF, :] = top_ref[...]
-    whole[HALF:, :] = bottom_ref[...]
-    add_list(panel, whole, vals, count_ref, lists_ref, piece_of(place_ref, *which), 0)
+def last_products(pieces, place_ref, count_ref, lists_ref, _, vals, *refs):
+    *arrays, panel, out_ref = refs
+    for k, (which, piece) in enumerate(zip(pieces, arrays)):
+        add_list(panel, piece, vals, count_ref, lists_ref, piece_of(place_ref, *which), k)
     core_messages(FIRST, (True,), place_ref, panel, out_ref)
+
+
+def pair_up(first_ref, second_ref, out_ref):
+    out_ref[0] = first_ref[...]
+    out_ref[1] = second_ref[...]
 
 
 def x_messages(place_ref, panel, rc_ref, out_ref):
@@ -221,53 +222,53 @@
 
 
 def base_value(part, here, rc_ref, rx_ref, other, z):
-    if part == FIRST:
-        return add(
-            here.partial(other, z, part), read_message(rc_ref, z, part[1]), read_message(rx_ref, z, part[1])
-        )
-    return add(here.partial(other, z, part), read_message(rc_ref, other * 8 + z, part[1]))
+    value = add(here.partial(other, z, part), read_message(rc_ref, other * 8 + z, part[1]))
+    return value if rx_ref is None else add(value, read_message(rx_ref, z, part[1]))
 
 
 def sides(part):
     return (0,) if part == FIRST else (0, 1)
 
 
-def z_start(part, place_ref, panel, rc_ref, rx_ref, down_ref, up_ref, two_ref, far_ref):
+def z_start(part, place_ref, panel, rc_ref, rx_ref, relay_ref, down_ref, up_ref):
     here = Here(place_ref, panel)
     for other in sides(part):
         for out_ref, index, shift in (
-            (down_ref, 2 * other, -4), (down_ref, 2 * other + 1, -1), (up_ref, other, 2),
-            (two_ref, other, -2), (far_ref, other, 3),
+            (relay_ref, other, -4), (down_ref, 2 * other, -3), (up_ref, 2 * other, 3),
+            (down_ref, 2 * other + 1, -1), (up_ref, 2 * other + 1, 1),
         ):
             write_message(out_ref, index, base_value(part, here, rc_ref, rx_ref, other, here.z_of(shift)))
 
 
-def z_middle(part, place_ref, panel, rc_ref, rx_ref, down_ref, up_ref, three_ref, one_ref):
+def z_middle(part, place_ref, panel, rc_ref, rx_ref, relay_ref, down_ref, up_ref, below_ref, above_ref):
     here = Here(place_ref, panel)
     count = part[1]
     for other in sides(part):
         value = functools.partial(base_value, part, here, rc_ref, rx_ref, other)
-        write_message(three_ref, other, add(value(here.z_of(-3)), read_message(down_ref, 2 * other, count)))
-        write_message(one_ref, other, add(value(here.z_of(1)), read_message(up_ref, other, count)))
-
-
-def arrivals(part, other, down_ref, *refs):
-    return [read_message(down_ref, 2 * other + 1, part[1])] + [read_message(ref, other, part[1]) for ref in refs]
+        come = add(read_message(relay_ref, other, count), read_message(down_ref, 2 * other, count))
+        write_message(below_ref, other, add(value(here.z_of(-2)), come))
+        write_message(above_ref, other, add(value(here.z_of(2)), read_message(up_ref, 2 * other, count)))
+
+
+def arrivals(part, other, down_ref, up_ref, below_ref, above_ref):
+    straight = [read_message(ref, 2 * other + 1, part[1]) for ref in (down_ref, up_ref)]
+    return straight + [read_message(ref, other, part[1]) for ref in (below_ref, above_ref)]
 
 
 def z_end(place_ref, panel, rc_ref, *refs):
     here = Here(place_ref, panel)
+    *arrived, out_ref, sum_ref = refs
     value = base_value(SECOND, here, rc_ref, None, 1, here.z)
-    write_message(refs[5], 0, add(value, *arrivals(SECOND, 1, *refs[:5])))
-
-
-def layer(place_ref, panel, rc1_ref, rx1_ref, rc2_ref, rx2_ref, *refs):
-    here = Here(place_ref, panel)
-    weight_ref, out_ref = refs[10], refs[11]
-    first = base_value(FIRST, here, rc1_ref, rx1_ref, 0, here.z)
-    first = add(first, *arrivals(FIRST, 0, *refs[:5]))
-    second = base_value(SECOND, here, rc2_ref, None, 0, here.z)
-    second = add(second, read_message(rx2_ref, 0, 1), *arrivals(SECOND, 0, *refs[5:10]))
+    write_message(out_ref, 0, add(value, *arrivals(SECOND, 1, *arrived)))
+    value = base_value(SECOND, here, rc_ref, None, 0, here.z)
+    sum_ref[...] = add(value, *arrivals(SECOND, 0, *arrived))[0]
+
+
+def layer(place_ref, panel, rc_ref, rx_ref, sum_ref, rx2_ref, *refs):
+    here = Here(place_ref, panel)
+    *arrived, weight_ref, out_ref = refs
+    first = add(base_value(FIRST, here, rc_ref, rx_ref, 0, here.z), *arrivals(FIRST, 0, *arrived))
+    second = add([sum_ref[...]], read_message(rx2_ref, 0, SECOND[1]))
     weight = weight_ref[...]
     for i, block in enumerate(first + second):
         high = block.astype(jnp.bfloat16)
@@ -306,18 +307,17 @@
             return functools.partial(kernel, part)
         return lambda place_ref, panel_ref, rc_ref, *refs: kernel(part, place_ref, panel_ref, rc_ref, None, *refs)
 
-    down, up, two, far = call(
-        fill(z_start), name + "_start", (messages(2 * count, part),) + (messages(count, part),) * 3,
-        [SMEM] + [VMEM] * (1 + len(have)), (VMEM,) * 4, (place, panel, *have), 0.6,
-    )
-    down, up = send_rep(down, 0, -1, 0), send_rep(up, 0, 1, 0)
-    two, far = send_rep(two, 0, -2, 0), send_rep(far, 0, 3, 0)
+    relay, down, up = call(
+        fill(z_start), name + "_start", (messages(count, part), messages(2 * count, part), messages(2 * count, part)),
+        [SMEM] + [VMEM] * (1 + len(have)), (VMEM,) * 3, (place, panel, *have), 0.6,
+    )
+    relay, down, up = send_rep(relay, 0, -2, 0), send_rep(down, 0, -1, 0), send_rep(up, 0, 1, 0)
     down, also = lax.optimization_barrier((down, also))
-    three, one = call(
+    below, above = call(
         fill(z_middle), name + "_middle", (messages(count, part),) * 2,
-        [SMEM] + [VMEM] * (3 + len(have)), (VMEM,) * 2, (place, panel, *have, down, up), 0.6,
-    )
-    return (down, two, far, send_rep(three, 0, -3, 0), send_rep(one, 0, 1, 0)), also
+        [SMEM] + [VMEM] * (4 + len(have)), (VMEM,) * 2, (place, panel, *have, relay, down, up), 0.6,
+    )
+    return (down, up, send_rep(below, 0, -2, 0), send_rep(above, 0, 2, 0)), also
 
 
 def local(node_feats, block_vals, block_rows, block_cols, block_count, weight):
@@ -328,42 +328,43 @@
     lists = (place, block_count.reshape(1, LISTS), slots)
     vals = block_vals.reshape(LISTS * SLOTS, BS, BS)
     panel_type = jax.ShapeDtypeStruct((PANEL_BLK + 1, BS, F), jnp.float32)
-    list_type = jax.ShapeDtypeStruct((SLOTS, BS, BS), jnp.bfloat16)
     piece_buffer = pltpu.VMEM((PIECE_ROWS, F), jnp.bfloat16)
 
     def list_buffers(count):
         return [pltpu.VMEM((count * SLOTS, BS, BS), jnp.bfloat16), pltpu.SemaphoreType.DMA((count * GROUPS,))]
 
     own = node_feats
-    flipped, below, above = send_blk(own, 0, 1), send_blk(own, 1), send_blk(own, -1)
+    flipped = send_blk(own, 0, 1)
     panel = call(
         first_products, "products_own", panel_type, [SMEM] * 3 + [ANY] * 2, VMEM, (*lists, own, vals), 3, 41,
         scratch_shapes=[piece_buffer, *list_buffers(1), pltpu.SemaphoreType.DMA],
     )
-    panel, flipped, below, above = lax.optimization_barrier((panel, flipped, below, above))
-    below_flipped, above_flipped = send_blk(flipped, 1), send_blk(flipped, -1)
-    far = send_blk(below[:HALF], 1), send_blk(above[HALF:], -1)
+    panel, flipped = lax.optimization_barrier((panel, flipped))
+    pair = call(
+        pair_up, "pair", jax.ShapeDtypeStruct((2, PIECE_ROWS, F), jnp.bfloat16), [VMEM] * 2, VMEM, (own, flipped), 0.3
+    )
+    below, above = send_blk(pair, 1), send_blk(pair, -1)
     panel = call(
-        functools.partial(more_products, ((0, True), (3, False), (1, False)), (), None), "products_near", panel_type,
-        [SMEM] * 3 + [VMEM, ANY] + [VMEM] * 3, VMEM, (*lists, panel, vals, flipped, below, above), 4, 41,
+        functools.partial(more_products, (((0, True), (0, 1)),), ()), "products_flipped", panel_type,
+        [SMEM] * 3 + [VMEM, ANY, VMEM], VMEM, (*lists, panel, vals, pair), 3, 41,
         input_output_aliases={3: 0},
-        scratch_shapes=[*list_buffers(3), piece_buffer],
-    )
-    panel, below_flipped, above_flipped, far = lax.optimization_barrier((panel, below_flipped, above_flipped, far))
-    far_flipped = send_blk(below_flipped[:HALF], 1), send_blk(above_flipped[HALF:], -1)
+        scratch_shapes=list_buffers(1),
+    )
+    panel, below, above = lax.optimization_barrier((panel, below, above))
+    far = send_blk(below[0], 1), send_blk(above[1], -1)
+    far_pieces = (2, False), (2, True)
+    near_pieces = ((3, False), (0, 0)), ((3, True), (0, 1)), ((1, False), (1, 0)), ((1, True), (1, 1))
     panel, last_vals = call(
-        functools.partial(more_products, ((3, True), (1, True)), ((2, False),), (2, True)),
-        "products_near_flipped", (panel_type, list_type),
-        [SMEM] * 3 + [VMEM, ANY] + [VMEM] * 4, (VMEM,) * 2,
-        (*lists, panel, vals, below_flipped, above_flipped, *far), 3, 41,
+        functools.partial(more_products, near_pieces, far_pieces), "products_near",
+        (panel_type, jax.ShapeDtypeStruct((2 * SLOTS, BS, BS), jnp.bfloat16)),
+        [SMEM] * 3 + [VMEM, ANY] + [VMEM] * 2, (VMEM,) * 2, (*lists, panel, vals, below, above), 3, 41,
         input_output_aliases={3: 0},
-        scratch_shapes=[pltpu.SemaphoreType.DMA((GROUPS,)), *list_buffers(3), piece_buffer],
+        scratch_shapes=[pltpu.SemaphoreType.DMA((2 * GROUPS,)), *list_buffers(4)],
     )
     panel, to_core = call(
-        functools.partial(last_products, (2, True)), "products_far", (panel_type, messages(8, FIRST)),
-        [SMEM] * 3 + [VMEM] * 4, (VMEM,) * 2, (*lists, panel, last_vals, *far_flipped), 3, 40,
+        functools.partial(last_products, far_pieces), "products_far", (panel_type, messages(8, FIRST)),
+        [SMEM] * 3 + [VMEM] * 4, (VMEM,) * 2, (*lists, panel, last_vals, *far), 3, 40,
         input_output_aliases={3: 0},
-        scratch_shapes=[piece_buffer],
     )
 
     def to_other_core(name, part, other_x):
@@ -378,15 +379,16 @@
     to_x = call(x_messages, "x_first", messages(8, FIRST), [SMEM, VMEM, VMEM], VMEM, (place, panel, rc_cross), 0.6)
     rx_first = send_rep(to_x, 1, 0, 0)
     second, rc_first = sum_along_z(SECOND, "second", place, panel, rc_second, None, rc_first)
-    to_x = call(
-        z_end, "x_second", messages(1, SECOND), [SMEM] + [VMEM] * 7, VMEM, (place, panel, rc_second, *second), 0.6
+    to_x, own_sum = call(
+        z_end, "x_second", (messages(1, SECOND), jax.ShapeDtypeStruct((BS, F), jnp.float32)),
+        [SMEM] + [VMEM] * 6, (VMEM,) * 2, (place, panel, rc_second, *second), 0.6,
     )
     panel, to_x = lax.optimization_barrier((panel, to_x))
     rx_second = send_rep(to_x, 1, 0, 0)
     first, _ = sum_along_z(FIRST, "first", place, panel, rc_first, rx_first)
     return call(
-        layer, "layer", jax.ShapeDtypeStruct((PIECE_ROWS, H), jnp.bfloat16), [SMEM] + [VMEM] * 16, VMEM,
-        (place, panel, rc_first, rx_first, rc_second, rx_second, *first, *second, weight), 1.5,
+        layer, "layer", jax.ShapeDtypeStruct((PIECE_ROWS, H), jnp.bfloat16), [SMEM] + [VMEM] * 10, VMEM,
+        (place, panel, rc_first, rx_first, own_sum, rx_second, *first, weight), 1.5,
     )
 
 

time: 76.5 us -> 77.6 us (1.014)
  waiting for transfers between devices: 15.7 us -> 25.8 us
  starting transfers between devices: 40.6 us -> 30.7 us
    ppermute x17 -> x15, waiting for transfers between devices: 11.5 us -> 20.5 us  [send_rep(): return lax.ppermute(array, 'rep', pairs)]
    ppermute x17 -> x15, starting transfers between devices: 27.7 us -> 22.4 us  [send_rep(): return lax.ppermute(array, 'rep', pairs)]
    ppermute x9 -> x5, starting transfers between devices: 12.9 us -> 8.25 us  [send_blk(): return lax.ppermute(array, 'blk', pairs)]
    ppermute x9 -> x5, waiting for transfers between devices: 4.22 us -> 5.31 us  [send_blk(): return lax.ppermute(array, 'blk', pairs)]
    pallas_call x13 -> x14, Pallas kernels: 17.6 us -> 17.9 us  [call(): pl.pallas_call(kernel, out_shape=out_shape, in_specs=in_specs, out_specs=...]
  transfers between devices with their start and end apart: 26 -> 20, of which waited for: 11 -> 12; matrix products, arithmetic and copies ran while one was open for 1% -> 1% of each run, Pallas kernels for 18% -> 17%
where the time goes in v2:
time: 77.6 us; the launch traced here: 76.9 us
  starting transfers between devices  30.7 us (40%)
  waiting for transfers between devices  25.8 us (33%)
  Pallas kernels  17.9 us (23%)
  local copies, waits for them, and re-layouts  1.65 us (2%)
    ppermute x15, starting transfers between devices, send_rep(): return lax.ppermute(array, 'rep', pairs)  22.4 us
    ppermute x15, waiting for transfers between devices, send_rep(): return lax.ppermute(array, 'rep', pairs)  20.5 us
    pallas_call x14, Pallas kernels, call(): pl.pallas_call(kernel, out_shape=out_shape, in_specs=in_specs, out_specs=...  17.9 us
    ppermute x5, starting transfers between devices, send_blk(): return lax.ppermute(array, 'blk', pairs)  8.25 us
    ppermute x5, waiting for transfers between devices, send_blk(): return lax.ppermute(array, 'blk', pairs)  5.31 us
    unnamed x6, local copies, waits for them, and re-layouts  1.55 us
  transfers between devices with their start and end apart: 20, of which 12 were waited for; matrix products, arithmetic and copies ran while one was open for 1% of the time, Pallas kernels for 17%

profile of v2, /device:TPU:2, one launch (start us, length us, event | category | flops | bytes accessed | tf_op | source)
XLA Modules:
  0.0 76.9 jit_solution(5350964716629223752)
XLA Ops:
  0.0 2.1 %collective-permute-start = (bf16[384,128]{1,0:T(8,128)(2,1)}, bf16[384,128]{1,0:T(8,128)(2,1)S(1)}, u32[]{:S(2)}, u32[]{:S(2)}) collective-permute-start(bf16[384,128]{1,0:T(8,128)(2,1)} %first_ref.1), channel_id=1, source_target_pairs={{0,32},{32,0},{64,96},{96,64},{128,160},{160,128},{192,224},{224,1... | collective-permute-start | bytes 294920 | tf_op jit(solution)/shard_map/ppermute | solution.py:290
  4.5 2.0 %products_own.1._ = f32[97,128,128]{2,1,0:T(8,128)S(1)} custom-call(s32[5]{0:T(128)S(1)} %stack.23.place_ref, s32[1,8]{1,0:T(1,128)S(1)} %bitcast.13, s32[8,40]{1,0:T(8,128)S(1)} %add_bitcast_fusion.lists_ref, bf16[384,128]{1,0:T(8,128)(2,1)S(1)} %copy-done, bf16[320,128,128]{2,1,0:T(8,128)(2,1)} %bitcast.17), custom_call_target="tpu_custom_call" | custom-call | bytes 9000000 | tf_op jit(solution)/shard_map/products_own/pallas_call | solution.py:37
  6.5 4.0 %collective-permute-start.2 = (bf16[2,384,128]{2,1,0:T(8,128)(2,1)S(1)}, bf16[2,384,128]{2,1,0:T(8,128)(2,1)S(1)}, u32[]{:S(2)}, u32[]{:S(2)}) collective-permute-start(bf16[2,384,128]{2,1,0:T(8,128)(2,1)S(1)} %pair.1.refs_0_), channel_id=1, source_target_pairs={{0,192},{32,224},{64,0},{96,32},{128,64},{160,96},{192,128},{224,1... | collective-permute-start | bytes 589832 | tf_op jit(solution)/shard_map/ppermute | solution.py:290
  10.5 2.1 %products_flipped.1._ = f32[97,128,128]{2,1,0:T(8,128)S(1)} custom-call(s32[5]{0:T(128)S(1)} %stack.23.place_ref, s32[1,8]{1,0:T(1,128)S(1)} %bitcast.14, s32[8,40]{1,0:T(8,128)S(1)} %add_bitcast_fusion.lists_ref, f32[97,128,128]{2,1,0:T(8,128)S(1)} %products_own.1._, bf16[320,128,128]{2,1,0:T(8,128)(2,1)} %bitcast.18, ...), custom_call_target="tpu_custom_call", output_to_operand_aliasing={{}: (3, {})} | custom-call | bytes 9000000 | tf_op jit(solution)/shard_map/products_flipped/pallas_call | solution.py:37
  13.7 3.7 %collective-permute-done.1.refs_0_ = bf16[2,384,128]{2,1,0:T(8,128)(2,1)S(1)} collective-permute-done((bf16[2,384,128]{2,1,0:T(8,128)(2,1)S(1)}, bf16[2,384,128]{2,1,0:T(8,128)(2,1)S(1)}, u32[]{:S(2)}, u32[]{:S(2)}) %collective-permute-start.1) | collective-permute-done | bytes 196640 | tf_op jit(solution)/shard_map/ppermute | solution.py:290
  17.5 2.0 %collective-permute-start.3 = (bf16[384,128]{1,0:T(8,128)(2,1)S(1)}, bf16[384,128]{1,0:T(8,128)(2,1)S(1)}, u32[]{:S(2)}, u32[]{:S(2)}) collective-permute-start(bf16[384,128]{1,0:T(8,128)(2,1)S(1)} %slice_bitcast_fusion.1), channel_id=1, source_target_pairs={{0,64},{32,96},{64,128},{96,160},{128,192},{160,224},{192,0},{224,... | collective-permute-start | bytes 294920 | tf_op jit(solution)/shard_map/ppermute | solution.py:290
  19.5 3.3 %products_near.1 = (f32[97,128,128]{2,1,0:T(8,128)S(1)}, bf16[80,128,128]{2,1,0:T(8,128)(2,1)S(1)}) custom-call(s32[5]{0:T(128)S(1)} %stack.23.place_ref, s32[1,8]{1,0:T(1,128)S(1)} %bitcast.15, s32[8,40]{1,0:T(8,128)S(1)} %add_bitcast_fusion.lists_ref, f32[97,128,128]{2,1,0:T(8,128)S(1)} %products_flipped.1._, ...), custom_call_target="tpu_custom_call", output_to_operand_aliasing={{0}: (3, {})} | custom-call | bytes 9000000 | tf_op jit(solution)/shard_map/products_near/pallas_call | solution.py:37
  23.4 2.0 %products_far.1 = (f32[97,128,128]{2,1,0:T(8,128)S(1)}, s16[8,272,128]{2,1,0:T(8,128)(2,1)S(1)}) custom-call(s32[5]{0:T(128)S(1)} %stack.23.place_ref, s32[1,8]{1,0:T(1,128)S(1)} %bitcast.16, s32[8,40]{1,0:T(8,128)S(1)} %add_bitcast_fusion.lists_ref, f32[97,128,128]{2,1,0:T(8,128)S(1)} %get-tuple-element.35._, ...), custom_call_target="tpu_custom_call", output_to_operand_aliasing={{0}: (3, {})} | custom-call | bytes 9000000 | tf_op jit(solution)/shard_map/products_far/pallas_call | solution.py:37
  29.4 4.0 %collective-permute-start.13 = (s16[8,272,128]{2,1,0:T(8,128)(2,1)S(1)}, s16[8,272,128]{2,1,0:T(8,128)(2,1)S(1)}, u32[]{:S(2)}, u32[]{:S(2)}) collective-permute-start(s16[8,272,128]{2,1,0:T(8,128)(2,1)S(1)} %x_first.1), channel_id=1, source_target_pairs={{0,16},{1,17},{2,18},{3,19},{4,20},{5,21},{6,22},{7,23},{8,24},{9,... | collective-permute-start | bytes 1671176 | tf_op jit(solution)/shard_map/ppermute | solution.py:298
  34.2 3.8 %collective-permute-start.6 = (s16[4,144,128]{2,1,0:T(8,128)(2,1)S(1)}, s16[4,144,128]{2,1,0:T(8,128)(2,1)S(1)}, u32[]{:S(2)}, u32[]{:S(2)}) collective-permute-start(s16[4,144,128]{2,1,0:T(8,128)(2,1)S(1)} %get-tuple-element.38), channel_id=1, source_target_pairs={{0,14},{1,15},{2,0},{3,1},{4,2},{5,3},{6,4},{7,5},{8,6},{9,7},{10,... | collective-permute-start | bytes 442376 | tf_op jit(solution)/shard_map/ppermute | solution.py:298
  38.0 1.9 %collective-permute-start.9 = (s16[2,144,128]{2,1,0:T(8,128)(2,1)S(1)}, s16[2,144,128]{2,1,0:T(8,128)(2,1)S(1)}, u32[]{:S(2)}, u32[]{:S(2)}) collective-permute-start(s16[2,144,128]{2,1,0:T(8,128)(2,1)S(1)} %get-tuple-element.41), channel_id=1, source_target_pairs={{0,12},{1,13},{2,14},{3,15},{4,0},{5,1},{6,2},{7,3},{8,4},{9,5},{1... | collective-permute-start | bytes 221192 | tf_op jit(solution)/shard_map/ppermute | solution.py:298
  40.0 2.2 %collective-permute-done.6.refs_1_.refs_0_ = s16[4,144,128]{2,1,0:T(8,128)(2,1)S(1)} collective-permute-done((s16[4,144,128]{2,1,0:T(8,128)(2,1)S(1)}, s16[4,144,128]{2,1,0:T(8,128)(2,1)S(1)}, u32[]{:S(2)}, u32[]{:S(2)}) %collective-permute-start.6) | collective-permute-done | bytes 147488 | tf_op jit(solution)/shard_map/ppermute | solution.py:298
  42.1 2.6 %collective-permute-done.9.refs_0_ = s16[2,144,128]{2,1,0:T(8,128)(2,1)S(1)} collective-permute-done((s16[2,144,128]{2,1,0:T(8,128)(2,1)S(1)}, s16[2,144,128]{2,1,0:T(8,128)(2,1)S(1)}, u32[]{:S(2)}, u32[]{:S(2)}) %collective-permute-start.9) | collective-permute-done | bytes 73760 | tf_op jit(solution)/shard_map/ppermute | solution.py:298
  45.6 3.2 %collective-permute-start.10 = (s16[2,144,128]{2,1,0:T(8,128)(2,1)S(1)}, s16[2,144,128]{2,1,0:T(8,128)(2,1)S(1)}, u32[]{:S(2)}, u32[]{:S(2)}) collective-permute-start(s16[2,144,128]{2,1,0:T(8,128)(2,1)S(1)} %get-tuple-element.42), channel_id=1, source_target_pairs={{0,12},{1,13},{2,14},{3,15},{4,0},{5,1},{6,2},{7,3},{8,4},{9,5},{1... | collective-permute-start | bytes 221192 | tf_op jit(solution)/shard_map/ppermute | solution.py:298
  48.8 3.5 %collective-permute-done.10.refs_2_ = s16[2,144,128]{2,1,0:T(8,128)(2,1)S(1)} collective-permute-done((s16[2,144,128]{2,1,0:T(8,128)(2,1)S(1)}, s16[2,144,128]{2,1,0:T(8,128)(2,1)S(1)}, u32[]{:S(2)}, u32[]{:S(2)}) %collective-permute-start.10) | collective-permute-done | bytes 73760 | tf_op jit(solution)/shard_map/ppermute | solution.py:298
  52.3 3.7 %collective-permute-done.11.refs_3_ = s16[2,144,128]{2,1,0:T(8,128)(2,1)S(1)} collective-permute-done((s16[2,144,128]{2,1,0:T(8,128)(2,1)S(1)}, s16[2,144,128]{2,1,0:T(8,128)(2,1)S(1)}, u32[]{:S(2)}, u32[]{:S(2)}) %collective-permute-start.11) | collective-permute-done | bytes 73760 | tf_op jit(solution)/shard_map/ppermute | solution.py:298
  57.7 2.0 %collective-permute-start.16 = (s16[2,272,128]{2,1,0:T(8,128)(2,1)S(1)}, s16[2,272,128]{2,1,0:T(8,128)(2,1)S(1)}, u32[]{:S(2)}, u32[]{:S(2)}) collective-permute-start(s16[2,272,128]{2,1,0:T(8,128)(2,1)S(1)} %get-tuple-element.51), channel_id=1, source_target_pairs={{0,2},{1,3},{2,4},{3,5},{4,6},{5,7},{6,8},{7,9},{8,10},{9,11},{10,... | collective-permute-start | bytes 417800 | tf_op jit(solution)/shard_map/ppermute | solution.py:298
  59.7 1.6 %collective-permute-start.17 = (s16[1,272,128]{2,1,0:T(8,128)(2,1)S(1)}, s16[1,272,128]{2,1,0:T(8,128)(2,1)S(1)}, u32[]{:S(2)}, u32[]{:S(2)}) collective-permute-start(s16[1,272,128]{2,1,0:T(8,128)(2,1)S(1)} %get-tuple-element.52), channel_id=1, source_target_pairs={{0,12},{1,13},{2,14},{3,15},{4,0},{5,1},{6,2},{7,3},{8,4},{9,5},{1... | collective-permute-start | bytes 208904 | tf_op jit(solution)/shard_map/ppermute | solution.py:298
  61.3 2.6 %collective-permute-done.15.down_ref.refs_0_ = s16[2,272,128]{2,1,0:T(8,128)(2,1)S(1)} collective-permute-done((s16[2,272,128]{2,1,0:T(8,128)(2,1)S(1)}, s16[2,272,128]{2,1,0:T(8,128)(2,1)S(1)}, u32[]{:S(2)}, u32[]{:S(2)}) %collective-permute-start.15) | collective-permute-done | bytes 139296 | tf_op jit(solution)/shard_map/ppermute | solution.py:298
  65.8 3.1 %collective-permute-start.18 = (s16[1,272,128]{2,1,0:T(8,128)(2,1)S(1)}, s16[1,272,128]{2,1,0:T(8,128)(2,1)S(1)}, u32[]{:S(2)}, u32[]{:S(2)}) collective-permute-start(s16[1,272,128]{2,1,0:T(8,128)(2,1)S(1)} %get-tuple-element.53), channel_id=1, source_target_pairs={{0,12},{1,13},{2,14},{3,15},{4,0},{5,1},{6,2},{7,3},{8,4},{9,5},{1... | collective-permute-start | bytes 208904 | tf_op jit(solution)/shard_map/ppermute | solution.py:298
  68.8 1.9 %collective-permute-start.14 = (s16[1,144,128]{2,1,0:T(8,128)(2,1)S(1)}, s16[1,144,128]{2,1,0:T(8,128)(2,1)S(1)}, u32[]{:S(2)}, u32[]{:S(2)}) collective-permute-start(s16[1,144,128]{2,1,0:T(8,128)(2,1)S(1)} %get-tuple-element.49), channel_id=1, source_target_pairs={{0,16},{1,17},{2,18},{3,19},{4,20},{5,21},{6,22},{7,23},{8,24},{9,... | collective-permute-start | bytes 110600 | tf_op jit(solution)/shard_map/ppermute | solution.py:298
  70.7 2.1 %collective-permute-done.14.rx2_ref = s16[1,144,128]{2,1,0:T(8,128)(2,1)S(1)} collective-permute-done((s16[1,144,128]{2,1,0:T(8,128)(2,1)S(1)}, s16[1,144,128]{2,1,0:T(8,128)(2,1)S(1)}, u32[]{:S(2)}, u32[]{:S(2)}) %collective-permute-start.14) | collective-permute-done | bytes 36896 | tf_op jit(solution)/shard_map/ppermute | solution.py:298
  72.8 2.5 %collective-permute-done.19.refs_3_ = s16[1,272,128]{2,1,0:T(8,128)(2,1)S(1)} collective-permute-done((s16[1,272,128]{2,1,0:T(8,128)(2,1)S(1)}, s16[1,272,128]{2,1,0:T(8,128)(2,1)S(1)}, u32[]{:S(2)}, u32[]{:S(2)}) %collective-permute-start.19) | collective-permute-done | bytes 69664 | tf_op jit(solution)/shard_map/ppermute | solution.py:298
  75.3 1.6 %layer.1 = bf16[384,256]{1,0:T(8,128)(2,1)} custom-call(s32[5]{0:T(128)S(1)} %stack.23.place_ref, f32[97,128,128]{2,1,0:T(8,128)S(1)} %get-tuple-element.45.panel.panel_ref, s16[8,272,128]{2,1,0:T(8,128)(2,1)S(1)} %collective-permute-done.7.rc_ref, s16[8,272,128]{2,1,0:T(8,128)(2,1)S(1)} %collective-permute-done.13.rx_ref, ...), custom_call_target="tpu_custom_call" | custom-call | bytes 4500000 | tf_op jit(solution)/shard_map/layer/pallas_call | solution.py:37
  (40 shorter events, 13.2 us)
Async XLA Ops:
  0.0 6.5 %collective-permute-start = (bf16[384,128]{1,0:T(8,128)(2,1)}, bf16[384,128]{1,0:T(8,128)(2,1)S(1)}, u32[]{:S(2)}, u32[]{:S(2)}) collective-permute-start(bf16[384,128]{1,0:T(8,128)(2,1)} %first_ref.1), channel_id=1, source_target_pairs={{0,32},{32,0},{64,96},{96,64},{128,160},{160,128},{192,224},{224,1... | collective-permute-start | bytes 294920 | tf_op jit(solution)/shard_map/ppermute | solution.py:290
  2.9 0.9 %copy-start = (bf16[384,128]{1,0:T(8,128)(2,1)S(1)}, bf16[384,128]{1,0:T(8,128)(2,1)}, u32[]{:S(2)}) copy-start(bf16[384,128]{1,0:T(8,128)(2,1)} %first_ref.1) | copy-start | bytes 294916
  3.8 0.7 copy-start.2
  6.5 7.2 %collective-permute-start.2 = (bf16[2,384,128]{2,1,0:T(8,128)(2,1)S(1)}, bf16[2,384,128]{2,1,0:T(8,128)(2,1)S(1)}, u32[]{:S(2)}, u32[]{:S(2)}) collective-permute-start(bf16[2,384,128]{2,1,0:T(8,128)(2,1)S(1)} %pair.1.refs_0_), channel_id=1, source_target_pairs={{0,192},{32,224},{64,0},{96,32},{128,64},{160,96},{192,128},{224,1... | collective-permute-start | bytes 589832 | tf_op jit(solution)/shard_map/ppermute | solution.py:290
  10.5 6.9 %collective-permute-start.1 = (bf16[2,384,128]{2,1,0:T(8,128)(2,1)S(1)}, bf16[2,384,128]{2,1,0:T(8,128)(2,1)S(1)}, u32[]{:S(2)}, u32[]{:S(2)}) collective-permute-start(bf16[2,384,128]{2,1,0:T(8,128)(2,1)S(1)} %pair.1.refs_0_), channel_id=1, source_target_pairs={{0,64},{32,96},{64,128},{96,160},{128,192},{160,224},{192,0},{224,... | collective-permute-start | bytes 589832 | tf_op jit(solution)/shard_map/ppermute | solution.py:290
  17.4 5.5 %collective-permute-start.4 = (bf16[384,128]{1,0:T(8,128)(2,1)S(1)}, bf16[384,128]{1,0:T(8,128)(2,1)S(1)}, u32[]{:S(2)}, u32[]{:S(2)}) collective-permute-start(bf16[384,128]{1,0:T(8,128)(2,1)S(1)} %slice_bitcast_fusion), channel_id=1, source_target_pairs={{0,192},{32,224},{64,0},{96,32},{128,64},{160,96},{192,128},{224,1... | collective-permute-start | bytes 294920 | tf_op jit(solution)/shard_map/ppermute | solution.py:290
  17.5 5.9 %collective-permute-start.3 = (bf16[384,128]{1,0:T(8,128)(2,1)S(1)}, bf16[384,128]{1,0:T(8,128)(2,1)S(1)}, u32[]{:S(2)}, u32[]{:S(2)}) collective-permute-start(bf16[384,128]{1,0:T(8,128)(2,1)S(1)} %slice_bitcast_fusion.1), channel_id=1, source_target_pairs={{0,64},{32,96},{64,128},{96,160},{128,192},{160,224},{192,0},{224,... | collective-permute-start | bytes 294920 | tf_op jit(solution)/shard_map/ppermute | solution.py:290
  25.4 2.9 %collective-permute-start.12 = (s16[8,272,128]{2,1,0:T(8,128)(2,1)S(1)}, s16[8,272,128]{2,1,0:T(8,128)(2,1)S(1)}, u32[]{:S(2)}, u32[]{:S(2)}) collective-permute-start(s16[8,272,128]{2,1,0:T(8,128)(2,1)S(1)} %get-tuple-element.47), channel_id=1, source_target_pairs={{0,1},{1,0},{2,3},{3,2},{4,5},{5,4},{6,7},{7,6},{8,9},{9,8},{10,11... | collective-permute-start | bytes 1671176 | tf_op jit(solution)/shard_map/ppermute | solution.py:298
  26.7 6.7 %collective-permute-start.5 = (s16[16,144,128]{2,1,0:T(8,128)(2,1)S(1)}, s16[16,144,128]{2,1,0:T(8,128)(2,1)S(1)}, u32[]{:S(2)}, u32[]{:S(2)}) collective-permute-start(s16[16,144,128]{2,1,0:T(8,128)(2,1)S(1)} %core_second.1), channel_id=1, source_target_pairs={{0,1},{1,0},{2,3},{3,2},{4,5},{5,4},{6,7},{7,6},{8,9},{9,8},{10,11... | collective-permute-start | bytes 1769480 | tf_op jit(solution)/shard_map/ppermute | solution.py:298
  28.3 11.7 %collective-permute-start.7 = (s16[8,272,128]{2,1,0:T(8,128)(2,1)S(1)}, s16[8,272,128]{2,1,0:T(8,128)(2,1)S(1)}, u32[]{:S(2)}, u32[]{:S(2)}) collective-permute-start(s16[8,272,128]{2,1,0:T(8,128)(2,1)S(1)} %core_first.1), channel_id=1, source_target_pairs={{0,1},{1,0},{2,3},{3,2},{4,5},{5,4},{6,7},{7,6},{8,9},{9,8},{10,11... | collective-permute-start | bytes 1671176 | tf_op jit(solution)/shard_map/ppermute | solution.py:298
  29.4 27.3 %collective-permute-start.13 = (s16[8,272,128]{2,1,0:T(8,128)(2,1)S(1)}, s16[8,272,128]{2,1,0:T(8,128)(2,1)S(1)}, u32[]{:S(2)}, u32[]{:S(2)}) collective-permute-start(s16[8,272,128]{2,1,0:T(8,128)(2,1)S(1)} %x_first.1), channel_id=1, source_target_pairs={{0,16},{1,17},{2,18},{3,19},{4,20},{5,21},{6,22},{7,23},{8,24},{9,... | collective-permute-start | bytes 1671176 | tf_op jit(solution)/shard_map/ppermute | solution.py:298
  34.2 7.9 %collective-permute-start.6 = (s16[4,144,128]{2,1,0:T(8,128)(2,1)S(1)}, s16[4,144,128]{2,1,0:T(8,128)(2,1)S(1)}, u32[]{:S(2)}, u32[]{:S(2)}) collective-permute-start(s16[4,144,128]{2,1,0:T(8,128)(2,1)S(1)} %get-tuple-element.38), channel_id=1, source_target_pairs={{0,14},{1,15},{2,0},{3,1},{4,2},{5,3},{6,4},{7,5},{8,6},{9,7},{10,... | collective-permute-start | bytes 442376 | tf_op jit(solution)/shard_map/ppermute | solution.py:298
  38.0 6.9 %collective-permute-start.8 = (s16[4,144,128]{2,1,0:T(8,128)(2,1)S(1)}, s16[4,144,128]{2,1,0:T(8,128)(2,1)S(1)}, u32[]{:S(2)}, u32[]{:S(2)}) collective-permute-start(s16[4,144,128]{2,1,0:T(8,128)(2,1)S(1)} %get-tuple-element.40), channel_id=1, source_target_pairs={{0,2},{1,3},{2,4},{3,5},{4,6},{5,7},{6,8},{7,9},{8,10},{9,11},{10,... | collective-permute-start | bytes 442376 | tf_op jit(solution)/shard_map/ppermute | solution.py:298
  38.0 6.7 %collective-permute-start.9 = (s16[2,144,128]{2,1,0:T(8,128)(2,1)S(1)}, s16[2,144,128]{2,1,0:T(8,128)(2,1)S(1)}, u32[]{:S(2)}, u32[]{:S(2)}) collective-permute-start(s16[2,144,128]{2,1,0:T(8,128)(2,1)S(1)} %get-tuple-element.41), channel_id=1, source_target_pairs={{0,12},{1,13},{2,14},{3,15},{4,0},{5,1},{6,2},{7,3},{8,4},{9,5},{1... | collective-permute-start | bytes 221192 | tf_op jit(solution)/shard_map/ppermute | solution.py:298
  45.6 6.7 %collective-permute-start.10 = (s16[2,144,128]{2,1,0:T(8,128)(2,1)S(1)}, s16[2,144,128]{2,1,0:T(8,128)(2,1)S(1)}, u32[]{:S(2)}, u32[]{:S(2)}) collective-permute-start(s16[2,144,128]{2,1,0:T(8,128)(2,1)S(1)} %get-tuple-element.42), channel_id=1, source_target_pairs={{0,12},{1,13},{2,14},{3,15},{4,0},{5,1},{6,2},{7,3},{8,4},{9,5},{1... | collective-permute-start | bytes 221192 | tf_op jit(solution)/shard_map/ppermute | solution.py:298
  48.8 7.2 %collective-permute-start.11 = (s16[2,144,128]{2,1,0:T(8,128)(2,1)S(1)}, s16[2,144,128]{2,1,0:T(8,128)(2,1)S(1)}, u32[]{:S(2)}, u32[]{:S(2)}) collective-permute-start(s16[2,144,128]{2,1,0:T(8,128)(2,1)S(1)} %get-tuple-element.43), channel_id=1, source_target_pairs={{0,4},{1,5},{2,6},{3,7},{4,8},{5,9},{6,10},{7,11},{8,12},{9,13},{1... | collective-permute-start | bytes 221192 | tf_op jit(solution)/shard_map/ppermute | solution.py:298
  56.7 18.6 %copy-start.1 = (bf16[128,256]{1,0:T(8,128)(2,1)S(1)}, bf16[128,256]{1,0:T(8,128)(2,1)}, u32[]{:S(2)}) copy-start(bf16[128,256]{1,0:T(8,128)(2,1)} %refs_4_.1) | copy-start | bytes 196612
  57.6 6.3 %collective-permute-start.15 = (s16[2,272,128]{2,1,0:T(8,128)(2,1)S(1)}, s16[2,272,128]{2,1,0:T(8,128)(2,1)S(1)}, u32[]{:S(2)}, u32[]{:S(2)}) collective-permute-start(s16[2,272,128]{2,1,0:T(8,128)(2,1)S(1)} %get-tuple-element.50), channel_id=1, source_target_pairs={{0,14},{1,15},{2,0},{3,1},{4,2},{5,3},{6,4},{7,5},{8,6},{9,7},{10,... | collective-permute-start | bytes 417800 | tf_op jit(solution)/shard_map/ppermute | solution.py:298
  57.7 7.4 %collective-permute-start.16 = (s16[2,272,128]{2,1,0:T(8,128)(2,1)S(1)}, s16[2,272,128]{2,1,0:T(8,128)(2,1)S(1)}, u32[]{:S(2)}, u32[]{:S(2)}) collective-permute-start(s16[2,272,128]{2,1,0:T(8,128)(2,1)S(1)} %get-tuple-element.51), channel_id=1, source_target_pairs={{0,2},{1,3},{2,4},{3,5},{4,6},{5,7},{6,8},{7,9},{8,10},{9,11},{10,... | collective-permute-start | bytes 417800 | tf_op jit(solution)/shard_map/ppermute | solution.py:298
  59.7 5.3 %collective-permute-start.17 = (s16[1,272,128]{2,1,0:T(8,128)(2,1)S(1)}, s16[1,272,128]{2,1,0:T(8,128)(2,1)S(1)}, u32[]{:S(2)}, u32[]{:S(2)}) collective-permute-start(s16[1,272,128]{2,1,0:T(8,128)(2,1)S(1)} %get-tuple-element.52), channel_id=1, source_target_pairs={{0,12},{1,13},{2,14},{3,15},{4,0},{5,1},{6,2},{7,3},{8,4},{9,5},{1... | collective-permute-start | bytes 208904 | tf_op jit(solution)/shard_map/ppermute | solution.py:298
  65.8 7.0 %collective-permute-start.18 = (s16[1,272,128]{2,1,0:T(8,128)(2,1)S(1)}, s16[1,272,128]{2,1,0:T(8,128)(2,1)S(1)}, u32[]{:S(2)}, u32[]{:S(2)}) collective-permute-start(s16[1,272,128]{2,1,0:T(8,128)(2,1)S(1)} %get-tuple-element.53), channel_id=1, source_target_pairs={{0,12},{1,13},{2,14},{3,15},{4,0},{5,1},{6,2},{7,3},{8,4},{9,5},{1... | collective-permute-start | bytes 208904 | tf_op jit(solution)/shard_map/ppermute | solution.py:298
  68.8 6.5 %collective-permute-start.19 = (s16[1,272,128]{2,1,0:T(8,128)(2,1)S(1)}, s16[1,272,128]{2,1,0:T(8,128)(2,1)S(1)}, u32[]{:S(2)}, u32[]{:S(2)}) collective-permute-start(s16[1,272,128]{2,1,0:T(8,128)(2,1)S(1)} %get-tuple-element.54), channel_id=1, source_target_pairs={{0,4},{1,5},{2,6},{3,7},{4,8},{5,9},{6,10},{7,11},{8,12},{9,13},{1... | collective-permute-start | bytes 208904 | tf_op jit(solution)/shard_map/ppermute | solution.py:298
  68.8 4.0 %collective-permute-start.14 = (s16[1,144,128]{2,1,0:T(8,128)(2,1)S(1)}, s16[1,144,128]{2,1,0:T(8,128)(2,1)S(1)}, u32[]{:S(2)}, u32[]{:S(2)}) collective-permute-start(s16[1,144,128]{2,1,0:T(8,128)(2,1)S(1)} %get-tuple-element.49), channel_id=1, source_target_pairs={{0,16},{1,17},{2,18},{3,19},{4,20},{5,21},{6,22},{7,23},{8,24},{9,... | collective-permute-start | bytes 110600 | tf_op jit(solution)/shard_map/ppermute | solution.py:298

commit v3 on v2

v3 whole, which is shorter than its diff:
```python
import functools

import jax
import jax.numpy as jnp
from jax import lax
from jax.experimental import pallas as pl
from jax.experimental.pallas import tpu as pltpu
from jax.sharding import PartitionSpec as P

BS = 128
F = 128
H = 256
SLOTS = 40
LISTS = 8
PIECE_BLK = 3
PIECE_ROWS = PIECE_BLK * BS
HALF = PIECE_ROWS // 2
PANEL_BLK = 96
GROUP = 8
GROUPS = SLOTS // GROUP
TOP = 32766.0
MIB = 1 << 20

FIRST, SECOND = (0, 144, 2), (288, 96, 1)


def message_rows(part):
    return part[1] * part[2] + 16


SMEM = pl.BlockSpec(memory_space=pltpu.SMEM)
VMEM = pl.BlockSpec(memory_space=pltpu.VMEM)
ANY = pl.BlockSpec(memory_space=pl.ANY)


def call(kernel, name, out_shape, in_specs, out_specs, args, us, mib=24, **more):
    return pl.pallas_call(
        kernel,
        out_shape=out_shape,
        in_specs=in_specs,
        out_specs=out_specs,
        compiler_params=pltpu.CompilerParams(vmem_limit_bytes=mib * MIB),
        cost_estimate=pl.CostEstimate(flops=0, bytes_accessed=int(us * 3.0e6), transcendentals=0),
        name=name,
        **more,
    )(*args)


def groups_of(count):
    return lax.div(jnp.clip(count, 0, SLOTS) + (GROUP - 1), GROUP)


def fetch(vals_ref, vals, sems, count_ref, j, k):
    def each(action):
        @pl.loop(0, groups_of(count_ref[0, j]))
        def _(g):
            action(
                pltpu.make_async_copy(
                    vals_ref.at[pl.ds(pl.multiple_of(j * SLOTS + g * GROUP, GROUP), GROUP)],
                    vals.at[pl.ds(pl.multiple_of(k * SLOTS + g * GROUP, GROUP), GROUP)],
                    sems.at[k * GROUPS + g],
                )
            )

    return each


def add_list(panel, piece, vals, count_ref, lists_ref, j, k, wait=None):
    count = count_ref[0, j]

    @pl.loop(0, groups_of(count))
    def _(g):
        if wait is not None:
            wait(g)
        products, rows = [], []
        for u in range(GROUP):
            q = g * GROUP + u
            entry = jnp.where(q < count, lists_ref[j, q], PANEL_BLK * 4)
            rows.append(pl.ds(pl.multiple_of((entry >> 2) * BS, BS), BS))
            products.append(
                jnp.dot(
                    vals[k * SLOTS + q],
                    piece[pl.ds(pl.multiple_of((entry & 3) * BS, BS), BS), :],
                    preferred_element_type=jnp.float32,
                )
            )
        for row, product in zip(rows, products):
            panel[row, :] += product


def group_wait(vals_ref, vals, sems, j, k):
    def wait(g):
        pltpu.make_async_copy(
            vals_ref.at[pl.ds(pl.multiple_of(j * SLOTS + g * GROUP, GROUP), GROUP)],
            vals.at[pl.ds(pl.multiple_of(k * SLOTS + g * GROUP, GROUP), GROUP)],
            sems.at[k * GROUPS + g],
        ).wait()

    return wait


def piece_of(shift, flip):
    place = lax.axis_index("blk")
    x_hi = lax.rem(place, 2)
    return lax.rem(lax.div(place, 2) + shift, 4) * 2 + (1 - x_hi if flip else x_hi)


def first_products(count_ref, lists_ref, own_ref, vals_ref, panel, own, vals, sems, own_sem):
    mine = piece_of(0, False)
    own_copy = pltpu.make_async_copy(own_ref, own, own_sem)
    own_copy.start()
    fetch(vals_ref, vals, sems, count_ref, mine, 0)(lambda copy: copy.start())

    @pl.loop(0, PANEL_BLK // 4)
    def _(k):
        panel[pl.ds(pl.multiple_of(k * 4 * BS, 4 * BS), 4 * BS), :] = jnp.zeros((4 * BS, F), jnp.float32)

    own_copy.wait()
    add_list(panel, own, vals, count_ref, lists_ref, mine, 0, group_wait(vals_ref, vals, sems, mine, 0))


def more_products(pieces, ahead, count_ref, lists_ref, _, vals_ref, *refs):
    inputs = 1 + max(array for _, (array, _) in pieces)
    pairs, (panel, *outputs) = refs[:inputs], refs[inputs:]
    vals, sems = outputs[-2:]
    todo = [piece_of(*which) for which, _ in pieces]
    for k, j in enumerate(todo):
        fetch(vals_ref, vals, sems, count_ref, j, k)(lambda copy: copy.start())
    later = [
        fetch(vals_ref, outputs[0], outputs[1], count_ref, piece_of(*which), k)
        for k, which in enumerate(ahead)
    ]
    for each in later:
        each(lambda copy: copy.start())
    for k, (j, (_, (array, half))) in enumerate(zip(todo, pieces)):
        add_list(
            panel, pairs[array].at[half], vals, count_ref, lists_ref, j, k,
            group_wait(vals_ref, vals, sems, j, k),
        )
    for each in later:
        each(lambda copy: copy.wait())


def quantize(block):
    peak = jnp.maximum(jnp.max(jnp.abs(block), axis=0, keepdims=True), 1e-32)
    exponent = jnp.ceil(jnp.log2(peak) + 0.001)
    scaled = block * (jnp.exp2(-exponent) * TOP)
    return jnp.round(scaled).astype(jnp.int32).astype(jnp.int16), exponent


def write_message(out_ref, index, part, blocks):
    _, rows, count = part
    row = lax.broadcasted_iota(jnp.int32, (16, F), 0)
    tail = jnp.zeros((16, F), jnp.float32)
    for i, block in enumerate(blocks):
        whole, exponent = quantize(block)
        out_ref[index, i * rows : (i + 1) * rows, :] = whole
        tail = jnp.where(row == i, exponent, tail)
    out_ref[index, count * rows : count * rows + 16, :] = tail.astype(jnp.int32).astype(jnp.int16)


def read_message(ref, index, part):
    _, rows, count = part
    tail = ref[index, count * rows : count * rows + 16, :].astype(jnp.int32).astype(jnp.float32)
    size = jnp.exp2(tail) * (1.0 / TOP)
    blocks = []
    for i in range(count):
        whole = ref[index, i * rows : (i + 1) * rows, :].astype(jnp.int32).astype(jnp.float32)
        blocks.append(whole * size[i : i + 1, :])
    return blocks


def add(first, *others):
    for other in others:
        first = [a + b for a, b in zip(first, other)]
    return first


class Here:
    def __init__(self, panel=None):
        place = lax.axis_index("rep")
        self.core, self.x, self.z = lax.rem(place, 2), lax.div(place, 16), lax.rem(lax.div(place, 2), 8)
        self.panel = panel

    def z_of(self, shift):
        return lax.rem(self.z + shift + 8, 8)

    def partial(self, other_x, z, part, other_core=False):
        start, rows, count = part
        core = 1 - self.core if other_core else self.core
        owner = (1 - self.x if other_x else self.x) * 16 + z * 2 + core
        base = owner * PIECE_ROWS + start
        return [self.panel[pl.ds(pl.multiple_of(base + i * rows, 16), rows), :] for i in range(count)]


def for_each_z(unroll, action):
    @pl.loop(0, 8 // unroll)
    def _(k):
        for u in range(unroll):
            action(k * unroll + u)


def core_messages(part, other_x, panel, out_ref):
    here = Here(panel)
    for k, other in enumerate(other_x):
        for_each_z(
            4, lambda z: write_message(out_ref, k * 8 + z, part, here.partial(other, z, part, other_core=True))
        )


def last_products(pieces, count_ref, lists_ref, _, vals, *refs):
    *arrays, panel, out_ref = refs
    for k, (which, piece) in enumerate(zip(pieces, arrays)):
        add_list(panel, piece, vals, count_ref, lists_ref, piece_of(*which), k)
    core_messages(FIRST, (True,), panel, out_ref)


def pair_up(first_ref, second_ref, out_ref):
    out_ref[0] = first_ref[...]
    out_ref[1] = second_ref[...]


def x_messages(panel, rc_ref, out_ref):
    here = Here(panel)
    for_each_z(
        4, lambda z: write_message(out_ref, z, FIRST, add(here.partial(True, z, FIRST), read_message(rc_ref, z, FIRST)))
    )


def base_value(part, here, rc_ref, rx_ref, other, z):
    value = add(here.partial(other, z, part), read_message(rc_ref, other * 8 + z, part))
    return value if rx_ref is None else add(value, read_message(rx_ref, z, part))


def sides(part):
    return (0,) if part == FIRST else (0, 1)


def z_start(part, panel, rc_ref, rx_ref, down_ref, up_ref, two_ref, far_ref):
    here = Here(panel)
    for other in sides(part):
        for out_ref, index, shift in (
            (down_ref, 2 * other, -4), (down_ref, 2 * other + 1, -1), (up_ref, other, 2),
            (two_ref, other, -2), (far_ref, other, 3),
        ):
            write_message(out_ref, index, part, base_value(part, here, rc_ref, rx_ref, other, here.z_of(shift)))


def z_middle(part, panel, rc_ref, rx_ref, down_ref, up_ref, three_ref, one_ref):
    here = Here(panel)
    for other in sides(part):
        value = functools.partial(base_value, part, here, rc_ref, rx_ref, other)
        come = read_message(down_ref, 2 * other, part)
        write_message(three_ref, other, part, add(value(here.z_of(-3)), come))
        come = read_message(up_ref, other, part)
        write_message(one_ref, other, part, add(value(here.z_of(1)), come))


def arrivals(part, other, down_ref, *refs):
    return [read_message(down_ref, 2 * other + 1, part)] + [read_message(ref, other, part) for ref in refs]


def z_end(panel, rc_ref, *refs):
    here = Here(panel)
    *arrived, out_ref, sum_ref = refs
    value = base_value(SECOND, here, rc_ref, None, 1, here.z)
    write_message(out_ref, 0, SECOND, add(value, *arrivals(SECOND, 1, *arrived)))
    value = base_value(SECOND, here, rc_ref, None, 0, here.z)
    sum_ref[...] = add(value, *arrivals(SECOND, 0, *arrived))[0]


def layer(panel, rc_ref, rx_ref, sum_ref, rx2_ref, *refs):
    here = Here(panel)
    *arrived, weight_ref, out_ref = refs
    first = add(base_value(FIRST, here, rc_ref, rx_ref, 0, here.z), *arrivals(FIRST, 0, *arrived))
    second = add([sum_ref[...]], read_message(rx2_ref, 0, SECOND))
    weight = weight_ref[...]
    row = 0
    for block in first + second:
        high = block.astype(jnp.bfloat16)
        rest = block - high.astype(jnp.float32)
        middle = rest.astype(jnp.bfloat16)
        low = (rest - middle.astype(jnp.float32)).astype(jnp.bfloat16)
        result = jnp.dot(low, weight, preferred_element_type=jnp.float32)
        result += jnp.dot(middle, weight, preferred_element_type=jnp.float32)
        result += jnp.dot(high, weight, preferred_element_type=jnp.float32)
        out_ref[row : row + block.shape[0], :] = jnp.maximum(result, 0.0).astype(jnp.bfloat16)
        row += block.shape[0]


def messages(count, part):
    return jax.ShapeDtypeStruct((count, message_rows(part), F), jnp.int16)


def send_blk(array, dy, flip=0):
    pairs = [(y * 2 + h, ((y + dy) % 4) * 2 + (h ^ flip)) for y in range(4) for h in range(2)]
    return lax.ppermute(array, "blk", pairs)


def send_rep(array, dx, dz, dc):
    pairs = [
        (x * 16 + z * 2 + c, (x ^ dx) * 16 + ((z + dz) % 8) * 2 + (c ^ dc))
        for x in range(2) for z in range(8) for c in range(2)
    ]
    return lax.ppermute(array, "rep", pairs)


def sum_along_z(part, name, panel, rc, rx):
    count = len(sides(part))
    have = (rc,) if rx is None else (rc, rx)

    def fill(kernel):
        if rx is not None:
            return functools.partial(kernel, part)
        return lambda panel_ref, rc_ref, *refs: kernel(part, panel_ref, rc_ref, None, *refs)

    down, up, two, far = call(
        fill(z_start), name + "_start", (messages(2 * count, part),) + (messages(count, part),) * 3,
        [VMEM] * (1 + len(have)), (VMEM,) * 4, (panel, *have), 0.6,
    )
    down, up = send_rep(down, 0, -1, 0), send_rep(up, 0, 1, 0)
    two, far = send_rep(two, 0, -2, 0), send_rep(far, 0, 3, 0)
    three, one = call(
        fill(z_middle), name + "_middle", (messages(count, part),) * 2,
        [VMEM] * (3 + len(have)), (VMEM,) * 2, (panel, *have, down, up), 0.6,
    )
    return down, two, far, send_rep(three, 0, -3, 0), send_rep(one, 0, 1, 0)


def local(node_feats, block_vals, block_rows, block_cols, block_count, weight):
    slots = block_rows.reshape(LISTS, SLOTS) * 4 + block_cols.reshape(LISTS, SLOTS)
    lists = (block_count.reshape(1, LISTS), slots)
    vals = block_vals.reshape(LISTS * SLOTS, BS, BS)
    panel_type = jax.ShapeDtypeStruct(((PANEL_BLK + 1) * BS, F), jnp.float32)
    piece_buffer = pltpu.VMEM((PIECE_ROWS, F), jnp.bfloat16)

    def list_buffers(count):
        return [pltpu.VMEM((count * SLOTS, BS, BS), jnp.bfloat16), pltpu.SemaphoreType.DMA((count * GROUPS,))]

    own = node_feats
    flipped = send_blk(own, 0, 1)
    panel = call(
        first_products, "products_own", panel_type, [SMEM] * 2 + [ANY] * 2, VMEM, (*lists, own, vals), 3, 41,
        scratch_shapes=[piece_buffer, *list_buffers(1), pltpu.SemaphoreType.DMA],
    )
    panel, flipped = lax.optimization_barrier((panel, flipped))
    pair = call(
        pair_up, "pair", jax.ShapeDtypeStruct((2, PIECE_ROWS, F), jnp.bfloat16), [VMEM] * 2, VMEM, (own, flipped), 0.3
    )
    below, above = send_blk(pair, 1), send_blk(pair, -1)
    panel = call(
        functools.partial(more_products, (((0, True), (0, 1)),), ()), "products_flipped", panel_type,
        [SMEM] * 2 + [VMEM, ANY, VMEM], VMEM, (*lists, panel, vals, pair), 3, 41,
        input_output_aliases={2: 0},
        scratch_shapes=list_buffers(1),
    )
    panel, below, above = lax.optimization_barrier((panel, below, above))
    far = send_blk(below[0], 1), send_blk(above[1], -1)
    far_pieces = (2, False), (2, True)
    near_pieces = ((3, False), (0, 0)), ((3, True), (0, 1)), ((1, False), (1, 0)), ((1, True), (1, 1))
    panel, last_vals = call(
        functools.partial(more_products, near_pieces, far_pieces), "products_near",
        (panel_type, jax.ShapeDtypeStruct((2 * SLOTS, BS, BS), jnp.bfloat16)),
        [SMEM] * 2 + [VMEM, ANY] + [VMEM] * 2, (VMEM,) * 2, (*lists, panel, vals, below, above), 3, 41,
        input_output_aliases={2: 0},
        scratch_shapes=[pltpu.SemaphoreType.DMA((2 * GROUPS,)), *list_buffers(4)],
    )
    panel, to_core = call(
        functools.partial(last_products, far_pieces), "products_far", (panel_type, messages(8, FIRST)),
        [SMEM] * 2 + [VMEM] * 4, (VMEM,) * 2, (*lists, panel, last_vals, *far), 3, 40,
        input_output_aliases={2: 0},
    )

    def to_other_core(name, panel, part, other_x):
        return call(
            functools.partial(core_messages, part, other_x), name, messages(8 * len(other_x), part),
            [VMEM], VMEM, (panel,), 0.6,
        )

    rc_cross = send_rep(to_core, 0, 0, 1)
    rc_second = send_rep(to_other_core("core_second", panel, SECOND, (False, True)), 0, 0, 1)
    rc_first = send_rep(to_other_core("core_first", panel, FIRST, (False,)), 0, 0, 1)
    to_x = call(x_messages, "x_first", messages(8, FIRST), [VMEM, VMEM], VMEM, (panel, rc_cross), 0.6)
    rx_first = send_rep(to_x, 1, 0, 0)
    rc_second, rc_first = lax.optimization_barrier((rc_second, rc_first))
    second = sum_along_z(SECOND, "second", panel, rc_second, None)
    to_x, own_sum = call(
        z_end, "x_second", (messages(1, SECOND), jax.ShapeDtypeStruct((SECOND[1], F), jnp.float32)),
        [VMEM] * 7, (VMEM,) * 2, (panel, rc_second, *second), 0.6,
    )
    panel, to_x = lax.optimization_barrier((panel, to_x))
    rx_second = send_rep(to_x, 1, 0, 0)
    first = sum_along_z(FIRST, "first", panel, rc_first, rx_first)
    return call(
        layer, "layer", jax.ShapeDtypeStruct((PIECE_ROWS, H), jnp.bfloat16), [VMEM] * 11, VMEM,
        (panel, rc_first, rx_first, own_sum, rx_second, *first, weight), 1.5,
    )


def solution(mesh):
    return jax.shard_map(
        local,
        mesh=mesh,
        in_specs=(
            P(("blk", "rep"), None),
            P("blk", "rep", None, None, None, None),
            P("blk", "rep", None, None),
            P("blk", "rep", None, None),
            P("blk", "rep", None),
            P(),
        ),
        out_specs=P(("blk", "rep"), None),
        check_vma=False,
    )
```

time: 77.6 us -> 66.9 us (0.86)
  waiting for transfers between devices: 25.8 us -> 16.5 us
  Pallas kernels: 17.9 us -> 11.9 us
  starting transfers between devices: 30.7 us -> 35.6 us
    ppermute x15 -> x17, waiting for transfers between devices: 20.5 us -> 11.2 us  [send_rep(): return lax.ppermute(array, 'rep', pairs)]
    pallas_call x14, Pallas kernels: 17.9 us -> 11.9 us  [call(): pl.pallas_call(kernel, out_shape=out_shape, in_specs=in_specs, out_specs=...]
    ppermute x15 -> x17, starting transfers between devices: 22.4 us -> 27.3 us  [send_rep(): return lax.ppermute(array, 'rep', pairs)]
  transfers between devices with their start and end apart: 20 -> 22, of which waited for: 12 -> 12; matrix products, arithmetic and copies ran while one was open for 1% -> 1% of each run, Pallas kernels for 17% -> 13%
where the time goes in v3:
time: 66.9 us; the launch traced here: 66.4 us
  starting transfers between devices  35.6 us (53%)
  waiting for transfers between devices  16.5 us (25%)
  Pallas kernels  11.9 us (18%)
  local copies, waits for them, and re-layouts  1.57 us (2%)
  other arithmetic  0.71 us (1%)
    ppermute x17, starting transfers between devices, send_rep(): return lax.ppermute(array, 'rep', pairs)  27.3 us
    pallas_call x14, Pallas kernels, call(): pl.pallas_call(kernel, out_shape=out_shape, in_specs=in_specs, out_specs=...  11.9 us
    ppermute x17, waiting for transfers between devices, send_rep(): return lax.ppermute(array, 'rep', pairs)  11.2 us
    ppermute x5, starting transfers between devices, send_blk(): return lax.ppermute(array, 'blk', pairs)  8.24 us
    ppermute x5, waiting for transfers between devices, send_blk(): return lax.ppermute(array, 'blk', pairs)  5.34 us
    unnamed x6, local copies, waits for them, and re-layouts  1.55 us
  transfers between devices with their start and end apart: 22, of which 12 were waited for; matrix products, arithmetic and copies ran while one was open for 1% of the time, Pallas kernels for 13%

profile of v3, /device:TPU:2, one launch (start us, length us, event | category | flops | bytes accessed | tf_op | source)
XLA Modules:
  0.0 66.4 jit_solution(13183643508402008167)
XLA Ops:
  0.0 2.1 %collective-permute-start = (bf16[384,128]{1,0:T(8,128)(2,1)}, bf16[384,128]{1,0:T(8,128)(2,1)S(1)}, u32[]{:S(2)}, u32[]{:S(2)}) collective-permute-start(bf16[384,128]{1,0:T(8,128)(2,1)} %first_ref.1), channel_id=1, source_target_pairs={{0,32},{32,0},{64,96},{96,64},{128,160},{160,128},{192,224},{224,1... | collective-permute-start | bytes 294920 | tf_op jit(solution)/shard_map/ppermute | solution.py:297
  4.4 2.0 %products_own.1._ = f32[12416,128]{1,0:T(8,128)S(1)} custom-call(s32[1,8]{1,0:T(1,128)S(1)} %bitcast.8, s32[8,40]{1,0:T(8,128)S(1)} %add_bitcast_fusion.lists_ref, bf16[384,128]{1,0:T(8,128)(2,1)S(1)} %copy-done, bf16[320,128,128]{2,1,0:T(8,128)(2,1)} %bitcast.12), custom_call_target="tpu_custom_call" | custom-call | bytes 9000000 | tf_op jit(solution)/shard_map/products_own/pallas_call | solution.py:37
  6.4 4.0 %collective-permute-start.2 = (bf16[2,384,128]{2,1,0:T(8,128)(2,1)S(1)}, bf16[2,384,128]{2,1,0:T(8,128)(2,1)S(1)}, u32[]{:S(2)}, u32[]{:S(2)}) collective-permute-start(bf16[2,384,128]{2,1,0:T(8,128)(2,1)S(1)} %pair.1.refs_0_), channel_id=1, source_target_pairs={{0,192},{32,224},{64,0},{96,32},{128,64},{160,96},{192,128},{224,1... | collective-permute-start | bytes 589832 | tf_op jit(solution)/shard_map/ppermute | solution.py:297
  10.4 1.9 %products_flipped.1._ = f32[12416,128]{1,0:T(8,128)S(1)} custom-call(s32[1,8]{1,0:T(1,128)S(1)} %bitcast.9, s32[8,40]{1,0:T(8,128)S(1)} %add_bitcast_fusion.lists_ref, f32[12416,128]{1,0:T(8,128)S(1)} %products_own.1._, bf16[320,128,128]{2,1,0:T(8,128)(2,1)} %bitcast.13, bf16[2,384,128]{2,1,0:T(8,128)(2,1)S(1)} %pair.1.refs_0_), custom_call_target="tpu_custom_call", output_to_operand_aliasing={{}: (2, {})} | custom-call | bytes 9000000 | tf_op jit(solution)/shard_map/products_flipped/pallas_call | solution.py:37
  12.3 1.3 %collective-permute-done.2.refs_1_ = bf16[2,384,128]{2,1,0:T(8,128)(2,1)S(1)} collective-permute-done((bf16[2,384,128]{2,1,0:T(8,128)(2,1)S(1)}, bf16[2,384,128]{2,1,0:T(8,128)(2,1)S(1)}, u32[]{:S(2)}, u32[]{:S(2)}) %collective-permute-start.2) | collective-permute-done | bytes 196640 | tf_op jit(solution)/shard_map/ppermute | solution.py:297
  13.6 3.7 %collective-permute-done.1.refs_0_ = bf16[2,384,128]{2,1,0:T(8,128)(2,1)S(1)} collective-permute-done((bf16[2,384,128]{2,1,0:T(8,128)(2,1)S(1)}, bf16[2,384,128]{2,1,0:T(8,128)(2,1)S(1)}, u32[]{:S(2)}, u32[]{:S(2)}) %collective-permute-start.1) | collective-permute-done | bytes 196640 | tf_op jit(solution)/shard_map/ppermute | solution.py:297
  17.4 2.0 %collective-permute-start.3 = (bf16[384,128]{1,0:T(8,128)(2,1)S(1)}, bf16[384,128]{1,0:T(8,128)(2,1)S(1)}, u32[]{:S(2)}, u32[]{:S(2)}) collective-permute-start(bf16[384,128]{1,0:T(8,128)(2,1)S(1)} %slice_bitcast_fusion.1), channel_id=1, source_target_pairs={{0,64},{32,96},{64,128},{96,160},{128,192},{160,224},{192,0},{224,... | collective-permute-start | bytes 294920 | tf_op jit(solution)/shard_map/ppermute | solution.py:297
  19.4 3.6 %products_near.1 = (f32[12416,128]{1,0:T(8,128)S(1)}, bf16[80,128,128]{2,1,0:T(8,128)(2,1)S(1)}) custom-call(s32[1,8]{1,0:T(1,128)S(1)} %bitcast.10, s32[8,40]{1,0:T(8,128)S(1)} %add_bitcast_fusion.lists_ref, f32[12416,128]{1,0:T(8,128)S(1)} %products_flipped.1._, bf16[320,128,128]{2,1,0:T(8,128)(2,1)} %bitcast.14, ...), custom_call_target="tpu_custom_call", output_to_operand_aliasing={{0}: (2, {})} | custom-call | bytes 9000000 | tf_op jit(solution)/shard_map/products_near/pallas_call | solution.py:37
  23.3 1.6 %products_far.1 = (f32[12416,128]{1,0:T(8,128)S(1)}, s16[8,304,128]{2,1,0:T(8,128)(2,1)S(1)}) custom-call(s32[1,8]{1,0:T(1,128)S(1)} %bitcast.11, s32[8,40]{1,0:T(8,128)S(1)} %add_bitcast_fusion.lists_ref, f32[12416,128]{1,0:T(8,128)S(1)} %get-tuple-element.37._, bf16[80,128,128]{2,1,0:T(8,128)(2,1)S(1)} %get-tuple-element.38.vals, ...), custom_call_target="tpu_custom_call", output_to_operand_aliasing={{0}: (2, {})} | custom-call | bytes 9000000 | tf_op jit(solution)/shard_map/products_far/pallas_call | solution.py:37
  27.4 2.1 %collective-permute-start.14 = (s16[8,304,128]{2,1,0:T(8,128)(2,1)S(1)}, s16[8,304,128]{2,1,0:T(8,128)(2,1)S(1)}, u32[]{:S(2)}, u32[]{:S(2)}) collective-permute-start(s16[8,304,128]{2,1,0:T(8,128)(2,1)S(1)} %x_first.1), channel_id=1, source_target_pairs={{0,16},{1,17},{2,18},{3,19},{4,20},{5,21},{6,22},{7,23},{8,24},{9,... | collective-permute-start | bytes 1867784 | tf_op jit(solution)/shard_map/ppermute | solution.py:305
  29.8 6.2 %collective-permute-start.7 = (s16[4,112,128]{2,1,0:T(8,128)(2,1)S(1)}, s16[4,112,128]{2,1,0:T(8,128)(2,1)S(1)}, u32[]{:S(2)}, u32[]{:S(2)}) collective-permute-start(s16[4,112,128]{2,1,0:T(8,128)(2,1)S(1)} %get-tuple-element.41), channel_id=1, source_target_pairs={{0,14},{1,15},{2,0},{3,1},{4,2},{5,3},{6,4},{7,5},{8,6},{9,7},{10,... | collective-permute-start | bytes 344072 | tf_op jit(solution)/shard_map/ppermute | solution.py:305
  35.9 3.2 %collective-permute-start.8 = (s16[2,112,128]{2,1,0:T(8,128)(2,1)S(1)}, s16[2,112,128]{2,1,0:T(8,128)(2,1)S(1)}, u32[]{:S(2)}, u32[]{:S(2)}) collective-permute-start(s16[2,112,128]{2,1,0:T(8,128)(2,1)S(1)} %get-tuple-element.42), channel_id=1, source_target_pairs={{0,12},{1,13},{2,14},{3,15},{4,0},{5,1},{6,2},{7,3},{8,4},{9,5},{1... | collective-permute-start | bytes 172040 | tf_op jit(solution)/shard_map/ppermute | solution.py:305
  39.1 2.2 %collective-permute-done.10.refs_1_ = s16[2,112,128]{2,1,0:T(8,128)(2,1)S(1)} collective-permute-done((s16[2,112,128]{2,1,0:T(8,128)(2,1)S(1)}, s16[2,112,128]{2,1,0:T(8,128)(2,1)S(1)}, u32[]{:S(2)}, u32[]{:S(2)}) %collective-permute-start.10) | collective-permute-done | bytes 57376 | tf_op jit(solution)/shard_map/ppermute | solution.py:305
  41.4 3.1 %collective-permute-start.11 = (s16[2,112,128]{2,1,0:T(8,128)(2,1)S(1)}, s16[2,112,128]{2,1,0:T(8,128)(2,1)S(1)}, u32[]{:S(2)}, u32[]{:S(2)}) collective-permute-start(s16[2,112,128]{2,1,0:T(8,128)(2,1)S(1)} %get-tuple-element.45), channel_id=1, source_target_pairs={{0,10},{1,11},{2,12},{3,13},{4,14},{5,15},{6,0},{7,1},{8,2},{9,3},... | collective-permute-start | bytes 172040 | tf_op jit(solution)/shard_map/ppermute | solution.py:305
  44.5 1.5 %collective-permute-start.12 = (s16[2,112,128]{2,1,0:T(8,128)(2,1)S(1)}, s16[2,112,128]{2,1,0:T(8,128)(2,1)S(1)}, u32[]{:S(2)}, u32[]{:S(2)}) collective-permute-start(s16[2,112,128]{2,1,0:T(8,128)(2,1)S(1)} %get-tuple-element.46), channel_id=1, source_target_pairs={{0,2},{1,3},{2,4},{3,5},{4,6},{5,7},{6,8},{7,9},{8,10},{9,11},{10,... | collective-permute-start | bytes 172040 | tf_op jit(solution)/shard_map/ppermute | solution.py:305
  46.1 1.1 %collective-permute-done.9.refs_2_ = s16[2,112,128]{2,1,0:T(8,128)(2,1)S(1)} collective-permute-done((s16[2,112,128]{2,1,0:T(8,128)(2,1)S(1)}, s16[2,112,128]{2,1,0:T(8,128)(2,1)S(1)}, u32[]{:S(2)}, u32[]{:S(2)}) %collective-permute-start.9) | collective-permute-done | bytes 57376 | tf_op jit(solution)/shard_map/ppermute | solution.py:305
  47.2 1.6 %collective-permute-done.11.refs_3_ = s16[2,112,128]{2,1,0:T(8,128)(2,1)S(1)} collective-permute-done((s16[2,112,128]{2,1,0:T(8,128)(2,1)S(1)}, s16[2,112,128]{2,1,0:T(8,128)(2,1)S(1)}, u32[]{:S(2)}, u32[]{:S(2)}) %collective-permute-start.11) | collective-permute-done | bytes 57376 | tf_op jit(solution)/shard_map/ppermute | solution.py:305
  48.8 1.1 %collective-permute-done.12.refs_4_ = s16[2,112,128]{2,1,0:T(8,128)(2,1)S(1)} collective-permute-done((s16[2,112,128]{2,1,0:T(8,128)(2,1)S(1)}, s16[2,112,128]{2,1,0:T(8,128)(2,1)S(1)}, u32[]{:S(2)}, u32[]{:S(2)}) %collective-permute-start.12) | collective-permute-done | bytes 57376 | tf_op jit(solution)/shard_map/ppermute | solution.py:305
  50.5 2.0 %collective-permute-start.19 = (s16[1,304,128]{2,1,0:T(8,128)(2,1)S(1)}, s16[1,304,128]{2,1,0:T(8,128)(2,1)S(1)}, u32[]{:S(2)}, u32[]{:S(2)}) collective-permute-start(s16[1,304,128]{2,1,0:T(8,128)(2,1)S(1)} %get-tuple-element.56), channel_id=1, source_target_pairs={{0,2},{1,3},{2,4},{3,5},{4,6},{5,7},{6,8},{7,9},{8,10},{9,11},{10,... | collective-permute-start | bytes 233480 | tf_op jit(solution)/shard_map/ppermute | solution.py:305
  52.5 1.9 %collective-permute-start.17 = (s16[1,304,128]{2,1,0:T(8,128)(2,1)S(1)}, s16[1,304,128]{2,1,0:T(8,128)(2,1)S(1)}, u32[]{:S(2)}, u32[]{:S(2)}) collective-permute-start(s16[1,304,128]{2,1,0:T(8,128)(2,1)S(1)} %get-tuple-element.54), channel_id=1, source_target_pairs={{0,12},{1,13},{2,14},{3,15},{4,0},{5,1},{6,2},{7,3},{8,4},{9,5},{1... | collective-permute-start | bytes 233480 | tf_op jit(solution)/shard_map/ppermute | solution.py:305
  55.2 1.2 %collective-permute-done.19.up_ref = s16[1,304,128]{2,1,0:T(8,128)(2,1)S(1)} collective-permute-done((s16[1,304,128]{2,1,0:T(8,128)(2,1)S(1)}, s16[1,304,128]{2,1,0:T(8,128)(2,1)S(1)}, u32[]{:S(2)}, u32[]{:S(2)}) %collective-permute-start.19) | collective-permute-done | bytes 77856 | tf_op jit(solution)/shard_map/ppermute | solution.py:305
  57.5 2.2 %collective-permute-start.20 = (s16[1,304,128]{2,1,0:T(8,128)(2,1)S(1)}, s16[1,304,128]{2,1,0:T(8,128)(2,1)S(1)}, u32[]{:S(2)}, u32[]{:S(2)}) collective-permute-start(s16[1,304,128]{2,1,0:T(8,128)(2,1)S(1)} %get-tuple-element.57), channel_id=1, source_target_pairs={{0,10},{1,11},{2,12},{3,13},{4,14},{5,15},{6,0},{7,1},{8,2},{9,3},... | collective-permute-start | bytes 233480 | tf_op jit(solution)/shard_map/ppermute | solution.py:305
  60.6 2.7 %collective-permute-start.15 = (s16[1,112,128]{2,1,0:T(8,128)(2,1)S(1)}, s16[1,112,128]{2,1,0:T(8,128)(2,1)S(1)}, u32[]{:S(2)}, u32[]{:S(2)}) collective-permute-start(s16[1,112,128]{2,1,0:T(8,128)(2,1)S(1)} %get-tuple-element.52), channel_id=1, source_target_pairs={{0,16},{1,17},{2,18},{3,19},{4,20},{5,21},{6,22},{7,23},{8,24},{9,... | collective-permute-start | bytes 86024 | tf_op jit(solution)/shard_map/ppermute | solution.py:305
  63.2 1.8 %collective-permute-done.15.rx2_ref = s16[1,112,128]{2,1,0:T(8,128)(2,1)S(1)} collective-permute-done((s16[1,112,128]{2,1,0:T(8,128)(2,1)S(1)}, s16[1,112,128]{2,1,0:T(8,128)(2,1)S(1)}, u32[]{:S(2)}, u32[]{:S(2)}) %collective-permute-start.15) | collective-permute-done | bytes 28704 | tf_op jit(solution)/shard_map/ppermute | solution.py:305
  (43 shorter events, 10.1 us)
Async XLA Ops:
  0.0 6.4 %collective-permute-start = (bf16[384,128]{1,0:T(8,128)(2,1)}, bf16[384,128]{1,0:T(8,128)(2,1)S(1)}, u32[]{:S(2)}, u32[]{:S(2)}) collective-permute-start(bf16[384,128]{1,0:T(8,128)(2,1)} %first_ref.1), channel_id=1, source_target_pairs={{0,32},{32,0},{64,96},{96,64},{128,160},{160,128},{192,224},{224,1... | collective-permute-start | bytes 294920 | tf_op jit(solution)/shard_map/ppermute | solution.py:297
  2.8 0.9 %copy-start = (bf16[384,128]{1,0:T(8,128)(2,1)S(1)}, bf16[384,128]{1,0:T(8,128)(2,1)}, u32[]{:S(2)}) copy-start(bf16[384,128]{1,0:T(8,128)(2,1)} %first_ref.1) | copy-start | bytes 294916
  6.4 7.2 %collective-permute-start.2 = (bf16[2,384,128]{2,1,0:T(8,128)(2,1)S(1)}, bf16[2,384,128]{2,1,0:T(8,128)(2,1)S(1)}, u32[]{:S(2)}, u32[]{:S(2)}) collective-permute-start(bf16[2,384,128]{2,1,0:T(8,128)(2,1)S(1)} %pair.1.refs_0_), channel_id=1, source_target_pairs={{0,192},{32,224},{64,0},{96,32},{128,64},{160,96},{192,128},{224,1... | collective-permute-start | bytes 589832 | tf_op jit(solution)/shard_map/ppermute | solution.py:297
  10.4 6.9 %collective-permute-start.1 = (bf16[2,384,128]{2,1,0:T(8,128)(2,1)S(1)}, bf16[2,384,128]{2,1,0:T(8,128)(2,1)S(1)}, u32[]{:S(2)}, u32[]{:S(2)}) collective-permute-start(bf16[2,384,128]{2,1,0:T(8,128)(2,1)S(1)} %pair.1.refs_0_), channel_id=1, source_target_pairs={{0,64},{32,96},{64,128},{96,160},{128,192},{160,224},{192,0},{224,... | collective-permute-start | bytes 589832 | tf_op jit(solution)/shard_map/ppermute | solution.py:297
  17.3 5.7 %collective-permute-start.4 = (bf16[384,128]{1,0:T(8,128)(2,1)S(1)}, bf16[384,128]{1,0:T(8,128)(2,1)S(1)}, u32[]{:S(2)}, u32[]{:S(2)}) collective-permute-start(bf16[384,128]{1,0:T(8,128)(2,1)S(1)} %slice_bitcast_fusion), channel_id=1, source_target_pairs={{0,192},{32,224},{64,0},{96,32},{128,64},{160,96},{192,128},{224,1... | collective-permute-start | bytes 294920 | tf_op jit(solution)/shard_map/ppermute | solution.py:297
  17.4 5.9 %collective-permute-start.3 = (bf16[384,128]{1,0:T(8,128)(2,1)S(1)}, bf16[384,128]{1,0:T(8,128)(2,1)S(1)}, u32[]{:S(2)}, u32[]{:S(2)}) collective-permute-start(bf16[384,128]{1,0:T(8,128)(2,1)S(1)} %slice_bitcast_fusion.1), channel_id=1, source_target_pairs={{0,64},{32,96},{64,128},{96,160},{128,192},{160,224},{192,0},{224,... | collective-permute-start | bytes 294920 | tf_op jit(solution)/shard_map/ppermute | solution.py:297
  24.9 2.1 %collective-permute-start.13 = (s16[8,304,128]{2,1,0:T(8,128)(2,1)S(1)}, s16[8,304,128]{2,1,0:T(8,128)(2,1)S(1)}, u32[]{:S(2)}, u32[]{:S(2)}) collective-permute-start(s16[8,304,128]{2,1,0:T(8,128)(2,1)S(1)} %get-tuple-element.50), channel_id=1, source_target_pairs={{0,1},{1,0},{2,3},{3,2},{4,5},{5,4},{6,7},{7,6},{8,9},{9,8},{10,11... | collective-permute-start | bytes 1867784 | tf_op jit(solution)/shard_map/ppermute | solution.py:305
  25.3 4.3 %collective-permute-start.6 = (s16[8,304,128]{2,1,0:T(8,128)(2,1)S(1)}, s16[8,304,128]{2,1,0:T(8,128)(2,1)S(1)}, u32[]{:S(2)}, u32[]{:S(2)}) collective-permute-start(s16[8,304,128]{2,1,0:T(8,128)(2,1)S(1)} %core_first.1), channel_id=1, source_target_pairs={{0,1},{1,0},{2,3},{3,2},{4,5},{5,4},{6,7},{7,6},{8,9},{9,8},{10,11... | collective-permute-start | bytes 1867784 | tf_op jit(solution)/shard_map/ppermute | solution.py:305
  26.1 3.5 %collective-permute-start.5 = (s16[16,112,128]{2,1,0:T(8,128)(2,1)S(1)}, s16[16,112,128]{2,1,0:T(8,128)(2,1)S(1)}, u32[]{:S(2)}, u32[]{:S(2)}) collective-permute-start(s16[16,112,128]{2,1,0:T(8,128)(2,1)S(1)} %core_second.1), channel_id=1, source_target_pairs={{0,1},{1,0},{2,3},{3,2},{4,5},{5,4},{6,7},{7,6},{8,9},{9,8},{10,11... | collective-permute-start | bytes 1376264 | tf_op jit(solution)/shard_map/ppermute | solution.py:305
  27.4 22.6 %collective-permute-start.14 = (s16[8,304,128]{2,1,0:T(8,128)(2,1)S(1)}, s16[8,304,128]{2,1,0:T(8,128)(2,1)S(1)}, u32[]{:S(2)}, u32[]{:S(2)}) collective-permute-start(s16[8,304,128]{2,1,0:T(8,128)(2,1)S(1)} %x_first.1), channel_id=1, source_target_pairs={{0,16},{1,17},{2,18},{3,19},{4,20},{5,21},{6,22},{7,23},{8,24},{9,... | collective-permute-start | bytes 1867784 | tf_op jit(solution)/shard_map/ppermute | solution.py:305
  29.8 11.6 %collective-permute-start.7 = (s16[4,112,128]{2,1,0:T(8,128)(2,1)S(1)}, s16[4,112,128]{2,1,0:T(8,128)(2,1)S(1)}, u32[]{:S(2)}, u32[]{:S(2)}) collective-permute-start(s16[4,112,128]{2,1,0:T(8,128)(2,1)S(1)} %get-tuple-element.41), channel_id=1, source_target_pairs={{0,14},{1,15},{2,0},{3,1},{4,2},{5,3},{6,4},{7,5},{8,6},{9,7},{10,... | collective-permute-start | bytes 344072 | tf_op jit(solution)/shard_map/ppermute | solution.py:305
  35.9 5.4 %collective-permute-start.10 = (s16[2,112,128]{2,1,0:T(8,128)(2,1)S(1)}, s16[2,112,128]{2,1,0:T(8,128)(2,1)S(1)}, u32[]{:S(2)}, u32[]{:S(2)}) collective-permute-start(s16[2,112,128]{2,1,0:T(8,128)(2,1)S(1)} %get-tuple-element.44), channel_id=1, source_target_pairs={{0,2},{1,3},{2,4},{3,5},{4,6},{5,7},{6,8},{7,9},{8,10},{9,11},{10,... | collective-permute-start | bytes 172040 | tf_op jit(solution)/shard_map/ppermute | solution.py:305
  35.9 10.1 %collective-permute-start.8 = (s16[2,112,128]{2,1,0:T(8,128)(2,1)S(1)}, s16[2,112,128]{2,1,0:T(8,128)(2,1)S(1)}, u32[]{:S(2)}, u32[]{:S(2)}) collective-permute-start(s16[2,112,128]{2,1,0:T(8,128)(2,1)S(1)} %get-tuple-element.42), channel_id=1, source_target_pairs={{0,12},{1,13},{2,14},{3,15},{4,0},{5,1},{6,2},{7,3},{8,4},{9,5},{1... | collective-permute-start | bytes 172040 | tf_op jit(solution)/shard_map/ppermute | solution.py:305
  39.1 8.1 %collective-permute-start.9 = (s16[2,112,128]{2,1,0:T(8,128)(2,1)S(1)}, s16[2,112,128]{2,1,0:T(8,128)(2,1)S(1)}, u32[]{:S(2)}, u32[]{:S(2)}) collective-permute-start(s16[2,112,128]{2,1,0:T(8,128)(2,1)S(1)} %get-tuple-element.43), channel_id=1, source_target_pairs={{0,6},{1,7},{2,8},{3,9},{4,10},{5,11},{6,12},{7,13},{8,14},{9,15},... | collective-permute-start | bytes 172040 | tf_op jit(solution)/shard_map/ppermute | solution.py:305
  41.4 7.4 %collective-permute-start.11 = (s16[2,112,128]{2,1,0:T(8,128)(2,1)S(1)}, s16[2,112,128]{2,1,0:T(8,128)(2,1)S(1)}, u32[]{:S(2)}, u32[]{:S(2)}) collective-permute-start(s16[2,112,128]{2,1,0:T(8,128)(2,1)S(1)} %get-tuple-element.45), channel_id=1, source_target_pairs={{0,10},{1,11},{2,12},{3,13},{4,14},{5,15},{6,0},{7,1},{8,2},{9,3},... | collective-permute-start | bytes 172040 | tf_op jit(solution)/shard_map/ppermute | solution.py:305
  44.5 5.4 %collective-permute-start.12 = (s16[2,112,128]{2,1,0:T(8,128)(2,1)S(1)}, s16[2,112,128]{2,1,0:T(8,128)(2,1)S(1)}, u32[]{:S(2)}, u32[]{:S(2)}) collective-permute-start(s16[2,112,128]{2,1,0:T(8,128)(2,1)S(1)} %get-tuple-element.46), channel_id=1, source_target_pairs={{0,2},{1,3},{2,4},{3,5},{4,6},{5,7},{6,8},{7,9},{8,10},{9,11},{10,... | collective-permute-start | bytes 172040 | tf_op jit(solution)/shard_map/ppermute | solution.py:305
  50.0 15.3 %copy-start.1 = (bf16[128,256]{1,0:T(8,128)(2,1)S(1)}, bf16[128,256]{1,0:T(8,128)(2,1)}, u32[]{:S(2)}) copy-start(bf16[128,256]{1,0:T(8,128)(2,1)} %refs_5_.1) | copy-start | bytes 196612
  50.4 6.9 %collective-permute-start.16 = (s16[2,304,128]{2,1,0:T(8,128)(2,1)S(1)}, s16[2,304,128]{2,1,0:T(8,128)(2,1)S(1)}, u32[]{:S(2)}, u32[]{:S(2)}) collective-permute-start(s16[2,304,128]{2,1,0:T(8,128)(2,1)S(1)} %get-tuple-element.53), channel_id=1, source_target_pairs={{0,14},{1,15},{2,0},{3,1},{4,2},{5,3},{6,4},{7,5},{8,6},{9,7},{10,... | collective-permute-start | bytes 466952 | tf_op jit(solution)/shard_map/ppermute | solution.py:305
  50.5 5.9 %collective-permute-start.19 = (s16[1,304,128]{2,1,0:T(8,128)(2,1)S(1)}, s16[1,304,128]{2,1,0:T(8,128)(2,1)S(1)}, u32[]{:S(2)}, u32[]{:S(2)}) collective-permute-start(s16[1,304,128]{2,1,0:T(8,128)(2,1)S(1)} %get-tuple-element.56), channel_id=1, source_target_pairs={{0,2},{1,3},{2,4},{3,5},{4,6},{5,7},{6,8},{7,9},{8,10},{9,11},{10,... | collective-permute-start | bytes 233480 | tf_op jit(solution)/shard_map/ppermute | solution.py:305
  52.5 12.6 %collective-permute-start.17 = (s16[1,304,128]{2,1,0:T(8,128)(2,1)S(1)}, s16[1,304,128]{2,1,0:T(8,128)(2,1)S(1)}, u32[]{:S(2)}, u32[]{:S(2)}) collective-permute-start(s16[1,304,128]{2,1,0:T(8,128)(2,1)S(1)} %get-tuple-element.54), channel_id=1, source_target_pairs={{0,12},{1,13},{2,14},{3,15},{4,0},{5,1},{6,2},{7,3},{8,4},{9,5},{1... | collective-permute-start | bytes 233480 | tf_op jit(solution)/shard_map/ppermute | solution.py:305
  54.4 10.7 %collective-permute-start.18 = (s16[1,304,128]{2,1,0:T(8,128)(2,1)S(1)}, s16[1,304,128]{2,1,0:T(8,128)(2,1)S(1)}, u32[]{:S(2)}, u32[]{:S(2)}) collective-permute-start(s16[1,304,128]{2,1,0:T(8,128)(2,1)S(1)} %get-tuple-element.55), channel_id=1, source_target_pairs={{0,6},{1,7},{2,8},{3,9},{4,10},{5,11},{6,12},{7,13},{8,14},{9,15},... | collective-permute-start | bytes 233480 | tf_op jit(solution)/shard_map/ppermute | solution.py:305
  57.5 7.6 %collective-permute-start.20 = (s16[1,304,128]{2,1,0:T(8,128)(2,1)S(1)}, s16[1,304,128]{2,1,0:T(8,128)(2,1)S(1)}, u32[]{:S(2)}, u32[]{:S(2)}) collective-permute-start(s16[1,304,128]{2,1,0:T(8,128)(2,1)S(1)} %get-tuple-element.57), channel_id=1, source_target_pairs={{0,10},{1,11},{2,12},{3,13},{4,14},{5,15},{6,0},{7,1},{8,2},{9,3},... | collective-permute-start | bytes 233480 | tf_op jit(solution)/shard_map/ppermute | solution.py:305
  59.7 5.6 %collective-permute-start.21 = (s16[1,304,128]{2,1,0:T(8,128)(2,1)S(1)}, s16[1,304,128]{2,1,0:T(8,128)(2,1)S(1)}, u32[]{:S(2)}, u32[]{:S(2)}) collective-permute-start(s16[1,304,128]{2,1,0:T(8,128)(2,1)S(1)} %get-tuple-element.58), channel_id=1, source_target_pairs={{0,2},{1,3},{2,4},{3,5},{4,6},{5,7},{6,8},{7,9},{8,10},{9,11},{10,... | collective-permute-start | bytes 233480 | tf_op jit(solution)/shard_map/ppermute | solution.py:305
  60.6 4.5 %collective-permute-start.15 = (s16[1,112,128]{2,1,0:T(8,128)(2,1)S(1)}, s16[1,112,128]{2,1,0:T(8,128)(2,1)S(1)}, u32[]{:S(2)}, u32[]{:S(2)}) collective-permute-start(s16[1,112,128]{2,1,0:T(8,128)(2,1)S(1)} %get-tuple-element.52), channel_id=1, source_target_pairs={{0,16},{1,17},{2,18},{3,19},{4,20},{5,21},{6,22},{7,23},{8,24},{9,... | collective-permute-start | bytes 86024 | tf_op jit(solution)/shard_map/ppermute | solution.py:305
  (1 other events, 0.7 us)

commit v4 on v3

v4 whole, which is shorter than its diff:
```python
import functools

import jax
import jax.numpy as jnp
from jax import lax
from jax.experimental import pallas as pl
from jax.experimental.pallas import tpu as pltpu
from jax.sharding import PartitionSpec as P

BS = 128
F = 128
H = 256
SLOTS = 40
LISTS = 8
PIECE_BLK = 3
PIECE_ROWS = PIECE_BLK * BS
HALF = PIECE_ROWS // 2
PANEL_BLK = 96
GROUP = 8
GROUPS = SLOTS // GROUP
TOP = 32766.0
MIB = 1 << 20

FIRST, SECOND = (0, 144, 2), (288, 96, 1)


SMEM = pl.BlockSpec(memory_space=pltpu.SMEM)
VMEM = pl.BlockSpec(memory_space=pltpu.VMEM)
ANY = pl.BlockSpec(memory_space=pl.ANY)


def call(kernel, name, out_shape, in_specs, out_specs, args, us, mib=24, **more):
    return pl.pallas_call(
        kernel,
        out_shape=out_shape,
        in_specs=in_specs,
        out_specs=out_specs,
        compiler_params=pltpu.CompilerParams(vmem_limit_bytes=mib * MIB),
        cost_estimate=pl.CostEstimate(flops=0, bytes_accessed=int(us * 3.0e6), transcendentals=0),
        name=name,
        **more,
    )(*args)


def groups_of(count):
    return lax.div(jnp.clip(count, 0, SLOTS) + (GROUP - 1), GROUP)


def fetch(vals_ref, vals, sems, lists_ref, j, k):
    def each(action):
        @pl.loop(0, groups_of(lists_ref[j, 0] & 63))
        def _(g):
            action(
                pltpu.make_async_copy(
                    vals_ref.at[pl.ds(pl.multiple_of(j * SLOTS + g * GROUP, GROUP), GROUP)],
                    vals.at[pl.ds(pl.multiple_of(k * SLOTS + g * GROUP, GROUP), GROUP)],
                    sems.at[k * GROUPS + g],
                )
            )

    return each


def add_list(panel, piece, vals, lists_ref, j, k, wait=None):
    count = lists_ref[j, 0] & 63

    @pl.loop(0, groups_of(count))
    def _(g):
        if wait is not None:
            wait(g)
        products, rows = [], []
        for u in range(GROUP):
            q = g * GROUP + u
            entry = jnp.where(q < count, lists_ref[j, q] >> 6, PANEL_BLK * 4)
            rows.append(pl.ds(pl.multiple_of((entry >> 2) * BS, BS), BS))
            products.append(
                jnp.dot(
                    vals[k * SLOTS + q],
                    piece[pl.ds(pl.multiple_of((entry & 3) * BS, BS), BS), :],
                    preferred_element_type=jnp.float32,
                )
            )
        for row, product in zip(rows, products):
            panel[row, :] += product


def group_wait(vals_ref, vals, sems, j, k):
    def wait(g):
        pltpu.make_async_copy(
            vals_ref.at[pl.ds(pl.multiple_of(j * SLOTS + g * GROUP, GROUP), GROUP)],
            vals.at[pl.ds(pl.multiple_of(k * SLOTS + g * GROUP, GROUP), GROUP)],
            sems.at[k * GROUPS + g],
        ).wait()

    return wait


def piece_of(shift, flip):
    place = lax.axis_index("blk")
    x_hi = lax.rem(place, 2)
    return lax.rem(lax.div(place, 2) + shift, 4) * 2 + (1 - x_hi if flip else x_hi)


def hold(own_ref, out_ref):
    out_ref[...] = own_ref[...]


def first_products(which, ahead, lists_ref, own_ref, flipped_ref, vals_ref, panel, next_vals, *scratch):
    vals, sems, next_sems = scratch
    todo = [piece_of(*piece) for piece in which]
    for k, j in enumerate(todo):
        fetch(vals_ref, vals, sems, lists_ref, j, k)(lambda copy: copy.start())
    later = [
        fetch(vals_ref, next_vals, next_sems, lists_ref, piece_of(*piece), k) for k, piece in enumerate(ahead)
    ]
    for each in later:
        each(lambda copy: copy.start())

    @pl.loop(0, PANEL_BLK // 4)
    def _(k):
        panel[pl.ds(pl.multiple_of(k * 4 * BS, 4 * BS), 4 * BS), :] = jnp.zeros((4 * BS, F), jnp.float32)

    for k, (j, piece) in enumerate(zip(todo, (own_ref, flipped_ref))):
        add_list(panel, piece, vals, lists_ref, j, k, group_wait(vals_ref, vals, sems, j, k))
    for each in later:
        each(lambda copy: copy.wait())


def more_products(pieces, first, lists_ref, _, vals, *refs):
    *arrays, panel = refs
    for k, (piece, array) in enumerate(zip(pieces, arrays)):
        add_list(panel, array, vals, lists_ref, piece_of(*piece), first + k)


def quantize(block):
    peak = jnp.maximum(jnp.max(jnp.abs(block), axis=0, keepdims=True), 1e-32)
    exponent = jnp.ceil(jnp.log2(peak) + 0.001)
    scaled = block * (jnp.exp2(-exponent) * TOP)
    return jnp.round(scaled).astype(jnp.int32).astype(jnp.int16), exponent


def messages(count, part):
    return jax.ShapeDtypeStruct((count * part[1] * part[2] + 16, F), jnp.int16)


def write_messages(out_ref, part, values):
    _, rows, count = part
    row = lax.broadcasted_iota(jnp.int32, (16, F), 0)
    tail = jnp.zeros((16, F), jnp.float32)
    k = 0
    for value in values:
        for block in value():
            whole, exponent = quantize(block)
            out_ref[k * rows : (k + 1) * rows, :] = whole
            tail = jnp.where(row == k, exponent, tail)
            k += 1
    out_ref[k * rows : k * rows + 16, :] = tail.astype(jnp.int32).astype(jnp.int16)


def read_message(ref, index, part):
    _, rows, count = part
    last = ref.shape[0] - 16
    row = lax.broadcasted_iota(jnp.int32, (16, F), 0)
    tail = ref[last : last + 16, :].astype(jnp.int32).astype(jnp.float32)
    blocks = []
    for i in range(count):
        k = index * count + i
        if isinstance(k, int):
            exponent = tail[k : k + 1, :]
            whole = ref[k * rows : (k + 1) * rows, :]
        else:
            exponent = jnp.sum(jnp.where(row == k, tail, 0.0), axis=0, keepdims=True)
            whole = ref[pl.ds(pl.multiple_of(k * rows, 16), rows), :]
        blocks.append(whole.astype(jnp.int32).astype(jnp.float32) * (jnp.exp2(exponent) * (1.0 / TOP)))
    return blocks


def add(first, *others):
    for other in others:
        first = [a + b for a, b in zip(first, other)]
    return first


class Here:
    def __init__(self, panel=None):
        place = lax.axis_index("rep")
        self.core, self.x, self.z = lax.rem(place, 2), lax.div(place, 16), lax.rem(lax.div(place, 2), 8)
        self.panel = panel

    def z_of(self, shift):
        return lax.rem(self.z + shift + 8, 8)

    def partial(self, other_x, z, part, other_core=False):
        start, rows, count = part
        core = 1 - self.core if other_core else self.core
        owner = (1 - self.x if other_x else self.x) * 16 + z * 2 + core
        base = owner * PIECE_ROWS + start
        return [self.panel[pl.ds(pl.multiple_of(base + i * rows, 16), rows), :] for i in range(count)]


def core_messages(part, other_x, panel, out_ref):
    here = Here(panel)
    write_messages(
        out_ref, part,
        [
            functools.partial(here.partial, other, z, part, other_core=True)
            for other in other_x for z in range(8)
        ],
    )


def last_products(pieces, first, *refs):
    more_products(pieces, first, *refs[:-1])
    core_messages(FIRST, (True,), *refs[-2:])


def x_messages(panel, rc_ref, out_ref):
    here = Here(panel)
    write_messages(
        out_ref, FIRST,
        [lambda z=z: add(here.partial(True, z, FIRST), read_message(rc_ref, z, FIRST)) for z in range(8)],
    )


def base_value(part, here, rc_ref, rx_ref, other, z):
    value = add(here.partial(other, z, part), read_message(rc_ref, other * 8 + z, part))
    return value if rx_ref is None else add(value, read_message(rx_ref, z, part))


def sides(part):
    return (0,) if part == FIRST else (0, 1)


def z_start(part, panel, rc_ref, rx_ref, down_ref, up_ref, two_ref, far_ref):
    here = Here(panel)
    for out_ref, shifts in ((down_ref, (-4, -1)), (up_ref, (2,)), (two_ref, (-2,)), (far_ref, (3,))):
        write_messages(
            out_ref, part,
            [
                functools.partial(base_value, part, here, rc_ref, rx_ref, other, here.z_of(shift))
                for other in sides(part) for shift in shifts
            ],
        )


def z_middle(part, panel, rc_ref, rx_ref, down_ref, up_ref, three_ref, one_ref):
    here = Here(panel)

    def through(come_ref, stride, shift):
        return [
            lambda other=other: add(
                base_value(part, here, rc_ref, rx_ref, other, here.z_of(shift)),
                read_message(come_ref, stride * other, part),
            )
            for other in sides(part)
        ]

    write_messages(three_ref, part, through(down_ref, 2, -3))
    write_messages(one_ref, part, through(up_ref, 1, 1))


def arrivals(part, other, down_ref, *refs):
    return [read_message(down_ref, 2 * other + 1, part)] + [read_message(ref, other, part) for ref in refs]


def z_end(panel, rc_ref, *refs):
    here = Here(panel)
    *arrived, out_ref, sum_ref = refs
    value = base_value(SECOND, here, rc_ref, None, 1, here.z)
    write_messages(out_ref, SECOND, [lambda: add(value, *arrivals(SECOND, 1, *arrived))])
    mine = base_value(SECOND, here, rc_ref, None, 0, here.z)
    sum_ref[...] = add(mine, *arrivals(SECOND, 0, *arrived))[0]


def layer(panel, rc_ref, rx_ref, sum_ref, rx2_ref, *refs):
    here = Here(panel)
    *arrived, weight_ref, out_ref = refs
    first = add(base_value(FIRST, here, rc_ref, rx_ref, 0, here.z), *arrivals(FIRST, 0, *arrived))
    second = add([sum_ref[...]], read_message(rx2_ref, 0, SECOND))
    weight = weight_ref[...]
    row = 0
    for block in first + second:
        high = block.astype(jnp.bfloat16)
        rest = block - high.astype(jnp.float32)
        middle = rest.astype(jnp.bfloat16)
        low = (rest - middle.astype(jnp.float32)).astype(jnp.bfloat16)
        result = jnp.dot(low, weight, preferred_element_type=jnp.float32)
        result += jnp.dot(middle, weight, preferred_element_type=jnp.float32)
        result += jnp.dot(high, weight, preferred_element_type=jnp.float32)
        out_ref[row : row + block.shape[0], :] = jnp.maximum(result, 0.0).astype(jnp.bfloat16)
        row += block.shape[0]


def send_blk(array, dy, flip=0):
    pairs = [(y * 2 + h, ((y + dy) % 4) * 2 + (h ^ flip)) for y in range(4) for h in range(2)]
    return lax.ppermute(array, "blk", pairs)


def send_rep(array, dx, dz, dc):
    pairs = [
        (x * 16 + z * 2 + c, (x ^ dx) * 16 + ((z + dz) % 8) * 2 + (c ^ dc))
        for x in range(2) for z in range(8) for c in range(2)
    ]
    return lax.ppermute(array, "rep", pairs)


def sum_along_z(part, name, panel, rc, rx):
    count = len(sides(part))
    have = (rc,) if rx is None else (rc, rx)

    def fill(kernel):
        if rx is not None:
            return functools.partial(kernel, part)
        return lambda panel_ref, rc_ref, *refs: kernel(part, panel_ref, rc_ref, None, *refs)

    down, up, two, far = call(
        fill(z_start), name + "_start", (messages(2 * count, part),) + (messages(count, part),) * 3,
        [VMEM] * (1 + len(have)), (VMEM,) * 4, (panel, *have), 0.6,
    )
    down, up = send_rep(down, 0, -1, 0), send_rep(up, 0, 1, 0)
    two, far = send_rep(two, 0, -2, 0), send_rep(far, 0, 3, 0)
    three, one = call(
        fill(z_middle), name + "_middle", (messages(count, part),) * 2,
        [VMEM] * (3 + len(have)), (VMEM,) * 2, (panel, *have, down, up), 0.6,
    )
    return down, two, far, send_rep(three, 0, -3, 0), send_rep(one, 0, 1, 0)


def local(node_feats, block_vals, block_rows, block_cols, block_count, weight):
    vals = block_vals.reshape(LISTS * SLOTS, BS, BS)
    panel_type = jax.ShapeDtypeStruct(((PANEL_BLK + 1) * BS, F), jnp.float32)
    here, near, far = ((0, False), (0, True)), ((3, False), (1, False), (3, True), (1, True)), ((2, False), (2, True))
    own = node_feats
    flipped, below, above = send_blk(own, 0, 1), send_blk(own, 1), send_blk(own, -1)
    own = call(hold, "own_piece", jax.ShapeDtypeStruct((PIECE_ROWS, F), jnp.bfloat16), [VMEM], VMEM, (own,), 1)
    slots = block_rows.reshape(LISTS, SLOTS) * 4 + block_cols.reshape(LISTS, SLOTS)
    lists = slots * 64 + block_count.reshape(LISTS, 1)
    flipped, own, lists = lax.optimization_barrier((flipped, own, lists))
    below_flipped, above_flipped = send_blk(flipped, 1), send_blk(flipped, -1)
    later = len(near) + len(far)
    panel, next_vals = call(
        functools.partial(first_products, here, near + far), "products_here",
        (panel_type, jax.ShapeDtypeStruct((later * SLOTS, BS, BS), jnp.bfloat16)),
        [SMEM, VMEM, VMEM, ANY], (VMEM,) * 2, (lists, own, flipped, vals), 4, 40,
        scratch_shapes=[
            pltpu.VMEM((2 * SLOTS, BS, BS), jnp.bfloat16),
            pltpu.SemaphoreType.DMA((2 * GROUPS,)),
            pltpu.SemaphoreType.DMA((later * GROUPS,)),
        ],
    )
    panel, below, above, below_flipped, above_flipped = lax.optimization_barrier(
        (panel, below, above, below_flipped, above_flipped)
    )
    far_own, far_flipped = send_blk(below, 1), send_blk(above_flipped, -1)
    panel = call(
        functools.partial(more_products, near, 0), "products_near", panel_type,
        [SMEM] + [VMEM] * 6, VMEM,
        (lists, panel, next_vals, below, above, below_flipped, above_flipped), 3, 24,
        input_output_aliases={1: 0},
    )
    panel, to_core = call(
        functools.partial(last_products, far, len(near)), "products_far", (panel_type, messages(8, FIRST)),
        [SMEM] + [VMEM] * 4, (VMEM,) * 2, (lists, panel, next_vals, far_own, far_flipped), 3, 24,
        input_output_aliases={1: 0},
    )

    def to_other_core(name, panel, part, other_x):
        return call(
            functools.partial(core_messages, part, other_x), name, messages(8 * len(other_x), part),
            [VMEM], VMEM, (panel,), 0.6,
        )

    rc_cross = send_rep(to_core, 0, 0, 1)
    rc_second = send_rep(to_other_core("core_second", panel, SECOND, (False, True)), 0, 0, 1)
    rc_first = send_rep(to_other_core("core_first", panel, FIRST, (False,)), 0, 0, 1)
    rc_cross, rc_second = lax.optimization_barrier((rc_cross, rc_second))
    to_x = call(x_messages, "x_first", messages(8, FIRST), [VMEM, VMEM], VMEM, (panel, rc_cross), 0.6)
    rx_first = send_rep(to_x, 1, 0, 0)
    rc_second, rc_first = lax.optimization_barrier((rc_second, rc_first))
    second = sum_along_z(SECOND, "second", panel, rc_second, None)
    to_x, own_sum = call(
        z_end, "x_second", (messages(1, SECOND), jax.ShapeDtypeStruct((SECOND[1], F), jnp.float32)),
        [VMEM] * 7, (VMEM,) * 2, (panel, rc_second, *second), 0.6,
    )
    panel, to_x = lax.optimization_barrier((panel, to_x))
    rx_second = send_rep(to_x, 1, 0, 0)
    first = sum_along_z(FIRST, "first", panel, rc_first, rx_first)
    return call(
        layer, "layer", jax.ShapeDtypeStruct((PIECE_ROWS, H), jnp.bfloat16), [VMEM] * 11, VMEM,
        (panel, rc_first, rx_first, own_sum, rx_second, *first, weight), 1.5,
    )


def solution(mesh):
    return jax.shard_map(
        local,
        mesh=mesh,
        in_specs=(
            P(("blk", "rep"), None),
            P("blk", "rep", None, None, None, None),
            P("blk", "rep", None, None),
            P("blk", "rep", None, None),
            P("blk", "rep", None),
            P(),
        ),
        out_specs=P(("blk", "rep"), None),
        check_vma=False,
    )
```

time: 66.9 us -> 65.1 us (0.973)
  Pallas kernels: 11.9 us -> 10.6 us
  local copies, waits for them, and re-layouts: 1.57 us -> 0.9 us
    ppermute x5 -> x7, starting transfers between devices: 8.24 us -> 11.7 us  [send_blk(): return lax.ppermute(array, 'blk', pairs)]
    ppermute x17, starting transfers between devices: 27.3 us -> 24 us  [send_rep(): return lax.ppermute(array, 'rep', pairs)]
    ppermute x5 -> x7, waiting for transfers between devices: 5.34 us -> 3.16 us  [send_blk(): return lax.ppermute(array, 'blk', pairs)]
    ppermute x17, waiting for transfers between devices: 11.2 us -> 13.3 us  [send_rep(): return lax.ppermute(array, 'rep', pairs)]
    pallas_call x14 -> x13, Pallas kernels: 11.9 us -> 10.6 us  [call(): pl.pallas_call(kernel, out_shape=out_shape, in_specs=in_specs, out_specs=...]
    unnamed x6 -> x4, local copies, waits for them, and re-layouts: 1.55 us -> 0.9 us
  transfers between devices with their start and end apart: 22 -> 24, of which waited for: 12 -> 12; matrix products, arithmetic and copies ran while one was open for 1% -> 1% of each run, Pallas kernels for 13% -> 10%
where the time goes in v4:
time: 65.1 us; the launch traced here: 64.5 us
  starting transfers between devices  35.7 us (55%)
  waiting for transfers between devices  16.5 us (25%)
  Pallas kernels  10.6 us (16%)
  local copies, waits for them, and re-layouts  0.9 us (1%)
  other arithmetic  0.77 us (1%)
    ppermute x17, starting transfers between devices, send_rep(): return lax.ppermute(array, 'rep', pairs)  24 us
    ppermute x17, waiting for transfers between devices, send_rep(): return lax.ppermute(array, 'rep', pairs)  13.3 us
    ppermute x7, starting transfers between devices, send_blk(): return lax.ppermute(array, 'blk', pairs)  11.7 us
    pallas_call x13, Pallas kernels, call(): pl.pallas_call(kernel, out_shape=out_shape, in_specs=in_specs, out_specs=...  10.6 us
    ppermute x7, waiting for transfers between devices, send_blk(): return lax.ppermute(array, 'blk', pairs)  3.16 us
  transfers between devices with their start and end apart: 24, of which 12 were waited for; matrix products, arithmetic and copies ran while one was open for 1% of the time, Pallas kernels for 10%

profile of v4, /device:TPU:2, one launch (start us, length us, event | category | flops | bytes accessed | tf_op | source)
XLA Modules:
  0.0 64.5 jit_solution(11895622428467667310)
XLA Ops:
  0.0 2.1 %collective-permute-start = (bf16[384,128]{1,0:T(8,128)(2,1)}, bf16[384,128]{1,0:T(8,128)(2,1)S(1)}, u32[]{:S(2)}, u32[]{:S(2)}) collective-permute-start(bf16[384,128]{1,0:T(8,128)(2,1)} %own_ref.1), channel_id=1, source_target_pairs={{0,32},{32,0},{64,96},{96,64},{128,160},{160,128},{192,224},{224,1... | collective-permute-start | bytes 294920 | tf_op jit(solution)/shard_map/ppermute | solution.py:296
  2.1 3.0 %collective-permute-start.2 = (bf16[384,128]{1,0:T(8,128)(2,1)}, bf16[384,128]{1,0:T(8,128)(2,1)S(1)}, u32[]{:S(2)}, u32[]{:S(2)}) collective-permute-start(bf16[384,128]{1,0:T(8,128)(2,1)} %own_ref.1), channel_id=1, source_target_pairs={{0,192},{32,224},{64,0},{96,32},{128,64},{160,96},{192,128},{224,1... | collective-permute-start | bytes 294920 | tf_op jit(solution)/shard_map/ppermute | solution.py:296
  6.8 3.3 %collective-permute-start.4 = (bf16[384,128]{1,0:T(8,128)(2,1)S(1)}, bf16[384,128]{1,0:T(8,128)(2,1)S(1)}, u32[]{:S(2)}, u32[]{:S(2)}) collective-permute-start(bf16[384,128]{1,0:T(8,128)(2,1)S(1)} %collective-permute-done.flipped_ref), channel_id=1, source_target_pairs={{0,192},{32,224},{64,0},{96,32},{128,64},{160,96},{192,128},{224,1... | collective-permute-start | bytes 294920 | tf_op jit(solution)/shard_map/ppermute | solution.py:296
  10.1 3.2 %products_here.1 = (f32[12416,128]{1,0:T(8,128)S(1)}, bf16[240,128,128]{2,1,0:T(8,128)(2,1)S(1)}) custom-call(s32[8,40]{1,0:T(8,128)S(1)} %bitcast_add_fusion.lists_ref.refs_0_, bf16[384,128]{1,0:T(8,128)(2,1)S(1)} %own_piece.1.own_ref, bf16[384,128]{1,0:T(8,128)(2,1)S(1)} %collective-permute-done.flipped_ref, bf16[320,128,128]{2,1,0:T(8,128)(2,1)} %bitcast.4), custom_call_target="tpu_custom_call" | custom-call | bytes 12000000 | tf_op jit(solution)/shard_map/products_here/pallas_call | solution.py:33
  13.3 2.6 %collective-permute-done.3.refs_2_ = bf16[384,128]{1,0:T(8,128)(2,1)S(1)} collective-permute-done((bf16[384,128]{1,0:T(8,128)(2,1)S(1)}, bf16[384,128]{1,0:T(8,128)(2,1)S(1)}, u32[]{:S(2)}, u32[]{:S(2)}) %collective-permute-start.3) | collective-permute-done | bytes 98336 | tf_op jit(solution)/shard_map/ppermute | solution.py:296
  16.0 3.2 %collective-permute-start.6 = (bf16[384,128]{1,0:T(8,128)(2,1)S(1)}, bf16[384,128]{1,0:T(8,128)(2,1)S(1)}, u32[]{:S(2)}, u32[]{:S(2)}) collective-permute-start(bf16[384,128]{1,0:T(8,128)(2,1)S(1)} %collective-permute-done.4.refs_3_), channel_id=1, source_target_pairs={{0,192},{32,224},{64,0},{96,32},{128,64},{160,96},{192,128},{224,1... | collective-permute-start | bytes 294920 | tf_op jit(solution)/shard_map/ppermute | solution.py:296
  19.2 2.1 %products_near.1.refs_1_ = f32[12416,128]{1,0:T(8,128)S(1)} custom-call(s32[8,40]{1,0:T(8,128)S(1)} %bitcast_add_fusion.lists_ref.refs_0_, f32[12416,128]{1,0:T(8,128)S(1)} %get-tuple-element.41._, bf16[240,128,128]{2,1,0:T(8,128)(2,1)S(1)} %get-tuple-element.42.vals.refs_2_, ...), custom_call_target="tpu_custom_call", output_to_operand_aliasing={{}: (1, {})} | custom-call | bytes 9000000 | tf_op jit(solution)/shard_map/products_near/pallas_call | solution.py:33
  21.8 2.5 %products_far.1 = (f32[12416,128]{1,0:T(8,128)S(1)}, s16[2320,128]{1,0:T(8,128)(2,1)S(1)}) custom-call(s32[8,40]{1,0:T(8,128)S(1)} %bitcast_add_fusion.lists_ref.refs_0_, f32[12416,128]{1,0:T(8,128)S(1)} %products_near.1.refs_1_, bf16[240,128,128]{2,1,0:T(8,128)(2,1)S(1)} %get-tuple-element.42.vals.refs_2_, ...), custom_call_target="tpu_custom_call", output_to_operand_aliasing={{0}: (1, {})} | custom-call | bytes 9000000 | tf_op jit(solution)/shard_map/products_far/pallas_call | solution.py:33
  25.5 1.5 %collective-permute-done.8.rc_ref = s16[1552,128]{1,0:T(8,128)(2,1)S(1)} collective-permute-done((s16[1552,128]{1,0:T(8,128)(2,1)S(1)}, s16[1552,128]{1,0:T(8,128)(2,1)S(1)}, u32[]{:S(2)}, u32[]{:S(2)}) %collective-permute-start.8) | collective-permute-done | bytes 397344 | tf_op jit(solution)/shard_map/ppermute | solution.py:304
  27.3 1.7 %collective-permute-start.16 = (s16[2320,128]{1,0:T(8,128)(2,1)S(1)}, s16[2320,128]{1,0:T(8,128)(2,1)S(1)}, u32[]{:S(2)}, u32[]{:S(2)}) collective-permute-start(s16[2320,128]{1,0:T(8,128)(2,1)S(1)} %x_first.1), channel_id=1, source_target_pairs={{0,16},{1,17},{2,18},{3,19},{4,20},{5,21},{6,22},{7,23},{8,24},{9,... | collective-permute-start | bytes 1781768 | tf_op jit(solution)/shard_map/ppermute | solution.py:304
  29.2 4.6 %collective-permute-start.10 = (s16[400,128]{1,0:T(8,128)(2,1)S(1)}, s16[400,128]{1,0:T(8,128)(2,1)S(1)}, u32[]{:S(2)}, u32[]{:S(2)}) collective-permute-start(s16[400,128]{1,0:T(8,128)(2,1)S(1)} %get-tuple-element.51), channel_id=1, source_target_pairs={{0,14},{1,15},{2,0},{3,1},{4,2},{5,3},{6,4},{7,5},{8,6},{9,7},{10,... | collective-permute-start | bytes 307208 | tf_op jit(solution)/shard_map/ppermute | solution.py:304
  33.8 2.7 %collective-permute-start.11 = (s16[208,128]{1,0:T(8,128)(2,1)S(1)}, s16[208,128]{1,0:T(8,128)(2,1)S(1)}, u32[]{:S(2)}, u32[]{:S(2)}) collective-permute-start(s16[208,128]{1,0:T(8,128)(2,1)S(1)} %get-tuple-element.52), channel_id=1, source_target_pairs={{0,12},{1,13},{2,14},{3,15},{4,0},{5,1},{6,2},{7,3},{8,4},{9,5},{1... | collective-permute-start | bytes 159752 | tf_op jit(solution)/shard_map/ppermute | solution.py:304
  37.0 2.2 %collective-permute-done.13.refs_1_ = s16[208,128]{1,0:T(8,128)(2,1)S(1)} collective-permute-done((s16[208,128]{1,0:T(8,128)(2,1)S(1)}, s16[208,128]{1,0:T(8,128)(2,1)S(1)}, u32[]{:S(2)}, u32[]{:S(2)}) %collective-permute-start.13) | collective-permute-done | bytes 53280 | tf_op jit(solution)/shard_map/ppermute | solution.py:304
  39.3 2.5 %collective-permute-start.14 = (s16[208,128]{1,0:T(8,128)(2,1)S(1)}, s16[208,128]{1,0:T(8,128)(2,1)S(1)}, u32[]{:S(2)}, u32[]{:S(2)}) collective-permute-start(s16[208,128]{1,0:T(8,128)(2,1)S(1)} %get-tuple-element.55), channel_id=1, source_target_pairs={{0,10},{1,11},{2,12},{3,13},{4,14},{5,15},{6,0},{7,1},{8,2},{9,3},... | collective-permute-start | bytes 159752 | tf_op jit(solution)/shard_map/ppermute | solution.py:304
  41.7 2.0 %collective-permute-start.15 = (s16[208,128]{1,0:T(8,128)(2,1)S(1)}, s16[208,128]{1,0:T(8,128)(2,1)S(1)}, u32[]{:S(2)}, u32[]{:S(2)}) collective-permute-start(s16[208,128]{1,0:T(8,128)(2,1)S(1)} %get-tuple-element.56), channel_id=1, source_target_pairs={{0,2},{1,3},{2,4},{3,5},{4,6},{5,7},{6,8},{7,9},{8,10},{9,11},{10,... | collective-permute-start | bytes 159752 | tf_op jit(solution)/shard_map/ppermute | solution.py:304
  43.9 1.7 %collective-permute-done.14.refs_3_ = s16[208,128]{1,0:T(8,128)(2,1)S(1)} collective-permute-done((s16[208,128]{1,0:T(8,128)(2,1)S(1)}, s16[208,128]{1,0:T(8,128)(2,1)S(1)}, u32[]{:S(2)}, u32[]{:S(2)}) %collective-permute-start.14) | collective-permute-done | bytes 53280 | tf_op jit(solution)/shard_map/ppermute | solution.py:304
  45.6 1.5 %collective-permute-done.15.refs_4_ = s16[208,128]{1,0:T(8,128)(2,1)S(1)} collective-permute-done((s16[208,128]{1,0:T(8,128)(2,1)S(1)}, s16[208,128]{1,0:T(8,128)(2,1)S(1)}, u32[]{:S(2)}, u32[]{:S(2)}) %collective-permute-start.15) | collective-permute-done | bytes 53280 | tf_op jit(solution)/shard_map/ppermute | solution.py:304
  48.5 1.3 %collective-permute-start.21 = (s16[304,128]{1,0:T(8,128)(2,1)S(1)}, s16[304,128]{1,0:T(8,128)(2,1)S(1)}, u32[]{:S(2)}, u32[]{:S(2)}) collective-permute-start(s16[304,128]{1,0:T(8,128)(2,1)S(1)} %get-tuple-element.66), channel_id=1, source_target_pairs={{0,2},{1,3},{2,4},{3,5},{4,6},{5,7},{6,8},{7,9},{8,10},{9,11},{10,... | collective-permute-start | bytes 233480 | tf_op jit(solution)/shard_map/ppermute | solution.py:304
  49.7 2.6 %collective-permute-start.19 = (s16[304,128]{1,0:T(8,128)(2,1)S(1)}, s16[304,128]{1,0:T(8,128)(2,1)S(1)}, u32[]{:S(2)}, u32[]{:S(2)}) collective-permute-start(s16[304,128]{1,0:T(8,128)(2,1)S(1)} %get-tuple-element.64), channel_id=1, source_target_pairs={{0,12},{1,13},{2,14},{3,15},{4,0},{5,1},{6,2},{7,3},{8,4},{9,5},{1... | collective-permute-start | bytes 233480 | tf_op jit(solution)/shard_map/ppermute | solution.py:304
  53.0 1.8 %collective-permute-done.21.up_ref = s16[304,128]{1,0:T(8,128)(2,1)S(1)} collective-permute-done((s16[304,128]{1,0:T(8,128)(2,1)S(1)}, s16[304,128]{1,0:T(8,128)(2,1)S(1)}, u32[]{:S(2)}, u32[]{:S(2)}) %collective-permute-start.21) | collective-permute-done | bytes 77856 | tf_op jit(solution)/shard_map/ppermute | solution.py:304
  55.5 2.1 %collective-permute-start.22 = (s16[304,128]{1,0:T(8,128)(2,1)S(1)}, s16[304,128]{1,0:T(8,128)(2,1)S(1)}, u32[]{:S(2)}, u32[]{:S(2)}) collective-permute-start(s16[304,128]{1,0:T(8,128)(2,1)S(1)} %get-tuple-element.67), channel_id=1, source_target_pairs={{0,10},{1,11},{2,12},{3,13},{4,14},{5,15},{6,0},{7,1},{8,2},{9,3},... | collective-permute-start | bytes 233480 | tf_op jit(solution)/shard_map/ppermute | solution.py:304
  58.5 1.0 %collective-permute-start.17 = (s16[112,128]{1,0:T(8,128)(2,1)S(1)}, s16[112,128]{1,0:T(8,128)(2,1)S(1)}, u32[]{:S(2)}, u32[]{:S(2)}) collective-permute-start(s16[112,128]{1,0:T(8,128)(2,1)S(1)} %get-tuple-element.62), channel_id=1, source_target_pairs={{0,16},{1,17},{2,18},{3,19},{4,20},{5,21},{6,22},{7,23},{8,24},{9,... | collective-permute-start | bytes 86024 | tf_op jit(solution)/shard_map/ppermute | solution.py:304
  59.5 2.9 %collective-permute-done.17.rx2_ref = s16[112,128]{1,0:T(8,128)(2,1)S(1)} collective-permute-done((s16[112,128]{1,0:T(8,128)(2,1)S(1)}, s16[112,128]{1,0:T(8,128)(2,1)S(1)}, u32[]{:S(2)}, u32[]{:S(2)}) %collective-permute-start.17) | collective-permute-done | bytes 28704 | tf_op jit(solution)/shard_map/ppermute | solution.py:304
  63.4 1.1 %layer.1 = bf16[384,256]{1,0:T(8,128)(2,1)} custom-call(f32[12416,128]{1,0:T(8,128)S(1)} %get-tuple-element.58.panel.panel_ref, s16[2320,128]{1,0:T(8,128)(2,1)S(1)} %collective-permute-done.9.rc_ref, s16[2320,128]{1,0:T(8,128)(2,1)S(1)} %collective-permute-done.16.rx_ref, f32[96,128]{1,0:T(8,128)S(1)} %get-tuple-element.61.sum_ref, ...), custom_call_target="tpu_custom_call" | custom-call | bytes 4500000 | tf_op jit(solution)/shard_map/layer/pallas_call | solution.py:33
  (42 shorter events, 9.3 us)
Async XLA Ops:
  0.0 6.8 %collective-permute-start = (bf16[384,128]{1,0:T(8,128)(2,1)}, bf16[384,128]{1,0:T(8,128)(2,1)S(1)}, u32[]{:S(2)}, u32[]{:S(2)}) collective-permute-start(bf16[384,128]{1,0:T(8,128)(2,1)} %own_ref.1), channel_id=1, source_target_pairs={{0,32},{32,0},{64,96},{96,64},{128,160},{160,128},{192,224},{224,1... | collective-permute-start | bytes 294920 | tf_op jit(solution)/shard_map/ppermute | solution.py:296
  2.1 11.2 %collective-permute-start.2 = (bf16[384,128]{1,0:T(8,128)(2,1)}, bf16[384,128]{1,0:T(8,128)(2,1)S(1)}, u32[]{:S(2)}, u32[]{:S(2)}) collective-permute-start(bf16[384,128]{1,0:T(8,128)(2,1)} %own_ref.1), channel_id=1, source_target_pairs={{0,192},{32,224},{64,0},{96,32},{128,64},{160,96},{192,128},{224,1... | collective-permute-start | bytes 294920 | tf_op jit(solution)/shard_map/ppermute | solution.py:296
  5.1 8.2 %collective-permute-start.1 = (bf16[384,128]{1,0:T(8,128)(2,1)}, bf16[384,128]{1,0:T(8,128)(2,1)S(1)}, u32[]{:S(2)}, u32[]{:S(2)}) collective-permute-start(bf16[384,128]{1,0:T(8,128)(2,1)} %own_ref.1), channel_id=1, source_target_pairs={{0,64},{32,96},{64,128},{96,160},{128,192},{160,224},{192,0},{224,... | collective-permute-start | bytes 294920 | tf_op jit(solution)/shard_map/ppermute | solution.py:296
  6.8 6.5 %collective-permute-start.4 = (bf16[384,128]{1,0:T(8,128)(2,1)S(1)}, bf16[384,128]{1,0:T(8,128)(2,1)S(1)}, u32[]{:S(2)}, u32[]{:S(2)}) collective-permute-start(bf16[384,128]{1,0:T(8,128)(2,1)S(1)} %collective-permute-done.flipped_ref), channel_id=1, source_target_pairs={{0,192},{32,224},{64,0},{96,32},{128,64},{160,96},{192,128},{224,1... | collective-permute-start | bytes 294920 | tf_op jit(solution)/shard_map/ppermute | solution.py:296
  10.1 5.8 %collective-permute-start.3 = (bf16[384,128]{1,0:T(8,128)(2,1)S(1)}, bf16[384,128]{1,0:T(8,128)(2,1)S(1)}, u32[]{:S(2)}, u32[]{:S(2)}) collective-permute-start(bf16[384,128]{1,0:T(8,128)(2,1)S(1)} %collective-permute-done.flipped_ref), channel_id=1, source_target_pairs={{0,64},{32,96},{64,128},{96,160},{128,192},{160,224},{192,0},{224,... | collective-permute-start | bytes 294920 | tf_op jit(solution)/shard_map/ppermute | solution.py:296
  16.0 5.8 %collective-permute-start.5 = (bf16[384,128]{1,0:T(8,128)(2,1)S(1)}, bf16[384,128]{1,0:T(8,128)(2,1)S(1)}, u32[]{:S(2)}, u32[]{:S(2)}) collective-permute-start(bf16[384,128]{1,0:T(8,128)(2,1)S(1)} %collective-permute-done.1.refs_0_), channel_id=1, source_target_pairs={{0,64},{32,96},{64,128},{96,160},{128,192},{160,224},{192,0},{224,... | collective-permute-start | bytes 294920 | tf_op jit(solution)/shard_map/ppermute | solution.py:296
  16.0 5.8 %collective-permute-start.6 = (bf16[384,128]{1,0:T(8,128)(2,1)S(1)}, bf16[384,128]{1,0:T(8,128)(2,1)S(1)}, u32[]{:S(2)}, u32[]{:S(2)}) collective-permute-start(bf16[384,128]{1,0:T(8,128)(2,1)S(1)} %collective-permute-done.4.refs_3_), channel_id=1, source_target_pairs={{0,192},{32,224},{64,0},{96,32},{128,64},{160,96},{192,128},{224,1... | collective-permute-start | bytes 294920 | tf_op jit(solution)/shard_map/ppermute | solution.py:296
  24.3 2.7 %collective-permute-start.7 = (s16[2320,128]{1,0:T(8,128)(2,1)S(1)}, s16[2320,128]{1,0:T(8,128)(2,1)S(1)}, u32[]{:S(2)}, u32[]{:S(2)}) collective-permute-start(s16[2320,128]{1,0:T(8,128)(2,1)S(1)} %get-tuple-element.48), channel_id=1, source_target_pairs={{0,1},{1,0},{2,3},{3,2},{4,5},{5,4},{6,7},{7,6},{8,9},{9,8},{10,11... | collective-permute-start | bytes 1781768 | tf_op jit(solution)/shard_map/ppermute | solution.py:304
  24.6 2.4 %collective-permute-start.8 = (s16[1552,128]{1,0:T(8,128)(2,1)S(1)}, s16[1552,128]{1,0:T(8,128)(2,1)S(1)}, u32[]{:S(2)}, u32[]{:S(2)}) collective-permute-start(s16[1552,128]{1,0:T(8,128)(2,1)S(1)} %core_second.1), channel_id=1, source_target_pairs={{0,1},{1,0},{2,3},{3,2},{4,5},{5,4},{6,7},{7,6},{8,9},{9,8},{10,11... | collective-permute-start | bytes 1191944 | tf_op jit(solution)/shard_map/ppermute | solution.py:304
  25.3 3.7 %collective-permute-start.9 = (s16[2320,128]{1,0:T(8,128)(2,1)S(1)}, s16[2320,128]{1,0:T(8,128)(2,1)S(1)}, u32[]{:S(2)}, u32[]{:S(2)}) collective-permute-start(s16[2320,128]{1,0:T(8,128)(2,1)S(1)} %core_first.1), channel_id=1, source_target_pairs={{0,1},{1,0},{2,3},{3,2},{4,5},{5,4},{6,7},{7,6},{8,9},{9,8},{10,11... | collective-permute-start | bytes 1781768 | tf_op jit(solution)/shard_map/ppermute | solution.py:304
  27.3 19.9 %collective-permute-start.16 = (s16[2320,128]{1,0:T(8,128)(2,1)S(1)}, s16[2320,128]{1,0:T(8,128)(2,1)S(1)}, u32[]{:S(2)}, u32[]{:S(2)}) collective-permute-start(s16[2320,128]{1,0:T(8,128)(2,1)S(1)} %x_first.1), channel_id=1, source_target_pairs={{0,16},{1,17},{2,18},{3,19},{4,20},{5,21},{6,22},{7,23},{8,24},{9,... | collective-permute-start | bytes 1781768 | tf_op jit(solution)/shard_map/ppermute | solution.py:304
  29.2 9.9 %collective-permute-start.10 = (s16[400,128]{1,0:T(8,128)(2,1)S(1)}, s16[400,128]{1,0:T(8,128)(2,1)S(1)}, u32[]{:S(2)}, u32[]{:S(2)}) collective-permute-start(s16[400,128]{1,0:T(8,128)(2,1)S(1)} %get-tuple-element.51), channel_id=1, source_target_pairs={{0,14},{1,15},{2,0},{3,1},{4,2},{5,3},{6,4},{7,5},{8,6},{9,7},{10,... | collective-permute-start | bytes 307208 | tf_op jit(solution)/shard_map/ppermute | solution.py:304
  33.8 5.3 %collective-permute-start.13 = (s16[208,128]{1,0:T(8,128)(2,1)S(1)}, s16[208,128]{1,0:T(8,128)(2,1)S(1)}, u32[]{:S(2)}, u32[]{:S(2)}) collective-permute-start(s16[208,128]{1,0:T(8,128)(2,1)S(1)} %get-tuple-element.54), channel_id=1, source_target_pairs={{0,2},{1,3},{2,4},{3,5},{4,6},{5,7},{6,8},{7,9},{8,10},{9,11},{10,... | collective-permute-start | bytes 159752 | tf_op jit(solution)/shard_map/ppermute | solution.py:304
  33.8 9.9 %collective-permute-start.11 = (s16[208,128]{1,0:T(8,128)(2,1)S(1)}, s16[208,128]{1,0:T(8,128)(2,1)S(1)}, u32[]{:S(2)}, u32[]{:S(2)}) collective-permute-start(s16[208,128]{1,0:T(8,128)(2,1)S(1)} %get-tuple-element.52), channel_id=1, source_target_pairs={{0,12},{1,13},{2,14},{3,15},{4,0},{5,1},{6,2},{7,3},{8,4},{9,5},{1... | collective-permute-start | bytes 159752 | tf_op jit(solution)/shard_map/ppermute | solution.py:304
  36.5 7.4 %collective-permute-start.12 = (s16[208,128]{1,0:T(8,128)(2,1)S(1)}, s16[208,128]{1,0:T(8,128)(2,1)S(1)}, u32[]{:S(2)}, u32[]{:S(2)}) collective-permute-start(s16[208,128]{1,0:T(8,128)(2,1)S(1)} %get-tuple-element.53), channel_id=1, source_target_pairs={{0,6},{1,7},{2,8},{3,9},{4,10},{5,11},{6,12},{7,13},{8,14},{9,15},... | collective-permute-start | bytes 159752 | tf_op jit(solution)/shard_map/ppermute | solution.py:304
  39.3 6.3 %collective-permute-start.14 = (s16[208,128]{1,0:T(8,128)(2,1)S(1)}, s16[208,128]{1,0:T(8,128)(2,1)S(1)}, u32[]{:S(2)}, u32[]{:S(2)}) collective-permute-start(s16[208,128]{1,0:T(8,128)(2,1)S(1)} %get-tuple-element.55), channel_id=1, source_target_pairs={{0,10},{1,11},{2,12},{3,13},{4,14},{5,15},{6,0},{7,1},{8,2},{9,3},... | collective-permute-start | bytes 159752 | tf_op jit(solution)/shard_map/ppermute | solution.py:304
  41.7 5.3 %collective-permute-start.15 = (s16[208,128]{1,0:T(8,128)(2,1)S(1)}, s16[208,128]{1,0:T(8,128)(2,1)S(1)}, u32[]{:S(2)}, u32[]{:S(2)}) collective-permute-start(s16[208,128]{1,0:T(8,128)(2,1)S(1)} %get-tuple-element.56), channel_id=1, source_target_pairs={{0,2},{1,3},{2,4},{3,5},{4,6},{5,7},{6,8},{7,9},{8,10},{9,11},{10,... | collective-permute-start | bytes 159752 | tf_op jit(solution)/shard_map/ppermute | solution.py:304
  47.6 7.7 %collective-permute-start.18 = (s16[592,128]{1,0:T(8,128)(2,1)S(1)}, s16[592,128]{1,0:T(8,128)(2,1)S(1)}, u32[]{:S(2)}, u32[]{:S(2)}) collective-permute-start(s16[592,128]{1,0:T(8,128)(2,1)S(1)} %get-tuple-element.63), channel_id=1, source_target_pairs={{0,14},{1,15},{2,0},{3,1},{4,2},{5,3},{6,4},{7,5},{8,6},{9,7},{10,... | collective-permute-start | bytes 454664 | tf_op jit(solution)/shard_map/ppermute | solution.py:304
  48.5 6.3 %collective-permute-start.21 = (s16[304,128]{1,0:T(8,128)(2,1)S(1)}, s16[304,128]{1,0:T(8,128)(2,1)S(1)}, u32[]{:S(2)}, u32[]{:S(2)}) collective-permute-start(s16[304,128]{1,0:T(8,128)(2,1)S(1)} %get-tuple-element.66), channel_id=1, source_target_pairs={{0,2},{1,3},{2,4},{3,5},{4,6},{5,7},{6,8},{7,9},{8,10},{9,11},{10,... | collective-permute-start | bytes 233480 | tf_op jit(solution)/shard_map/ppermute | solution.py:304
  49.7 12.7 %collective-permute-start.19 = (s16[304,128]{1,0:T(8,128)(2,1)S(1)}, s16[304,128]{1,0:T(8,128)(2,1)S(1)}, u32[]{:S(2)}, u32[]{:S(2)}) collective-permute-start(s16[304,128]{1,0:T(8,128)(2,1)S(1)} %get-tuple-element.64), channel_id=1, source_target_pairs={{0,12},{1,13},{2,14},{3,15},{4,0},{5,1},{6,2},{7,3},{8,4},{9,5},{1... | collective-permute-start | bytes 233480 | tf_op jit(solution)/shard_map/ppermute | solution.py:304
  52.3 10.1 %collective-permute-start.20 = (s16[304,128]{1,0:T(8,128)(2,1)S(1)}, s16[304,128]{1,0:T(8,128)(2,1)S(1)}, u32[]{:S(2)}, u32[]{:S(2)}) collective-permute-start(s16[304,128]{1,0:T(8,128)(2,1)S(1)} %get-tuple-element.65), channel_id=1, source_target_pairs={{0,6},{1,7},{2,8},{3,9},{4,10},{5,11},{6,12},{7,13},{8,14},{9,15},... | collective-permute-start | bytes 233480 | tf_op jit(solution)/shard_map/ppermute | solution.py:304
  55.5 7.0 %collective-permute-start.22 = (s16[304,128]{1,0:T(8,128)(2,1)S(1)}, s16[304,128]{1,0:T(8,128)(2,1)S(1)}, u32[]{:S(2)}, u32[]{:S(2)}) collective-permute-start(s16[304,128]{1,0:T(8,128)(2,1)S(1)} %get-tuple-element.67), channel_id=1, source_target_pairs={{0,10},{1,11},{2,12},{3,13},{4,14},{5,15},{6,0},{7,1},{8,2},{9,3},... | collective-permute-start | bytes 233480 | tf_op jit(solution)/shard_map/ppermute | solution.py:304
  57.6 5.8 %collective-permute-start.23 = (s16[304,128]{1,0:T(8,128)(2,1)S(1)}, s16[304,128]{1,0:T(8,128)(2,1)S(1)}, u32[]{:S(2)}, u32[]{:S(2)}) collective-permute-start(s16[304,128]{1,0:T(8,128)(2,1)S(1)} %get-tuple-element.68), channel_id=1, source_target_pairs={{0,2},{1,3},{2,4},{3,5},{4,6},{5,7},{6,8},{7,9},{8,10},{9,11},{10,... | collective-permute-start | bytes 233480 | tf_op jit(solution)/shard_map/ppermute | solution.py:304
  58.5 3.9 %collective-permute-start.17 = (s16[112,128]{1,0:T(8,128)(2,1)S(1)}, s16[112,128]{1,0:T(8,128)(2,1)S(1)}, u32[]{:S(2)}, u32[]{:S(2)}) collective-permute-start(s16[112,128]{1,0:T(8,128)(2,1)S(1)} %get-tuple-element.62), channel_id=1, source_target_pairs={{0,16},{1,17},{2,18},{3,19},{4,20},{5,21},{6,22},{7,23},{8,24},{9,... | collective-permute-start | bytes 86024 | tf_op jit(solution)/shard_map/ppermute | solution.py:304
  (2 other events, 17.1 us)

commit v5 on v4

--- a/solution.py
+++ b/solution.py
@@ -214,6 +214,16 @@
     core_messages(FIRST, (True,), *refs[-2:])
 
 
+def rest_to_core(panel, out_ref):
+    core_messages(SECOND, (False, True), panel, core_part(out_ref, SECOND))
+    core_messages(FIRST, (False,), panel, core_part(out_ref, FIRST))
+
+
+def core_part(ref, part):
+    second_rows, first_rows = messages(16, SECOND).shape[0], messages(8, FIRST).shape[0]
+    return ref.at[pl.ds(0, second_rows)] if part == SECOND else ref.at[pl.ds(second_rows, first_rows)]
+
+
 def x_messages(panel, rc_ref, out_ref):
     here = Here(panel)
     write_messages(
@@ -223,7 +233,7 @@
 
 
 def base_value(part, here, rc_ref, rx_ref, other, z):
-    value = add(here.partial(other, z, part), read_message(rc_ref, other * 8 + z, part))
+    value = add(here.partial(other, z, part), read_message(core_part(rc_ref, part), other * 8 + z, part))
     return value if rx_ref is None else add(value, read_message(rx_ref, z, part))
 
 
@@ -329,14 +339,14 @@
 def local(node_feats, block_vals, block_rows, block_cols, block_count, weight):
     vals = block_vals.reshape(LISTS * SLOTS, BS, BS)
     panel_type = jax.ShapeDtypeStruct(((PANEL_BLK + 1) * BS, F), jnp.float32)
-    here, near, far = ((0, False), (0, True)), ((3, False), (1, False), (3, True), (1, True)), ((2, False), (2, True))
+    here, near, far = ((0, False), (0, True)), ((3, False), (1, False), (3, True), (1, True), (2, False)), ((2, True),)
     own = node_feats
     flipped, below, above = send_blk(own, 0, 1), send_blk(own, 1), send_blk(own, -1)
     own = call(hold, "own_piece", jax.ShapeDtypeStruct((PIECE_ROWS, F), jnp.bfloat16), [VMEM], VMEM, (own,), 1)
     slots = block_rows.reshape(LISTS, SLOTS) * 4 + block_cols.reshape(LISTS, SLOTS)
     lists = slots * 64 + block_count.reshape(LISTS, 1)
     flipped, own, lists = lax.optimization_barrier((flipped, own, lists))
-    below_flipped, above_flipped = send_blk(flipped, 1), send_blk(flipped, -1)
+    below_flipped, above_flipped, far_own = send_blk(flipped, 1), send_blk(flipped, -1), send_blk(below, 1)
     later = len(near) + len(far)
     panel, next_vals = call(
         functools.partial(first_products, here, near + far), "products_here",
@@ -348,46 +358,42 @@
             pltpu.SemaphoreType.DMA((later * GROUPS,)),
         ],
     )
-    panel, below, above, below_flipped, above_flipped = lax.optimization_barrier(
-        (panel, below, above, below_flipped, above_flipped)
-    )
-    far_own, far_flipped = send_blk(below, 1), send_blk(above_flipped, -1)
+    panel, above, below_flipped, above_flipped, far_own = lax.optimization_barrier(
+        (panel, above, below_flipped, above_flipped, far_own)
+    )
+    far_flipped = send_blk(above_flipped, -1)
     panel = call(
         functools.partial(more_products, near, 0), "products_near", panel_type,
-        [SMEM] + [VMEM] * 6, VMEM,
-        (lists, panel, next_vals, below, above, below_flipped, above_flipped), 3, 24,
+        [SMEM] + [VMEM] * 7, VMEM,
+        (lists, panel, next_vals, below, above, below_flipped, above_flipped, far_own), 3, 24,
         input_output_aliases={1: 0},
     )
     panel, to_core = call(
         functools.partial(last_products, far, len(near)), "products_far", (panel_type, messages(8, FIRST)),
-        [SMEM] + [VMEM] * 4, (VMEM,) * 2, (lists, panel, next_vals, far_own, far_flipped), 3, 24,
+        [SMEM] + [VMEM] * 3, (VMEM,) * 2, (lists, panel, next_vals, far_flipped), 3, 24,
         input_output_aliases={1: 0},
     )
 
-    def to_other_core(name, panel, part, other_x):
-        return call(
-            functools.partial(core_messages, part, other_x), name, messages(8 * len(other_x), part),
-            [VMEM], VMEM, (panel,), 0.6,
-        )
-
     rc_cross = send_rep(to_core, 0, 0, 1)
-    rc_second = send_rep(to_other_core("core_second", panel, SECOND, (False, True)), 0, 0, 1)
-    rc_first = send_rep(to_other_core("core_first", panel, FIRST, (False,)), 0, 0, 1)
-    rc_cross, rc_second = lax.optimization_barrier((rc_cross, rc_second))
+    second_rows, first_rows = messages(16, SECOND).shape[0], messages(8, FIRST).shape[0]
+    to_core = call(
+        rest_to_core, "core_rest", jax.ShapeDtypeStruct((second_rows + first_rows, F), jnp.int16),
+        [VMEM], VMEM, (panel,), 0.3,
+    )
+    rc = send_rep(to_core, 0, 0, 1)
     to_x = call(x_messages, "x_first", messages(8, FIRST), [VMEM, VMEM], VMEM, (panel, rc_cross), 0.6)
     rx_first = send_rep(to_x, 1, 0, 0)
-    rc_second, rc_first = lax.optimization_barrier((rc_second, rc_first))
-    second = sum_along_z(SECOND, "second", panel, rc_second, None)
+    second = sum_along_z(SECOND, "second", panel, rc, None)
     to_x, own_sum = call(
         z_end, "x_second", (messages(1, SECOND), jax.ShapeDtypeStruct((SECOND[1], F), jnp.float32)),
-        [VMEM] * 7, (VMEM,) * 2, (panel, rc_second, *second), 0.6,
+        [VMEM] * 7, (VMEM,) * 2, (panel, rc, *second), 0.6,
     )
     panel, to_x = lax.optimization_barrier((panel, to_x))
     rx_second = send_rep(to_x, 1, 0, 0)
-    first = sum_along_z(FIRST, "first", panel, rc_first, rx_first)
+    first = sum_along_z(FIRST, "first", panel, rc, rx_first)
     return call(
         layer, "layer", jax.ShapeDtypeStruct((PIECE_ROWS, H), jnp.bfloat16), [VMEM] * 11, VMEM,
-        (panel, rc_first, rx_first, own_sum, rx_second, *first, weight), 1.5,
+        (panel, rc, rx_first, own_sum, rx_second, *first, weight), 1.5,
     )
 
 

time: 65.1 us -> 63.4 us (0.974)
  starting transfers between devices: 35.7 us -> 33.7 us
    ppermute x7, starting transfers between devices: 11.7 us -> 9.23 us  [send_blk(): return lax.ppermute(array, 'blk', pairs)]
    ppermute x17 -> x16, starting transfers between devices: 24 us -> 24.5 us  [send_rep(): return lax.ppermute(array, 'rep', pairs)]
    ppermute x17 -> x16, waiting for transfers between devices: 13.3 us -> 13.1 us  [send_rep(): return lax.ppermute(array, 'rep', pairs)]
    pallas_call x13 -> x12, Pallas kernels: 10.6 us -> 10.8 us  [call(): pl.pallas_call(kernel, out_shape=out_shape, in_specs=in_specs, out_specs=...]
  transfers between devices with their start and end apart: 24 -> 23, of which waited for: 12 -> 11; matrix products, arithmetic and copies ran while one was open for 1% -> 1% of each run, Pallas kernels for 10% -> 13%
where the time goes in v5:
time: 63.4 us; the launch traced here: 62.7 us
  starting transfers between devices  33.7 us (53%)
  waiting for transfers between devices  16.4 us (26%)
  Pallas kernels  10.8 us (17%)
  local copies, waits for them, and re-layouts  0.9 us (1%)
  other arithmetic  0.77 us (1%)
    ppermute x16, starting transfers between devices, send_rep(): return lax.ppermute(array, 'rep', pairs)  24.5 us
    ppermute x16, waiting for transfers between devices, send_rep(): return lax.ppermute(array, 'rep', pairs)  13.1 us
    pallas_call x12, Pallas kernels, call(): pl.pallas_call(kernel, out_shape=out_shape, in_specs=in_specs, out_specs=...  10.8 us
    ppermute x7, starting transfers between devices, send_blk(): return lax.ppermute(array, 'blk', pairs)  9.23 us
    ppermute x7, waiting for transfers between devices, send_blk(): return lax.ppermute(array, 'blk', pairs)  3.25 us
  transfers between devices with their start and end apart: 23, of which 11 were waited for; matrix products, arithmetic and copies ran while one was open for 1% of the time, Pallas kernels for 13%

profile of v5, /device:TPU:2, one launch (start us, length us, event | category | flops | bytes accessed | tf_op | source)
XLA Modules:
  0.0 62.7 jit_solution(8396041134057296830)
XLA Ops:
  0.0 2.1 %collective-permute-start = (bf16[384,128]{1,0:T(8,128)(2,1)}, bf16[384,128]{1,0:T(8,128)(2,1)S(1)}, u32[]{:S(2)}, u32[]{:S(2)}) collective-permute-start(bf16[384,128]{1,0:T(8,128)(2,1)} %own_ref.1), channel_id=1, source_target_pairs={{0,32},{32,0},{64,96},{96,64},{128,160},{160,128},{192,224},{224,1... | collective-permute-start | bytes 294920 | tf_op jit(solution)/shard_map/ppermute | solution.py:306
  2.1 1.6 %collective-permute-start.4 = (bf16[384,128]{1,0:T(8,128)(2,1)}, bf16[384,128]{1,0:T(8,128)(2,1)S(1)}, u32[]{:S(2)}, u32[]{:S(2)}) collective-permute-start(bf16[384,128]{1,0:T(8,128)(2,1)} %own_ref.1), channel_id=1, source_target_pairs={{0,64},{32,96},{64,128},{96,160},{128,192},{160,224},{192,0},{224,... | collective-permute-start | bytes 294920 | tf_op jit(solution)/shard_map/ppermute | solution.py:306
  3.7 1.7 %collective-permute-start.1 = (bf16[384,128]{1,0:T(8,128)(2,1)}, bf16[384,128]{1,0:T(8,128)(2,1)S(1)}, u32[]{:S(2)}, u32[]{:S(2)}) collective-permute-start(bf16[384,128]{1,0:T(8,128)(2,1)} %own_ref.1), channel_id=1, source_target_pairs={{0,192},{32,224},{64,0},{96,32},{128,64},{160,96},{192,128},{224,1... | collective-permute-start | bytes 294920 | tf_op jit(solution)/shard_map/ppermute | solution.py:306
  7.0 2.3 %collective-permute-start.3 = (bf16[384,128]{1,0:T(8,128)(2,1)S(1)}, bf16[384,128]{1,0:T(8,128)(2,1)S(1)}, u32[]{:S(2)}, u32[]{:S(2)}) collective-permute-start(bf16[384,128]{1,0:T(8,128)(2,1)S(1)} %collective-permute-done.flipped_ref), channel_id=1, source_target_pairs={{0,192},{32,224},{64,0},{96,32},{128,64},{160,96},{192,128},{224,1... | collective-permute-start | bytes 294920 | tf_op jit(solution)/shard_map/ppermute | solution.py:306
  9.9 3.2 %products_here.1 = (f32[12416,128]{1,0:T(8,128)S(1)}, bf16[240,128,128]{2,1,0:T(8,128)(2,1)S(1)}) custom-call(s32[8,40]{1,0:T(8,128)S(1)} %bitcast_add_fusion.lists_ref.refs_0_, bf16[384,128]{1,0:T(8,128)(2,1)S(1)} %own_piece.1.own_ref, bf16[384,128]{1,0:T(8,128)(2,1)S(1)} %collective-permute-done.flipped_ref, bf16[320,128,128]{2,1,0:T(8,128)(2,1)} %bitcast.4), custom_call_target="tpu_custom_call" | custom-call | bytes 12000000 | tf_op jit(solution)/shard_map/products_here/pallas_call | solution.py:33
  13.1 2.0 %collective-permute-done.2.refs_2_ = bf16[384,128]{1,0:T(8,128)(2,1)S(1)} collective-permute-done((bf16[384,128]{1,0:T(8,128)(2,1)S(1)}, bf16[384,128]{1,0:T(8,128)(2,1)S(1)}, u32[]{:S(2)}, u32[]{:S(2)}) %collective-permute-start.2) | collective-permute-done | bytes 98336 | tf_op jit(solution)/shard_map/ppermute | solution.py:306
  17.2 3.5 %products_near.1.refs_1_ = f32[12416,128]{1,0:T(8,128)S(1)} custom-call(s32[8,40]{1,0:T(8,128)S(1)} %bitcast_add_fusion.lists_ref.refs_0_, f32[12416,128]{1,0:T(8,128)S(1)} %get-tuple-element.37._, bf16[240,128,128]{2,1,0:T(8,128)(2,1)S(1)} %get-tuple-element.38.vals.refs_2_, ...), custom_call_target="tpu_custom_call", output_to_operand_aliasing={{}: (1, {})} | custom-call | bytes 9000000 | tf_op jit(solution)/shard_map/products_near/pallas_call | solution.py:33
  20.8 1.3 %products_far.1 = (f32[12416,128]{1,0:T(8,128)S(1)}, s16[2320,128]{1,0:T(8,128)(2,1)S(1)}) custom-call(s32[8,40]{1,0:T(8,128)S(1)} %bitcast_add_fusion.lists_ref.refs_0_, f32[12416,128]{1,0:T(8,128)S(1)} %products_near.1.refs_1_, bf16[240,128,128]{2,1,0:T(8,128)(2,1)S(1)} %get-tuple-element.38.vals.refs_2_, ...), custom_call_target="tpu_custom_call", output_to_operand_aliasing={{0}: (1, {})} | custom-call | bytes 9000000 | tf_op jit(solution)/shard_map/products_far/pallas_call | solution.py:33
  23.2 1.1 %collective-permute-done.14.rc_ref = s16[2320,128]{1,0:T(8,128)(2,1)S(1)} collective-permute-done((s16[2320,128]{1,0:T(8,128)(2,1)S(1)}, s16[2320,128]{1,0:T(8,128)(2,1)S(1)}, u32[]{:S(2)}, u32[]{:S(2)}) %collective-permute-start.14) | collective-permute-done | bytes 593952 | tf_op jit(solution)/shard_map/ppermute | solution.py:314
  24.6 1.8 %collective-permute-start.15 = (s16[2320,128]{1,0:T(8,128)(2,1)S(1)}, s16[2320,128]{1,0:T(8,128)(2,1)S(1)}, u32[]{:S(2)}, u32[]{:S(2)}) collective-permute-start(s16[2320,128]{1,0:T(8,128)(2,1)S(1)} %x_first.1), channel_id=1, source_target_pairs={{0,16},{1,17},{2,18},{3,19},{4,20},{5,21},{6,22},{7,23},{8,24},{9,... | collective-permute-start | bytes 1781768 | tf_op jit(solution)/shard_map/ppermute | solution.py:314
  26.6 5.2 %collective-permute-start.8 = (s16[400,128]{1,0:T(8,128)(2,1)S(1)}, s16[400,128]{1,0:T(8,128)(2,1)S(1)}, u32[]{:S(2)}, u32[]{:S(2)}) collective-permute-start(s16[400,128]{1,0:T(8,128)(2,1)S(1)} %get-tuple-element.44), channel_id=1, source_target_pairs={{0,14},{1,15},{2,0},{3,1},{4,2},{5,3},{6,4},{7,5},{8,6},{9,7},{10,... | collective-permute-start | bytes 307208 | tf_op jit(solution)/shard_map/ppermute | solution.py:314
  31.8 3.2 %collective-permute-start.9 = (s16[208,128]{1,0:T(8,128)(2,1)S(1)}, s16[208,128]{1,0:T(8,128)(2,1)S(1)}, u32[]{:S(2)}, u32[]{:S(2)}) collective-permute-start(s16[208,128]{1,0:T(8,128)(2,1)S(1)} %get-tuple-element.45), channel_id=1, source_target_pairs={{0,12},{1,13},{2,14},{3,15},{4,0},{5,1},{6,2},{7,3},{8,4},{9,5},{1... | collective-permute-start | bytes 159752 | tf_op jit(solution)/shard_map/ppermute | solution.py:314
  35.0 2.1 %collective-permute-done.11.refs_1_ = s16[208,128]{1,0:T(8,128)(2,1)S(1)} collective-permute-done((s16[208,128]{1,0:T(8,128)(2,1)S(1)}, s16[208,128]{1,0:T(8,128)(2,1)S(1)}, u32[]{:S(2)}, u32[]{:S(2)}) %collective-permute-start.11) | collective-permute-done | bytes 53280 | tf_op jit(solution)/shard_map/ppermute | solution.py:314
  37.3 3.0 %collective-permute-start.12 = (s16[208,128]{1,0:T(8,128)(2,1)S(1)}, s16[208,128]{1,0:T(8,128)(2,1)S(1)}, u32[]{:S(2)}, u32[]{:S(2)}) collective-permute-start(s16[208,128]{1,0:T(8,128)(2,1)S(1)} %get-tuple-element.48), channel_id=1, source_target_pairs={{0,10},{1,11},{2,12},{3,13},{4,14},{5,15},{6,0},{7,1},{8,2},{9,3},... | collective-permute-start | bytes 159752 | tf_op jit(solution)/shard_map/ppermute | solution.py:314
  40.3 1.5 %collective-permute-start.13 = (s16[208,128]{1,0:T(8,128)(2,1)S(1)}, s16[208,128]{1,0:T(8,128)(2,1)S(1)}, u32[]{:S(2)}, u32[]{:S(2)}) collective-permute-start(s16[208,128]{1,0:T(8,128)(2,1)S(1)} %get-tuple-element.49), channel_id=1, source_target_pairs={{0,2},{1,3},{2,4},{3,5},{4,6},{5,7},{6,8},{7,9},{8,10},{9,11},{10,... | collective-permute-start | bytes 159752 | tf_op jit(solution)/shard_map/ppermute | solution.py:314
  41.7 1.4 %collective-permute-done.10.refs_2_ = s16[208,128]{1,0:T(8,128)(2,1)S(1)} collective-permute-done((s16[208,128]{1,0:T(8,128)(2,1)S(1)}, s16[208,128]{1,0:T(8,128)(2,1)S(1)}, u32[]{:S(2)}, u32[]{:S(2)}) %collective-permute-start.10) | collective-permute-done | bytes 53280 | tf_op jit(solution)/shard_map/ppermute | solution.py:314
  43.1 1.4 %collective-permute-done.12.refs_3_ = s16[208,128]{1,0:T(8,128)(2,1)S(1)} collective-permute-done((s16[208,128]{1,0:T(8,128)(2,1)S(1)}, s16[208,128]{1,0:T(8,128)(2,1)S(1)}, u32[]{:S(2)}, u32[]{:S(2)}) %collective-permute-start.12) | collective-permute-done | bytes 53280 | tf_op jit(solution)/shard_map/ppermute | solution.py:314
  46.5 1.8 %collective-permute-start.20 = (s16[304,128]{1,0:T(8,128)(2,1)S(1)}, s16[304,128]{1,0:T(8,128)(2,1)S(1)}, u32[]{:S(2)}, u32[]{:S(2)}) collective-permute-start(s16[304,128]{1,0:T(8,128)(2,1)S(1)} %get-tuple-element.58), channel_id=1, source_target_pairs={{0,2},{1,3},{2,4},{3,5},{4,6},{5,7},{6,8},{7,9},{8,10},{9,11},{10,... | collective-permute-start | bytes 233480 | tf_op jit(solution)/shard_map/ppermute | solution.py:314
  48.3 1.8 %collective-permute-start.18 = (s16[304,128]{1,0:T(8,128)(2,1)S(1)}, s16[304,128]{1,0:T(8,128)(2,1)S(1)}, u32[]{:S(2)}, u32[]{:S(2)}) collective-permute-start(s16[304,128]{1,0:T(8,128)(2,1)S(1)} %get-tuple-element.56), channel_id=1, source_target_pairs={{0,12},{1,13},{2,14},{3,15},{4,0},{5,1},{6,2},{7,3},{8,4},{9,5},{1... | collective-permute-start | bytes 233480 | tf_op jit(solution)/shard_map/ppermute | solution.py:314
  50.9 1.7 %collective-permute-done.20.up_ref = s16[304,128]{1,0:T(8,128)(2,1)S(1)} collective-permute-done((s16[304,128]{1,0:T(8,128)(2,1)S(1)}, s16[304,128]{1,0:T(8,128)(2,1)S(1)}, u32[]{:S(2)}, u32[]{:S(2)}) %collective-permute-start.20) | collective-permute-done | bytes 77856 | tf_op jit(solution)/shard_map/ppermute | solution.py:314
  53.2 2.2 %collective-permute-start.21 = (s16[304,128]{1,0:T(8,128)(2,1)S(1)}, s16[304,128]{1,0:T(8,128)(2,1)S(1)}, u32[]{:S(2)}, u32[]{:S(2)}) collective-permute-start(s16[304,128]{1,0:T(8,128)(2,1)S(1)} %get-tuple-element.59), channel_id=1, source_target_pairs={{0,10},{1,11},{2,12},{3,13},{4,14},{5,15},{6,0},{7,1},{8,2},{9,3},... | collective-permute-start | bytes 233480 | tf_op jit(solution)/shard_map/ppermute | solution.py:314
  55.4 2.3 %collective-permute-start.22 = (s16[304,128]{1,0:T(8,128)(2,1)S(1)}, s16[304,128]{1,0:T(8,128)(2,1)S(1)}, u32[]{:S(2)}, u32[]{:S(2)}) collective-permute-start(s16[304,128]{1,0:T(8,128)(2,1)S(1)} %get-tuple-element.60), channel_id=1, source_target_pairs={{0,2},{1,3},{2,4},{3,5},{4,6},{5,7},{6,8},{7,9},{8,10},{9,11},{10,... | collective-permute-start | bytes 233480 | tf_op jit(solution)/shard_map/ppermute | solution.py:314
  57.7 3.9 %collective-permute-done.16.rx2_ref = s16[112,128]{1,0:T(8,128)(2,1)S(1)} collective-permute-done((s16[112,128]{1,0:T(8,128)(2,1)S(1)}, s16[112,128]{1,0:T(8,128)(2,1)S(1)}, u32[]{:S(2)}, u32[]{:S(2)}) %collective-permute-start.16) | collective-permute-done | bytes 28704 | tf_op jit(solution)/shard_map/ppermute | solution.py:314
  61.6 1.1 %layer.1 = bf16[384,256]{1,0:T(8,128)(2,1)} custom-call(f32[12416,128]{1,0:T(8,128)S(1)} %get-tuple-element.51.panel.panel_ref, s16[3872,128]{1,0:T(8,128)(2,1)S(1)} %collective-permute-done.7.rc_ref, s16[2320,128]{1,0:T(8,128)(2,1)S(1)} %collective-permute-done.15.rx_ref, f32[96,128]{1,0:T(8,128)S(1)} %get-tuple-element.53.sum_ref, ...), custom_call_target="tpu_custom_call" | custom-call | bytes 4500000 | tf_op jit(solution)/shard_map/layer/pallas_call | solution.py:33
  (39 shorter events, 9.6 us)
Async XLA Ops:
  0.0 7.0 %collective-permute-start = (bf16[384,128]{1,0:T(8,128)(2,1)}, bf16[384,128]{1,0:T(8,128)(2,1)S(1)}, u32[]{:S(2)}, u32[]{:S(2)}) collective-permute-start(bf16[384,128]{1,0:T(8,128)(2,1)} %own_ref.1), channel_id=1, source_target_pairs={{0,32},{32,0},{64,96},{96,64},{128,160},{160,128},{192,224},{224,1... | collective-permute-start | bytes 294920 | tf_op jit(solution)/shard_map/ppermute | solution.py:306
  2.1 7.2 %collective-permute-start.4 = (bf16[384,128]{1,0:T(8,128)(2,1)}, bf16[384,128]{1,0:T(8,128)(2,1)S(1)}, u32[]{:S(2)}, u32[]{:S(2)}) collective-permute-start(bf16[384,128]{1,0:T(8,128)(2,1)} %own_ref.1), channel_id=1, source_target_pairs={{0,64},{32,96},{64,128},{96,160},{128,192},{160,224},{192,0},{224,... | collective-permute-start | bytes 294920 | tf_op jit(solution)/shard_map/ppermute | solution.py:306
  3.7 9.4 %collective-permute-start.1 = (bf16[384,128]{1,0:T(8,128)(2,1)}, bf16[384,128]{1,0:T(8,128)(2,1)S(1)}, u32[]{:S(2)}, u32[]{:S(2)}) collective-permute-start(bf16[384,128]{1,0:T(8,128)(2,1)} %own_ref.1), channel_id=1, source_target_pairs={{0,192},{32,224},{64,0},{96,32},{128,64},{160,96},{192,128},{224,1... | collective-permute-start | bytes 294920 | tf_op jit(solution)/shard_map/ppermute | solution.py:306
  7.0 6.1 %collective-permute-start.3 = (bf16[384,128]{1,0:T(8,128)(2,1)S(1)}, bf16[384,128]{1,0:T(8,128)(2,1)S(1)}, u32[]{:S(2)}, u32[]{:S(2)}) collective-permute-start(bf16[384,128]{1,0:T(8,128)(2,1)S(1)} %collective-permute-done.flipped_ref), channel_id=1, source_target_pairs={{0,192},{32,224},{64,0},{96,32},{128,64},{160,96},{192,128},{224,1... | collective-permute-start | bytes 294920 | tf_op jit(solution)/shard_map/ppermute | solution.py:306
  9.3 5.8 %collective-permute-start.2 = (bf16[384,128]{1,0:T(8,128)(2,1)S(1)}, bf16[384,128]{1,0:T(8,128)(2,1)S(1)}, u32[]{:S(2)}, u32[]{:S(2)}) collective-permute-start(bf16[384,128]{1,0:T(8,128)(2,1)S(1)} %collective-permute-done.flipped_ref), channel_id=1, source_target_pairs={{0,64},{32,96},{64,128},{96,160},{128,192},{160,224},{192,0},{224,... | collective-permute-start | bytes 294920 | tf_op jit(solution)/shard_map/ppermute | solution.py:306
  9.4 6.9 %collective-permute-start.5 = (bf16[384,128]{1,0:T(8,128)(2,1)S(1)}, bf16[384,128]{1,0:T(8,128)(2,1)S(1)}, u32[]{:S(2)}, u32[]{:S(2)}) collective-permute-start(bf16[384,128]{1,0:T(8,128)(2,1)S(1)} %collective-permute-done.4.refs_0_), channel_id=1, source_target_pairs={{0,64},{32,96},{64,128},{96,160},{128,192},{160,224},{192,0},{224,... | collective-permute-start | bytes 294920 | tf_op jit(solution)/shard_map/ppermute | solution.py:306
  16.2 4.6 %collective-permute-start.6 = (bf16[384,128]{1,0:T(8,128)(2,1)S(1)}, bf16[384,128]{1,0:T(8,128)(2,1)S(1)}, u32[]{:S(2)}, u32[]{:S(2)}) collective-permute-start(bf16[384,128]{1,0:T(8,128)(2,1)S(1)} %collective-permute-done.3.refs_3_), channel_id=1, source_target_pairs={{0,192},{32,224},{64,0},{96,32},{128,64},{160,96},{192,128},{224,1... | collective-permute-start | bytes 294920 | tf_op jit(solution)/shard_map/ppermute | solution.py:306
  22.1 2.1 %collective-permute-start.14 = (s16[2320,128]{1,0:T(8,128)(2,1)S(1)}, s16[2320,128]{1,0:T(8,128)(2,1)S(1)}, u32[]{:S(2)}, u32[]{:S(2)}) collective-permute-start(s16[2320,128]{1,0:T(8,128)(2,1)S(1)} %get-tuple-element.52), channel_id=1, source_target_pairs={{0,1},{1,0},{2,3},{3,2},{4,5},{5,4},{6,7},{7,6},{8,9},{9,8},{10,11... | collective-permute-start | bytes 1781768 | tf_op jit(solution)/shard_map/ppermute | solution.py:314
  22.6 3.8 %collective-permute-start.7 = (s16[3872,128]{1,0:T(8,128)(2,1)S(1)}, s16[3872,128]{1,0:T(8,128)(2,1)S(1)}, u32[]{:S(2)}, u32[]{:S(2)}) collective-permute-start(s16[3872,128]{1,0:T(8,128)(2,1)S(1)} %core_rest.1), channel_id=1, source_target_pairs={{0,1},{1,0},{2,3},{3,2},{4,5},{5,4},{6,7},{7,6},{8,9},{9,8},{10,11... | collective-permute-start | bytes 2973704 | tf_op jit(solution)/shard_map/ppermute | solution.py:314
  24.6 21.1 %collective-permute-start.15 = (s16[2320,128]{1,0:T(8,128)(2,1)S(1)}, s16[2320,128]{1,0:T(8,128)(2,1)S(1)}, u32[]{:S(2)}, u32[]{:S(2)}) collective-permute-start(s16[2320,128]{1,0:T(8,128)(2,1)S(1)} %x_first.1), channel_id=1, source_target_pairs={{0,16},{1,17},{2,18},{3,19},{4,20},{5,21},{6,22},{7,23},{8,24},{9,... | collective-permute-start | bytes 1781768 | tf_op jit(solution)/shard_map/ppermute | solution.py:314
  26.6 10.5 %collective-permute-start.8 = (s16[400,128]{1,0:T(8,128)(2,1)S(1)}, s16[400,128]{1,0:T(8,128)(2,1)S(1)}, u32[]{:S(2)}, u32[]{:S(2)}) collective-permute-start(s16[400,128]{1,0:T(8,128)(2,1)S(1)} %get-tuple-element.44), channel_id=1, source_target_pairs={{0,14},{1,15},{2,0},{3,1},{4,2},{5,3},{6,4},{7,5},{8,6},{9,7},{10,... | collective-permute-start | bytes 307208 | tf_op jit(solution)/shard_map/ppermute | solution.py:314
  31.8 5.3 %collective-permute-start.11 = (s16[208,128]{1,0:T(8,128)(2,1)S(1)}, s16[208,128]{1,0:T(8,128)(2,1)S(1)}, u32[]{:S(2)}, u32[]{:S(2)}) collective-permute-start(s16[208,128]{1,0:T(8,128)(2,1)S(1)} %get-tuple-element.47), channel_id=1, source_target_pairs={{0,2},{1,3},{2,4},{3,5},{4,6},{5,7},{6,8},{7,9},{8,10},{9,11},{10,... | collective-permute-start | bytes 159752 | tf_op jit(solution)/shard_map/ppermute | solution.py:314
  31.8 9.9 %collective-permute-start.9 = (s16[208,128]{1,0:T(8,128)(2,1)S(1)}, s16[208,128]{1,0:T(8,128)(2,1)S(1)}, u32[]{:S(2)}, u32[]{:S(2)}) collective-permute-start(s16[208,128]{1,0:T(8,128)(2,1)S(1)} %get-tuple-element.45), channel_id=1, source_target_pairs={{0,12},{1,13},{2,14},{3,15},{4,0},{5,1},{6,2},{7,3},{8,4},{9,5},{1... | collective-permute-start | bytes 159752 | tf_op jit(solution)/shard_map/ppermute | solution.py:314
  35.0 8.1 %collective-permute-start.10 = (s16[208,128]{1,0:T(8,128)(2,1)S(1)}, s16[208,128]{1,0:T(8,128)(2,1)S(1)}, u32[]{:S(2)}, u32[]{:S(2)}) collective-permute-start(s16[208,128]{1,0:T(8,128)(2,1)S(1)} %get-tuple-element.46), channel_id=1, source_target_pairs={{0,6},{1,7},{2,8},{3,9},{4,10},{5,11},{6,12},{7,13},{8,14},{9,15},... | collective-permute-start | bytes 159752 | tf_op jit(solution)/shard_map/ppermute | solution.py:314
  37.3 7.3 %collective-permute-start.12 = (s16[208,128]{1,0:T(8,128)(2,1)S(1)}, s16[208,128]{1,0:T(8,128)(2,1)S(1)}, u32[]{:S(2)}, u32[]{:S(2)}) collective-permute-start(s16[208,128]{1,0:T(8,128)(2,1)S(1)} %get-tuple-element.48), channel_id=1, source_target_pairs={{0,10},{1,11},{2,12},{3,13},{4,14},{5,15},{6,0},{7,1},{8,2},{9,3},... | collective-permute-start | bytes 159752 | tf_op jit(solution)/shard_map/ppermute | solution.py:314
  40.3 5.3 %collective-permute-start.13 = (s16[208,128]{1,0:T(8,128)(2,1)S(1)}, s16[208,128]{1,0:T(8,128)(2,1)S(1)}, u32[]{:S(2)}, u32[]{:S(2)}) collective-permute-start(s16[208,128]{1,0:T(8,128)(2,1)S(1)} %get-tuple-element.49), channel_id=1, source_target_pairs={{0,2},{1,3},{2,4},{3,5},{4,6},{5,7},{6,8},{7,9},{8,10},{9,11},{10,... | collective-permute-start | bytes 159752 | tf_op jit(solution)/shard_map/ppermute | solution.py:314
  45.7 15.9 %copy-start.1 = (bf16[128,256]{1,0:T(8,128)(2,1)S(1)}, bf16[128,256]{1,0:T(8,128)(2,1)}, u32[]{:S(2)}) copy-start(bf16[128,256]{1,0:T(8,128)(2,1)} %refs_5_.1) | copy-start | bytes 196612
  46.1 6.9 %collective-permute-start.17 = (s16[592,128]{1,0:T(8,128)(2,1)S(1)}, s16[592,128]{1,0:T(8,128)(2,1)S(1)}, u32[]{:S(2)}, u32[]{:S(2)}) collective-permute-start(s16[592,128]{1,0:T(8,128)(2,1)S(1)} %get-tuple-element.55), channel_id=1, source_target_pairs={{0,14},{1,15},{2,0},{3,1},{4,2},{5,3},{6,4},{7,5},{8,6},{9,7},{10,... | collective-permute-start | bytes 454664 | tf_op jit(solution)/shard_map/ppermute | solution.py:314
  46.5 6.1 %collective-permute-start.20 = (s16[304,128]{1,0:T(8,128)(2,1)S(1)}, s16[304,128]{1,0:T(8,128)(2,1)S(1)}, u32[]{:S(2)}, u32[]{:S(2)}) collective-permute-start(s16[304,128]{1,0:T(8,128)(2,1)S(1)} %get-tuple-element.58), channel_id=1, source_target_pairs={{0,2},{1,3},{2,4},{3,5},{4,6},{5,7},{6,8},{7,9},{8,10},{9,11},{10,... | collective-permute-start | bytes 233480 | tf_op jit(solution)/shard_map/ppermute | solution.py:314
  48.3 13.3 %collective-permute-start.18 = (s16[304,128]{1,0:T(8,128)(2,1)S(1)}, s16[304,128]{1,0:T(8,128)(2,1)S(1)}, u32[]{:S(2)}, u32[]{:S(2)}) collective-permute-start(s16[304,128]{1,0:T(8,128)(2,1)S(1)} %get-tuple-element.56), channel_id=1, source_target_pairs={{0,12},{1,13},{2,14},{3,15},{4,0},{5,1},{6,2},{7,3},{8,4},{9,5},{1... | collective-permute-start | bytes 233480 | tf_op jit(solution)/shard_map/ppermute | solution.py:314
  50.1 11.5 %collective-permute-start.19 = (s16[304,128]{1,0:T(8,128)(2,1)S(1)}, s16[304,128]{1,0:T(8,128)(2,1)S(1)}, u32[]{:S(2)}, u32[]{:S(2)}) collective-permute-start(s16[304,128]{1,0:T(8,128)(2,1)S(1)} %get-tuple-element.57), channel_id=1, source_target_pairs={{0,6},{1,7},{2,8},{3,9},{4,10},{5,11},{6,12},{7,13},{8,14},{9,15},... | collective-permute-start | bytes 233480 | tf_op jit(solution)/shard_map/ppermute | solution.py:314
  53.2 8.3 %collective-permute-start.21 = (s16[304,128]{1,0:T(8,128)(2,1)S(1)}, s16[304,128]{1,0:T(8,128)(2,1)S(1)}, u32[]{:S(2)}, u32[]{:S(2)}) collective-permute-start(s16[304,128]{1,0:T(8,128)(2,1)S(1)} %get-tuple-element.59), channel_id=1, source_target_pairs={{0,10},{1,11},{2,12},{3,13},{4,14},{5,15},{6,0},{7,1},{8,2},{9,3},... | collective-permute-start | bytes 233480 | tf_op jit(solution)/shard_map/ppermute | solution.py:314
  55.4 6.1 %collective-permute-start.22 = (s16[304,128]{1,0:T(8,128)(2,1)S(1)}, s16[304,128]{1,0:T(8,128)(2,1)S(1)}, u32[]{:S(2)}, u32[]{:S(2)}) collective-permute-start(s16[304,128]{1,0:T(8,128)(2,1)S(1)} %get-tuple-element.60), channel_id=1, source_target_pairs={{0,2},{1,3},{2,4},{3,5},{4,6},{5,7},{6,8},{7,9},{8,10},{9,11},{10,... | collective-permute-start | bytes 233480 | tf_op jit(solution)/shard_map/ppermute | solution.py:314
  57.7 3.9 %collective-permute-start.16 = (s16[112,128]{1,0:T(8,128)(2,1)S(1)}, s16[112,128]{1,0:T(8,128)(2,1)S(1)}, u32[]{:S(2)}, u32[]{:S(2)}) collective-permute-start(s16[112,128]{1,0:T(8,128)(2,1)S(1)} %get-tuple-element.54), channel_id=1, source_target_pairs={{0,16},{1,17},{2,18},{3,19},{4,20},{5,21},{6,22},{7,23},{8,24},{9,... | collective-permute-start | bytes 86024 | tf_op jit(solution)/shard_map/ppermute | solution.py:314
  (1 other events, 0.9 us)

commit v6 on v5

--- a/solution.py
+++ b/solution.py
@@ -241,9 +241,9 @@
     return (0,) if part == FIRST else (0, 1)
 
 
-def z_start(part, panel, rc_ref, rx_ref, down_ref, up_ref, two_ref, far_ref):
-    here = Here(panel)
-    for out_ref, shifts in ((down_ref, (-4, -1)), (up_ref, (2,)), (two_ref, (-2,)), (far_ref, (3,))):
+def z_start(part, panel, rc_ref, rx_ref, down_ref, up_ref, two_ref):
+    here = Here(panel)
+    for out_ref, shifts in ((down_ref, (-4, -1)), (up_ref, (2,)), (two_ref, (-2,))):
         write_messages(
             out_ref, part,
             [
@@ -253,7 +253,7 @@
         )
 
 
-def z_middle(part, panel, rc_ref, rx_ref, down_ref, up_ref, three_ref, one_ref):
+def z_middle(part, panel, rc_ref, rx_ref, down_ref, up_ref, three_ref, one_ref, far_ref):
     here = Here(panel)
 
     def through(come_ref, stride, shift):
@@ -267,6 +267,10 @@
 
     write_messages(three_ref, part, through(down_ref, 2, -3))
     write_messages(one_ref, part, through(up_ref, 1, 1))
+    write_messages(
+        far_ref, part,
+        [functools.partial(base_value, part, here, rc_ref, rx_ref, other, here.z_of(3)) for other in sides(part)],
+    )
 
 
 def arrivals(part, other, down_ref, *refs):
@@ -323,17 +327,17 @@
             return functools.partial(kernel, part)
         return lambda panel_ref, rc_ref, *refs: kernel(part, panel_ref, rc_ref, None, *refs)
 
-    down, up, two, far = call(
-        fill(z_start), name + "_start", (messages(2 * count, part),) + (messages(count, part),) * 3,
-        [VMEM] * (1 + len(have)), (VMEM,) * 4, (panel, *have), 0.6,
+    down, up, two = call(
+        fill(z_start), name + "_start", (messages(2 * count, part),) + (messages(count, part),) * 2,
+        [VMEM] * (1 + len(have)), (VMEM,) * 3, (panel, *have), 0.6,
     )
     down, up = send_rep(down, 0, -1, 0), send_rep(up, 0, 1, 0)
-    two, far = send_rep(two, 0, -2, 0), send_rep(far, 0, 3, 0)
-    three, one = call(
-        fill(z_middle), name + "_middle", (messages(count, part),) * 2,
-        [VMEM] * (3 + len(have)), (VMEM,) * 2, (panel, *have, down, up), 0.6,
-    )
-    return down, two, far, send_rep(three, 0, -3, 0), send_rep(one, 0, 1, 0)
+    two = send_rep(two, 0, -2, 0)
+    three, one, far = call(
+        fill(z_middle), name + "_middle", (messages(count, part),) * 3,
+        [VMEM] * (3 + len(have)), (VMEM,) * 3, (panel, *have, down, up), 0.6,
+    )
+    return down, two, send_rep(far, 0, 3, 0), send_rep(three, 0, -3, 0), send_rep(one, 0, 1, 0)
 
 
 def local(node_feats, block_vals, block_rows, block_cols, block_count, weight):

time: 63.4 us -> 67.2 us (1.060)
  waiting for transfers between devices: 16.4 us -> 19.8 us
  starting transfers between devices: 33.7 us -> 34.6 us
    ppermute x16, waiting for transfers between devices: 13.1 us -> 16.2 us  [send_rep(): return lax.ppermute(array, 'rep', pairs)]
    ppermute x16, starting transfers between devices: 24.5 us -> 25.4 us  [send_rep(): return lax.ppermute(array, 'rep', pairs)]
  transfers between devices with their start and end apart: 23 -> 23, of which waited for: 11 -> 11; matrix products, arithmetic and copies ran while one was open for 1% -> 1% of each run, Pallas kernels for 13% -> 12%
where the time goes in v6:
time: 67.2 us; the launch traced here: 66.4 us
  starting transfers between devices  34.6 us (51%)
  waiting for transfers between devices  19.8 us (29%)
  Pallas kernels  10.2 us (15%)
  local copies, waits for them, and re-layouts  0.9 us (1%)
  other arithmetic  0.77 us (1%)
    ppermute x16, starting transfers between devices, send_rep(): return lax.ppermute(array, 'rep', pairs)  25.4 us
    ppermute x16, waiting for transfers between devices, send_rep(): return lax.ppermute(array, 'rep', pairs)  16.2 us
    pallas_call x12, Pallas kernels, call(): pl.pallas_call(kernel, out_shape=out_shape, in_specs=in_specs, out_specs=...  10.2 us
    ppermute x7, starting transfers between devices, send_blk(): return lax.ppermute(array, 'blk', pairs)  9.23 us
    ppermute x7, waiting for transfers between devices, send_blk(): return lax.ppermute(array, 'blk', pairs)  3.64 us
  transfers between devices with their start and end apart: 23, of which 11 were waited for; matrix products, arithmetic and copies ran while one was open for 1% of the time, Pallas kernels for 12%

profile of v6, /device:TPU:2, one launch (start us, length us, event | category | flops | bytes accessed | tf_op | source)
XLA Modules:
  0.0 66.4 jit_solution(24457720314209674)
XLA Ops:
  0.0 2.1 %collective-permute-start = (bf16[384,128]{1,0:T(8,128)(2,1)}, bf16[384,128]{1,0:T(8,128)(2,1)S(1)}, u32[]{:S(2)}, u32[]{:S(2)}) collective-permute-start(bf16[384,128]{1,0:T(8,128)(2,1)} %own_ref.1), channel_id=1, source_target_pairs={{0,32},{32,0},{64,96},{96,64},{128,160},{160,128},{192,224},{224,1... | collective-permute-start | bytes 294920 | tf_op jit(solution)/shard_map/ppermute | solution.py:310
  2.1 1.6 %collective-permute-start.4 = (bf16[384,128]{1,0:T(8,128)(2,1)}, bf16[384,128]{1,0:T(8,128)(2,1)S(1)}, u32[]{:S(2)}, u32[]{:S(2)}) collective-permute-start(bf16[384,128]{1,0:T(8,128)(2,1)} %own_ref.1), channel_id=1, source_target_pairs={{0,64},{32,96},{64,128},{96,160},{128,192},{160,224},{192,0},{224,... | collective-permute-start | bytes 294920 | tf_op jit(solution)/shard_map/ppermute | solution.py:310
  3.7 1.7 %collective-permute-start.1 = (bf16[384,128]{1,0:T(8,128)(2,1)}, bf16[384,128]{1,0:T(8,128)(2,1)S(1)}, u32[]{:S(2)}, u32[]{:S(2)}) collective-permute-start(bf16[384,128]{1,0:T(8,128)(2,1)} %own_ref.1), channel_id=1, source_target_pairs={{0,192},{32,224},{64,0},{96,32},{128,64},{160,96},{192,128},{224,1... | collective-permute-start | bytes 294920 | tf_op jit(solution)/shard_map/ppermute | solution.py:310
  7.0 2.3 %collective-permute-start.3 = (bf16[384,128]{1,0:T(8,128)(2,1)S(1)}, bf16[384,128]{1,0:T(8,128)(2,1)S(1)}, u32[]{:S(2)}, u32[]{:S(2)}) collective-permute-start(bf16[384,128]{1,0:T(8,128)(2,1)S(1)} %collective-permute-done.flipped_ref), channel_id=1, source_target_pairs={{0,192},{32,224},{64,0},{96,32},{128,64},{160,96},{192,128},{224,1... | collective-permute-start | bytes 294920 | tf_op jit(solution)/shard_map/ppermute | solution.py:310
  9.9 3.5 %products_here.1 = (f32[12416,128]{1,0:T(8,128)S(1)}, bf16[240,128,128]{2,1,0:T(8,128)(2,1)S(1)}) custom-call(s32[8,40]{1,0:T(8,128)S(1)} %bitcast_add_fusion.lists_ref.refs_0_, bf16[384,128]{1,0:T(8,128)(2,1)S(1)} %own_piece.1.own_ref, bf16[384,128]{1,0:T(8,128)(2,1)S(1)} %collective-permute-done.flipped_ref, bf16[320,128,128]{2,1,0:T(8,128)(2,1)} %bitcast.4), custom_call_target="tpu_custom_call" | custom-call | bytes 12000000 | tf_op jit(solution)/shard_map/products_here/pallas_call | solution.py:33
  13.5 1.7 %collective-permute-done.2.refs_2_ = bf16[384,128]{1,0:T(8,128)(2,1)S(1)} collective-permute-done((bf16[384,128]{1,0:T(8,128)(2,1)S(1)}, bf16[384,128]{1,0:T(8,128)(2,1)S(1)}, u32[]{:S(2)}, u32[]{:S(2)}) %collective-permute-start.2) | collective-permute-done | bytes 98336 | tf_op jit(solution)/shard_map/ppermute | solution.py:310
  15.2 1.1 %collective-permute-done.5.refs_4_ = bf16[384,128]{1,0:T(8,128)(2,1)S(1)} collective-permute-done((bf16[384,128]{1,0:T(8,128)(2,1)S(1)}, bf16[384,128]{1,0:T(8,128)(2,1)S(1)}, u32[]{:S(2)}, u32[]{:S(2)}) %collective-permute-start.5) | collective-permute-done | bytes 98336 | tf_op jit(solution)/shard_map/ppermute | solution.py:310
  17.2 2.8 %products_near.1.refs_1_ = f32[12416,128]{1,0:T(8,128)S(1)} custom-call(s32[8,40]{1,0:T(8,128)S(1)} %bitcast_add_fusion.lists_ref.refs_0_, f32[12416,128]{1,0:T(8,128)S(1)} %get-tuple-element.37._, bf16[240,128,128]{2,1,0:T(8,128)(2,1)S(1)} %get-tuple-element.38.vals.refs_2_, ...), custom_call_target="tpu_custom_call", output_to_operand_aliasing={{}: (1, {})} | custom-call | bytes 9000000 | tf_op jit(solution)/shard_map/products_near/pallas_call | solution.py:33
  20.8 1.1 %products_far.1 = (f32[12416,128]{1,0:T(8,128)S(1)}, s16[2320,128]{1,0:T(8,128)(2,1)S(1)}) custom-call(s32[8,40]{1,0:T(8,128)S(1)} %bitcast_add_fusion.lists_ref.refs_0_, f32[12416,128]{1,0:T(8,128)S(1)} %products_near.1.refs_1_, bf16[240,128,128]{2,1,0:T(8,128)(2,1)S(1)} %get-tuple-element.38.vals.refs_2_, ...), custom_call_target="tpu_custom_call", output_to_operand_aliasing={{0}: (1, {})} | custom-call | bytes 9000000 | tf_op jit(solution)/shard_map/products_far/pallas_call | solution.py:33
  22.9 1.1 %collective-permute-done.14.rc_ref = s16[2320,128]{1,0:T(8,128)(2,1)S(1)} collective-permute-done((s16[2320,128]{1,0:T(8,128)(2,1)S(1)}, s16[2320,128]{1,0:T(8,128)(2,1)S(1)}, u32[]{:S(2)}, u32[]{:S(2)}) %collective-permute-start.14) | collective-permute-done | bytes 593952 | tf_op jit(solution)/shard_map/ppermute | solution.py:318
  24.4 1.3 %collective-permute-start.15 = (s16[2320,128]{1,0:T(8,128)(2,1)S(1)}, s16[2320,128]{1,0:T(8,128)(2,1)S(1)}, u32[]{:S(2)}, u32[]{:S(2)}) collective-permute-start(s16[2320,128]{1,0:T(8,128)(2,1)S(1)} %x_first.1), channel_id=1, source_target_pairs={{0,16},{1,17},{2,18},{3,19},{4,20},{5,21},{6,22},{7,23},{8,24},{9,... | collective-permute-start | bytes 1781768 | tf_op jit(solution)/shard_map/ppermute | solution.py:318
  25.9 5.9 %collective-permute-start.8 = (s16[400,128]{1,0:T(8,128)(2,1)S(1)}, s16[400,128]{1,0:T(8,128)(2,1)S(1)}, u32[]{:S(2)}, u32[]{:S(2)}) collective-permute-start(s16[400,128]{1,0:T(8,128)(2,1)S(1)} %get-tuple-element.44), channel_id=1, source_target_pairs={{0,14},{1,15},{2,0},{3,1},{4,2},{5,3},{6,4},{7,5},{8,6},{9,7},{10,... | collective-permute-start | bytes 307208 | tf_op jit(solution)/shard_map/ppermute | solution.py:318
  31.8 2.5 %collective-permute-start.9 = (s16[208,128]{1,0:T(8,128)(2,1)S(1)}, s16[208,128]{1,0:T(8,128)(2,1)S(1)}, u32[]{:S(2)}, u32[]{:S(2)}) collective-permute-start(s16[208,128]{1,0:T(8,128)(2,1)S(1)} %get-tuple-element.45), channel_id=1, source_target_pairs={{0,12},{1,13},{2,14},{3,15},{4,0},{5,1},{6,2},{7,3},{8,4},{9,5},{1... | collective-permute-start | bytes 159752 | tf_op jit(solution)/shard_map/ppermute | solution.py:318
  34.3 2.9 %collective-permute-done.10.refs_1_ = s16[208,128]{1,0:T(8,128)(2,1)S(1)} collective-permute-done((s16[208,128]{1,0:T(8,128)(2,1)S(1)}, s16[208,128]{1,0:T(8,128)(2,1)S(1)}, u32[]{:S(2)}, u32[]{:S(2)}) %collective-permute-start.10) | collective-permute-done | bytes 53280 | tf_op jit(solution)/shard_map/ppermute | solution.py:318
  38.2 4.4 %collective-permute-start.12 = (s16[208,128]{1,0:T(8,128)(2,1)S(1)}, s16[208,128]{1,0:T(8,128)(2,1)S(1)}, u32[]{:S(2)}, u32[]{:S(2)}) collective-permute-start(s16[208,128]{1,0:T(8,128)(2,1)S(1)} %get-tuple-element.48), channel_id=1, source_target_pairs={{0,10},{1,11},{2,12},{3,13},{4,14},{5,15},{6,0},{7,1},{8,2},{9,3},... | collective-permute-start | bytes 159752 | tf_op jit(solution)/shard_map/ppermute | solution.py:318
  42.6 2.6 %collective-permute-done.11.refs_2_ = s16[208,128]{1,0:T(8,128)(2,1)S(1)} collective-permute-done((s16[208,128]{1,0:T(8,128)(2,1)S(1)}, s16[208,128]{1,0:T(8,128)(2,1)S(1)}, u32[]{:S(2)}, u32[]{:S(2)}) %collective-permute-start.11) | collective-permute-done | bytes 53280 | tf_op jit(solution)/shard_map/ppermute | solution.py:318
  45.3 2.7 %collective-permute-done.13.refs_4_ = s16[208,128]{1,0:T(8,128)(2,1)S(1)} collective-permute-done((s16[208,128]{1,0:T(8,128)(2,1)S(1)}, s16[208,128]{1,0:T(8,128)(2,1)S(1)}, u32[]{:S(2)}, u32[]{:S(2)}) %collective-permute-start.13) | collective-permute-done | bytes 53280 | tf_op jit(solution)/shard_map/ppermute | solution.py:318
  48.5 2.0 %collective-permute-start.19 = (s16[304,128]{1,0:T(8,128)(2,1)S(1)}, s16[304,128]{1,0:T(8,128)(2,1)S(1)}, u32[]{:S(2)}, u32[]{:S(2)}) collective-permute-start(s16[304,128]{1,0:T(8,128)(2,1)S(1)} %get-tuple-element.57), channel_id=1, source_target_pairs={{0,2},{1,3},{2,4},{3,5},{4,6},{5,7},{6,8},{7,9},{8,10},{9,11},{10,... | collective-permute-start | bytes 233480 | tf_op jit(solution)/shard_map/ppermute | solution.py:318
  50.9 3.3 %collective-permute-done.19.up_ref = s16[304,128]{1,0:T(8,128)(2,1)S(1)} collective-permute-done((s16[304,128]{1,0:T(8,128)(2,1)S(1)}, s16[304,128]{1,0:T(8,128)(2,1)S(1)}, u32[]{:S(2)}, u32[]{:S(2)}) %collective-permute-start.19) | collective-permute-done | bytes 77856 | tf_op jit(solution)/shard_map/ppermute | solution.py:318
  54.6 1.0 %collective-permute-start.20 = (s16[304,128]{1,0:T(8,128)(2,1)S(1)}, s16[304,128]{1,0:T(8,128)(2,1)S(1)}, u32[]{:S(2)}, u32[]{:S(2)}) collective-permute-start(s16[304,128]{1,0:T(8,128)(2,1)S(1)} %get-tuple-element.58), channel_id=1, source_target_pairs={{0,6},{1,7},{2,8},{3,9},{4,10},{5,11},{6,12},{7,13},{8,14},{9,15},... | collective-permute-start | bytes 233480 | tf_op jit(solution)/shard_map/ppermute | solution.py:318
  55.6 4.1 %collective-permute-start.21 = (s16[304,128]{1,0:T(8,128)(2,1)S(1)}, s16[304,128]{1,0:T(8,128)(2,1)S(1)}, u32[]{:S(2)}, u32[]{:S(2)}) collective-permute-start(s16[304,128]{1,0:T(8,128)(2,1)S(1)} %get-tuple-element.59), channel_id=1, source_target_pairs={{0,10},{1,11},{2,12},{3,13},{4,14},{5,15},{6,0},{7,1},{8,2},{9,3},... | collective-permute-start | bytes 233480 | tf_op jit(solution)/shard_map/ppermute | solution.py:318
  59.7 1.4 %collective-permute-start.22 = (s16[304,128]{1,0:T(8,128)(2,1)S(1)}, s16[304,128]{1,0:T(8,128)(2,1)S(1)}, u32[]{:S(2)}, u32[]{:S(2)}) collective-permute-start(s16[304,128]{1,0:T(8,128)(2,1)S(1)} %get-tuple-element.60), channel_id=1, source_target_pairs={{0,2},{1,3},{2,4},{3,5},{4,6},{5,7},{6,8},{7,9},{8,10},{9,11},{10,... | collective-permute-start | bytes 233480 | tf_op jit(solution)/shard_map/ppermute | solution.py:318
  61.8 3.1 %collective-permute-done.16.rx2_ref = s16[112,128]{1,0:T(8,128)(2,1)S(1)} collective-permute-done((s16[112,128]{1,0:T(8,128)(2,1)S(1)}, s16[112,128]{1,0:T(8,128)(2,1)S(1)}, u32[]{:S(2)}, u32[]{:S(2)}) %collective-permute-start.16) | collective-permute-done | bytes 28704 | tf_op jit(solution)/shard_map/ppermute | solution.py:318
  65.3 1.1 %layer.1 = bf16[384,256]{1,0:T(8,128)(2,1)} custom-call(f32[12416,128]{1,0:T(8,128)S(1)} %get-tuple-element.51.panel.panel_ref, s16[3872,128]{1,0:T(8,128)(2,1)S(1)} %collective-permute-done.7.rc_ref, s16[2320,128]{1,0:T(8,128)(2,1)S(1)} %collective-permute-done.15.rx_ref, f32[96,128]{1,0:T(8,128)S(1)} %get-tuple-element.53.sum_ref, ...), custom_call_target="tpu_custom_call" | custom-call | bytes 4500000 | tf_op jit(solution)/shard_map/layer/pallas_call | solution.py:33
  (39 shorter events, 9.0 us)
Async XLA Ops:
  0.0 7.0 %collective-permute-start = (bf16[384,128]{1,0:T(8,128)(2,1)}, bf16[384,128]{1,0:T(8,128)(2,1)S(1)}, u32[]{:S(2)}, u32[]{:S(2)}) collective-permute-start(bf16[384,128]{1,0:T(8,128)(2,1)} %own_ref.1), channel_id=1, source_target_pairs={{0,32},{32,0},{64,96},{96,64},{128,160},{160,128},{192,224},{224,1... | collective-permute-start | bytes 294920 | tf_op jit(solution)/shard_map/ppermute | solution.py:310
  2.1 7.2 %collective-permute-start.4 = (bf16[384,128]{1,0:T(8,128)(2,1)}, bf16[384,128]{1,0:T(8,128)(2,1)S(1)}, u32[]{:S(2)}, u32[]{:S(2)}) collective-permute-start(bf16[384,128]{1,0:T(8,128)(2,1)} %own_ref.1), channel_id=1, source_target_pairs={{0,64},{32,96},{64,128},{96,160},{128,192},{160,224},{192,0},{224,... | collective-permute-start | bytes 294920 | tf_op jit(solution)/shard_map/ppermute | solution.py:310
  3.7 9.7 %collective-permute-start.1 = (bf16[384,128]{1,0:T(8,128)(2,1)}, bf16[384,128]{1,0:T(8,128)(2,1)S(1)}, u32[]{:S(2)}, u32[]{:S(2)}) collective-permute-start(bf16[384,128]{1,0:T(8,128)(2,1)} %own_ref.1), channel_id=1, source_target_pairs={{0,192},{32,224},{64,0},{96,32},{128,64},{160,96},{192,128},{224,1... | collective-permute-start | bytes 294920 | tf_op jit(solution)/shard_map/ppermute | solution.py:310
  7.0 6.4 %collective-permute-start.3 = (bf16[384,128]{1,0:T(8,128)(2,1)S(1)}, bf16[384,128]{1,0:T(8,128)(2,1)S(1)}, u32[]{:S(2)}, u32[]{:S(2)}) collective-permute-start(bf16[384,128]{1,0:T(8,128)(2,1)S(1)} %collective-permute-done.flipped_ref), channel_id=1, source_target_pairs={{0,192},{32,224},{64,0},{96,32},{128,64},{160,96},{192,128},{224,1... | collective-permute-start | bytes 294920 | tf_op jit(solution)/shard_map/ppermute | solution.py:310
  9.3 5.8 %collective-permute-start.2 = (bf16[384,128]{1,0:T(8,128)(2,1)S(1)}, bf16[384,128]{1,0:T(8,128)(2,1)S(1)}, u32[]{:S(2)}, u32[]{:S(2)}) collective-permute-start(bf16[384,128]{1,0:T(8,128)(2,1)S(1)} %collective-permute-done.flipped_ref), channel_id=1, source_target_pairs={{0,64},{32,96},{64,128},{96,160},{128,192},{160,224},{192,0},{224,... | collective-permute-start | bytes 294920 | tf_op jit(solution)/shard_map/ppermute | solution.py:310
  9.4 6.9 %collective-permute-start.5 = (bf16[384,128]{1,0:T(8,128)(2,1)S(1)}, bf16[384,128]{1,0:T(8,128)(2,1)S(1)}, u32[]{:S(2)}, u32[]{:S(2)}) collective-permute-start(bf16[384,128]{1,0:T(8,128)(2,1)S(1)} %collective-permute-done.4.refs_0_), channel_id=1, source_target_pairs={{0,64},{32,96},{64,128},{96,160},{128,192},{160,224},{192,0},{224,... | collective-permute-start | bytes 294920 | tf_op jit(solution)/shard_map/ppermute | solution.py:310
  16.2 4.6 %collective-permute-start.6 = (bf16[384,128]{1,0:T(8,128)(2,1)S(1)}, bf16[384,128]{1,0:T(8,128)(2,1)S(1)}, u32[]{:S(2)}, u32[]{:S(2)}) collective-permute-start(bf16[384,128]{1,0:T(8,128)(2,1)S(1)} %collective-permute-done.3.refs_3_), channel_id=1, source_target_pairs={{0,192},{32,224},{64,0},{96,32},{128,64},{160,96},{192,128},{224,1... | collective-permute-start | bytes 294920 | tf_op jit(solution)/shard_map/ppermute | solution.py:310
  21.9 2.1 %collective-permute-start.14 = (s16[2320,128]{1,0:T(8,128)(2,1)S(1)}, s16[2320,128]{1,0:T(8,128)(2,1)S(1)}, u32[]{:S(2)}, u32[]{:S(2)}) collective-permute-start(s16[2320,128]{1,0:T(8,128)(2,1)S(1)} %get-tuple-element.52), channel_id=1, source_target_pairs={{0,1},{1,0},{2,3},{3,2},{4,5},{5,4},{6,7},{7,6},{8,9},{9,8},{10,11... | collective-permute-start | bytes 1781768 | tf_op jit(solution)/shard_map/ppermute | solution.py:318
  22.4 3.4 %collective-permute-start.7 = (s16[3872,128]{1,0:T(8,128)(2,1)S(1)}, s16[3872,128]{1,0:T(8,128)(2,1)S(1)}, u32[]{:S(2)}, u32[]{:S(2)}) collective-permute-start(s16[3872,128]{1,0:T(8,128)(2,1)S(1)} %core_rest.1), channel_id=1, source_target_pairs={{0,1},{1,0},{2,3},{3,2},{4,5},{5,4},{6,7},{7,6},{8,9},{9,8},{10,11... | collective-permute-start | bytes 2973704 | tf_op jit(solution)/shard_map/ppermute | solution.py:318
  24.4 23.7 %collective-permute-start.15 = (s16[2320,128]{1,0:T(8,128)(2,1)S(1)}, s16[2320,128]{1,0:T(8,128)(2,1)S(1)}, u32[]{:S(2)}, u32[]{:S(2)}) collective-permute-start(s16[2320,128]{1,0:T(8,128)(2,1)S(1)} %x_first.1), channel_id=1, source_target_pairs={{0,16},{1,17},{2,18},{3,19},{4,20},{5,21},{6,22},{7,23},{8,24},{9,... | collective-permute-start | bytes 1781768 | tf_op jit(solution)/shard_map/ppermute | solution.py:318
  25.9 11.3 %collective-permute-start.8 = (s16[400,128]{1,0:T(8,128)(2,1)S(1)}, s16[400,128]{1,0:T(8,128)(2,1)S(1)}, u32[]{:S(2)}, u32[]{:S(2)}) collective-permute-start(s16[400,128]{1,0:T(8,128)(2,1)S(1)} %get-tuple-element.44), channel_id=1, source_target_pairs={{0,14},{1,15},{2,0},{3,1},{4,2},{5,3},{6,4},{7,5},{8,6},{9,7},{10,... | collective-permute-start | bytes 307208 | tf_op jit(solution)/shard_map/ppermute | solution.py:318
  31.8 5.3 %collective-permute-start.10 = (s16[208,128]{1,0:T(8,128)(2,1)S(1)}, s16[208,128]{1,0:T(8,128)(2,1)S(1)}, u32[]{:S(2)}, u32[]{:S(2)}) collective-permute-start(s16[208,128]{1,0:T(8,128)(2,1)S(1)} %get-tuple-element.46), channel_id=1, source_target_pairs={{0,2},{1,3},{2,4},{3,5},{4,6},{5,7},{6,8},{7,9},{8,10},{9,11},{10,... | collective-permute-start | bytes 159752 | tf_op jit(solution)/shard_map/ppermute | solution.py:318
  31.8 10.8 %collective-permute-start.9 = (s16[208,128]{1,0:T(8,128)(2,1)S(1)}, s16[208,128]{1,0:T(8,128)(2,1)S(1)}, u32[]{:S(2)}, u32[]{:S(2)}) collective-permute-start(s16[208,128]{1,0:T(8,128)(2,1)S(1)} %get-tuple-element.45), channel_id=1, source_target_pairs={{0,12},{1,13},{2,14},{3,15},{4,0},{5,1},{6,2},{7,3},{8,4},{9,5},{1... | collective-permute-start | bytes 159752 | tf_op jit(solution)/shard_map/ppermute | solution.py:318
  37.3 7.9 %collective-permute-start.11 = (s16[208,128]{1,0:T(8,128)(2,1)S(1)}, s16[208,128]{1,0:T(8,128)(2,1)S(1)}, u32[]{:S(2)}, u32[]{:S(2)}) collective-permute-start(s16[208,128]{1,0:T(8,128)(2,1)S(1)} %get-tuple-element.47), channel_id=1, source_target_pairs={{0,6},{1,7},{2,8},{3,9},{4,10},{5,11},{6,12},{7,13},{8,14},{9,15},... | collective-permute-start | bytes 159752 | tf_op jit(solution)/shard_map/ppermute | solution.py:318
  38.2 7.0 %collective-permute-start.12 = (s16[208,128]{1,0:T(8,128)(2,1)S(1)}, s16[208,128]{1,0:T(8,128)(2,1)S(1)}, u32[]{:S(2)}, u32[]{:S(2)}) collective-permute-start(s16[208,128]{1,0:T(8,128)(2,1)S(1)} %get-tuple-element.48), channel_id=1, source_target_pairs={{0,10},{1,11},{2,12},{3,13},{4,14},{5,15},{6,0},{7,1},{8,2},{9,3},... | collective-permute-start | bytes 159752 | tf_op jit(solution)/shard_map/ppermute | solution.py:318
  42.6 5.3 %collective-permute-start.13 = (s16[208,128]{1,0:T(8,128)(2,1)S(1)}, s16[208,128]{1,0:T(8,128)(2,1)S(1)}, u32[]{:S(2)}, u32[]{:S(2)}) collective-permute-start(s16[208,128]{1,0:T(8,128)(2,1)S(1)} %get-tuple-element.49), channel_id=1, source_target_pairs={{0,2},{1,3},{2,4},{3,5},{4,6},{5,7},{6,8},{7,9},{8,10},{9,11},{10,... | collective-permute-start | bytes 159752 | tf_op jit(solution)/shard_map/ppermute | solution.py:318
  48.1 17.2 %copy-start.1 = (bf16[128,256]{1,0:T(8,128)(2,1)S(1)}, bf16[128,256]{1,0:T(8,128)(2,1)}, u32[]{:S(2)}) copy-start(bf16[128,256]{1,0:T(8,128)(2,1)} %refs_5_.1) | copy-start | bytes 196612
  48.4 5.9 %collective-permute-start.17 = (s16[592,128]{1,0:T(8,128)(2,1)S(1)}, s16[592,128]{1,0:T(8,128)(2,1)S(1)}, u32[]{:S(2)}, u32[]{:S(2)}) collective-permute-start(s16[592,128]{1,0:T(8,128)(2,1)S(1)} %get-tuple-element.55), channel_id=1, source_target_pairs={{0,14},{1,15},{2,0},{3,1},{4,2},{5,3},{6,4},{7,5},{8,6},{9,7},{10,... | collective-permute-start | bytes 454664 | tf_op jit(solution)/shard_map/ppermute | solution.py:318
  48.5 5.7 %collective-permute-start.19 = (s16[304,128]{1,0:T(8,128)(2,1)S(1)}, s16[304,128]{1,0:T(8,128)(2,1)S(1)}, u32[]{:S(2)}, u32[]{:S(2)}) collective-permute-start(s16[304,128]{1,0:T(8,128)(2,1)S(1)} %get-tuple-element.57), channel_id=1, source_target_pairs={{0,2},{1,3},{2,4},{3,5},{4,6},{5,7},{6,8},{7,9},{8,10},{9,11},{10,... | collective-permute-start | bytes 233480 | tf_op jit(solution)/shard_map/ppermute | solution.py:318
  50.5 14.4 %collective-permute-start.18 = (s16[304,128]{1,0:T(8,128)(2,1)S(1)}, s16[304,128]{1,0:T(8,128)(2,1)S(1)}, u32[]{:S(2)}, u32[]{:S(2)}) collective-permute-start(s16[304,128]{1,0:T(8,128)(2,1)S(1)} %get-tuple-element.56), channel_id=1, source_target_pairs={{0,12},{1,13},{2,14},{3,15},{4,0},{5,1},{6,2},{7,3},{8,4},{9,5},{1... | collective-permute-start | bytes 233480 | tf_op jit(solution)/shard_map/ppermute | solution.py:318
  54.6 10.4 %collective-permute-start.20 = (s16[304,128]{1,0:T(8,128)(2,1)S(1)}, s16[304,128]{1,0:T(8,128)(2,1)S(1)}, u32[]{:S(2)}, u32[]{:S(2)}) collective-permute-start(s16[304,128]{1,0:T(8,128)(2,1)S(1)} %get-tuple-element.58), channel_id=1, source_target_pairs={{0,6},{1,7},{2,8},{3,9},{4,10},{5,11},{6,12},{7,13},{8,14},{9,15},... | collective-permute-start | bytes 233480 | tf_op jit(solution)/shard_map/ppermute | solution.py:318
  55.6 9.4 %collective-permute-start.21 = (s16[304,128]{1,0:T(8,128)(2,1)S(1)}, s16[304,128]{1,0:T(8,128)(2,1)S(1)}, u32[]{:S(2)}, u32[]{:S(2)}) collective-permute-start(s16[304,128]{1,0:T(8,128)(2,1)S(1)} %get-tuple-element.59), channel_id=1, source_target_pairs={{0,10},{1,11},{2,12},{3,13},{4,14},{5,15},{6,0},{7,1},{8,2},{9,3},... | collective-permute-start | bytes 233480 | tf_op jit(solution)/shard_map/ppermute | solution.py:318
  59.7 5.6 %collective-permute-start.22 = (s16[304,128]{1,0:T(8,128)(2,1)S(1)}, s16[304,128]{1,0:T(8,128)(2,1)S(1)}, u32[]{:S(2)}, u32[]{:S(2)}) collective-permute-start(s16[304,128]{1,0:T(8,128)(2,1)S(1)} %get-tuple-element.60), channel_id=1, source_target_pairs={{0,2},{1,3},{2,4},{3,5},{4,6},{5,7},{6,8},{7,9},{8,10},{9,11},{10,... | collective-permute-start | bytes 233480 | tf_op jit(solution)/shard_map/ppermute | solution.py:318
  61.1 3.9 %collective-permute-start.16 = (s16[112,128]{1,0:T(8,128)(2,1)S(1)}, s16[112,128]{1,0:T(8,128)(2,1)S(1)}, u32[]{:S(2)}, u32[]{:S(2)}) collective-permute-start(s16[112,128]{1,0:T(8,128)(2,1)S(1)} %get-tuple-element.54), channel_id=1, source_target_pairs={{0,16},{1,17},{2,18},{3,19},{4,20},{5,21},{6,22},{7,23},{8,24},{9,... | collective-permute-start | bytes 86024 | tf_op jit(solution)/shard_map/ppermute | solution.py:318
  (1 other events, 0.9 us)

commit v7 on v5

--- a/solution.py
+++ b/solution.py
@@ -63,13 +63,14 @@
 
 def add_list(panel, piece, vals, lists_ref, j, k, wait=None):
     count = lists_ref[j, 0] & 63
-
-    @pl.loop(0, groups_of(count))
-    def _(g):
+    groups = groups_of(count)
+
+    def add_groups(g, many):
         if wait is not None:
-            wait(g)
+            for i in range(many):
+                wait(g + i)
         products, rows = [], []
-        for u in range(GROUP):
+        for u in range(many * GROUP):
             q = g * GROUP + u
             entry = jnp.where(q < count, lists_ref[j, q] >> 6, PANEL_BLK * 4)
             rows.append(pl.ds(pl.multiple_of((entry >> 2) * BS, BS), BS))
@@ -83,6 +84,26 @@
         for row, product in zip(rows, products):
             panel[row, :] += product
 
+    @pl.loop(0, lax.div(groups, 2))
+    def _(pair):
+        add_groups(2 * pair, 2)
+
+    @pl.when(lax.rem(groups, 2) == 1)
+    def _():
+        add_groups(groups - 1, 1)
+
+
+def add_lists(panel, arrays, pieces, vals, lists_ref, which, wait=None):
+    for k, array in enumerate(arrays):
+        pieces[k] = array[...]
+
+    @pl.loop(0, len(which))
+    def _(k):
+        j = piece_of(*which[0])
+        for i, piece in enumerate(which[1:], 1):
+            j = jnp.where(k == i, piece_of(*piece), j)
+        add_list(panel, pieces.at[k], vals, lists_ref, j, k, wait and wait(j, k))
+
 
 def group_wait(vals_ref, vals, sems, j, k):
     def wait(g):
@@ -106,7 +127,7 @@
 
 
 def first_products(which, ahead, lists_ref, own_ref, flipped_ref, vals_ref, panel, next_vals, *scratch):
-    vals, sems, next_sems = scratch
+    pieces, vals, sems, next_sems = scratch
     todo = [piece_of(*piece) for piece in which]
     for k, j in enumerate(todo):
         fetch(vals_ref, vals, sems, lists_ref, j, k)(lambda copy: copy.start())
@@ -120,16 +141,17 @@
     def _(k):
         panel[pl.ds(pl.multiple_of(k * 4 * BS, 4 * BS), 4 * BS), :] = jnp.zeros((4 * BS, F), jnp.float32)
 
-    for k, (j, piece) in enumerate(zip(todo, (own_ref, flipped_ref))):
-        add_list(panel, piece, vals, lists_ref, j, k, group_wait(vals_ref, vals, sems, j, k))
+    add_lists(
+        panel, (own_ref, flipped_ref), pieces, vals, lists_ref, which,
+        functools.partial(group_wait, vals_ref, vals, sems),
+    )
     for each in later:
         each(lambda copy: copy.wait())
 
 
-def more_products(pieces, first, lists_ref, _, vals, *refs):
-    *arrays, panel = refs
-    for k, (piece, array) in enumerate(zip(pieces, arrays)):
-        add_list(panel, array, vals, lists_ref, piece_of(*piece), first + k)
+def more_products(which, lists_ref, _, vals, *refs):
+    *arrays, panel, pieces = refs
+    add_lists(panel, arrays, pieces, vals, lists_ref, which)
 
 
 def quantize(block):
@@ -209,9 +231,9 @@
     )
 
 
-def last_products(pieces, first, *refs):
-    more_products(pieces, first, *refs[:-1])
-    core_messages(FIRST, (True,), *refs[-2:])
+def last_products(which, place, lists_ref, _, vals, piece, panel, out_ref):
+    add_list(panel, piece, vals, lists_ref, piece_of(*which), place)
+    core_messages(FIRST, (True,), panel, out_ref)
 
 
 def rest_to_core(panel, out_ref):
@@ -353,6 +375,7 @@
         (panel_type, jax.ShapeDtypeStruct((later * SLOTS, BS, BS), jnp.bfloat16)),
         [SMEM, VMEM, VMEM, ANY], (VMEM,) * 2, (lists, own, flipped, vals), 4, 40,
         scratch_shapes=[
+            pltpu.VMEM((len(here), PIECE_ROWS, F), jnp.bfloat16),
             pltpu.VMEM((2 * SLOTS, BS, BS), jnp.bfloat16),
             pltpu.SemaphoreType.DMA((2 * GROUPS,)),
             pltpu.SemaphoreType.DMA((later * GROUPS,)),
@@ -363,13 +386,14 @@
     )
     far_flipped = send_blk(above_flipped, -1)
     panel = call(
-        functools.partial(more_products, near, 0), "products_near", panel_type,
+        functools.partial(more_products, near), "products_near", panel_type,
         [SMEM] + [VMEM] * 7, VMEM,
         (lists, panel, next_vals, below, above, below_flipped, above_flipped, far_own), 3, 24,
         input_output_aliases={1: 0},
+        scratch_shapes=[pltpu.VMEM((len(near), PIECE_ROWS, F), jnp.bfloat16)],
     )
     panel, to_core = call(
-        functools.partial(last_products, far, len(near)), "products_far", (panel_type, messages(8, FIRST)),
+        functools.partial(last_products, far[0], len(near)), "products_far", (panel_type, messages(8, FIRST)),
         [SMEM] + [VMEM] * 3, (VMEM,) * 2, (lists, panel, next_vals, far_flipped), 3, 24,
         input_output_aliases={1: 0},
     )

time: 63.4 us -> 62.9 us (level)
  Pallas kernels: 10.8 us -> 8.91 us
  waiting for transfers between devices: 16.4 us -> 17.8 us
    pallas_call x12, Pallas kernels: 10.8 us -> 8.91 us  [call(): pl.pallas_call(kernel, out_shape=out_shape, in_specs=in_specs, out_specs=...]
    ppermute x7, waiting for transfers between devices: 3.25 us -> 4.91 us  [send_blk(): return lax.ppermute(array, 'blk', pairs)]
  transfers between devices with their start and end apart: 23 -> 23, of which waited for: 11 -> 10; matrix products, arithmetic and copies ran while one was open for 1% -> 1% of each run, Pallas kernels for 13% -> 10%
where the time goes in v7:
time: 62.9 us; the launch traced here: 62.7 us
  starting transfers between devices  34.2 us (54%)
  waiting for transfers between devices  17.8 us (28%)
  Pallas kernels  8.91 us (14%)
  local copies, waits for them, and re-layouts  0.9 us (1%)
  other arithmetic  0.77 us (1%)
    ppermute x16, starting transfers between devices, send_rep(): return lax.ppermute(array, 'rep', pairs)  25 us
    ppermute x16, waiting for transfers between devices, send_rep(): return lax.ppermute(array, 'rep', pairs)  12.9 us
    ppermute x7, starting transfers between devices, send_blk(): return lax.ppermute(array, 'blk', pairs)  9.23 us
    pallas_call x12, Pallas kernels, call(): pl.pallas_call(kernel, out_shape=out_shape, in_specs=in_specs, out_specs=...  8.91 us
    ppermute x7, waiting for transfers between devices, send_blk(): return lax.ppermute(array, 'blk', pairs)  4.91 us
  transfers between devices with their start and end apart: 23, of which 10 were waited for; matrix products, arithmetic and copies ran while one was open for 1% of the time, Pallas kernels for 10%

profile of v7, /device:TPU:2, one launch (start us, length us, event | category | flops | bytes accessed | tf_op | source)
XLA Modules:
  0.0 62.7 jit_solution(9059993867919276846)
XLA Ops:
  0.0 2.1 %collective-permute-start = (bf16[384,128]{1,0:T(8,128)(2,1)}, bf16[384,128]{1,0:T(8,128)(2,1)S(1)}, u32[]{:S(2)}, u32[]{:S(2)}) collective-permute-start(bf16[384,128]{1,0:T(8,128)(2,1)} %own_ref.1), channel_id=1, source_target_pairs={{0,32},{32,0},{64,96},{96,64},{128,160},{160,128},{192,224},{224,1... | collective-permute-start | bytes 294920 | tf_op jit(solution)/shard_map/ppermute | solution.py:328
  2.1 1.6 %collective-permute-start.4 = (bf16[384,128]{1,0:T(8,128)(2,1)}, bf16[384,128]{1,0:T(8,128)(2,1)S(1)}, u32[]{:S(2)}, u32[]{:S(2)}) collective-permute-start(bf16[384,128]{1,0:T(8,128)(2,1)} %own_ref.1), channel_id=1, source_target_pairs={{0,64},{32,96},{64,128},{96,160},{128,192},{160,224},{192,0},{224,... | collective-permute-start | bytes 294920 | tf_op jit(solution)/shard_map/ppermute | solution.py:328
  3.7 1.7 %collective-permute-start.1 = (bf16[384,128]{1,0:T(8,128)(2,1)}, bf16[384,128]{1,0:T(8,128)(2,1)S(1)}, u32[]{:S(2)}, u32[]{:S(2)}) collective-permute-start(bf16[384,128]{1,0:T(8,128)(2,1)} %own_ref.1), channel_id=1, source_target_pairs={{0,192},{32,224},{64,0},{96,32},{128,64},{160,96},{192,128},{224,1... | collective-permute-start | bytes 294920 | tf_op jit(solution)/shard_map/ppermute | solution.py:328
  7.0 2.3 %collective-permute-start.3 = (bf16[384,128]{1,0:T(8,128)(2,1)S(1)}, bf16[384,128]{1,0:T(8,128)(2,1)S(1)}, u32[]{:S(2)}, u32[]{:S(2)}) collective-permute-start(bf16[384,128]{1,0:T(8,128)(2,1)S(1)} %collective-permute-done.flipped_ref), channel_id=1, source_target_pairs={{0,192},{32,224},{64,0},{96,32},{128,64},{160,96},{192,128},{224,1... | collective-permute-start | bytes 294920 | tf_op jit(solution)/shard_map/ppermute | solution.py:328
  9.9 2.8 %products_here.1 = (f32[12416,128]{1,0:T(8,128)S(1)}, bf16[240,128,128]{2,1,0:T(8,128)(2,1)S(1)}) custom-call(s32[8,40]{1,0:T(8,128)S(1)} %bitcast_add_fusion.lists_ref, bf16[384,128]{1,0:T(8,128)(2,1)S(1)} %own_piece.1.own_ref, bf16[384,128]{1,0:T(8,128)(2,1)S(1)} %collective-permute-done.flipped_ref, bf16[320,128,128]{2,1,0:T(8,128)(2,1)} %bitcast.4), custom_call_target="tpu_custom_call" | custom-call | bytes 12000000 | tf_op jit(solution)/shard_map/products_here/pallas_call | solution.py:33
  12.7 2.5 %collective-permute-done.2.refs_2_ = bf16[384,128]{1,0:T(8,128)(2,1)S(1)} collective-permute-done((bf16[384,128]{1,0:T(8,128)(2,1)S(1)}, bf16[384,128]{1,0:T(8,128)(2,1)S(1)}, u32[]{:S(2)}, u32[]{:S(2)}) %collective-permute-start.2) | collective-permute-done | bytes 98336 | tf_op jit(solution)/shard_map/ppermute | solution.py:328
  17.2 2.2 %products_near.1._ = f32[12416,128]{1,0:T(8,128)S(1)} custom-call(s32[8,40]{1,0:T(8,128)S(1)} %bitcast_add_fusion.lists_ref, f32[12416,128]{1,0:T(8,128)S(1)} %get-tuple-element.37._, bf16[240,128,128]{2,1,0:T(8,128)(2,1)S(1)} %get-tuple-element.38.vals, bf16[384,128]{1,0:T(8,128)(2,1)S(1)} %collective-permute-done.4.refs_0_, ...), custom_call_target="tpu_custom_call", output_to_operand_aliasing={{}: (1, {})} | custom-call | bytes 9000000 | tf_op jit(solution)/shard_map/products_near/pallas_call | solution.py:33
  19.5 1.4 %collective-permute-done.6.piece = bf16[384,128]{1,0:T(8,128)(2,1)S(1)} collective-permute-done((bf16[384,128]{1,0:T(8,128)(2,1)S(1)}, bf16[384,128]{1,0:T(8,128)(2,1)S(1)}, u32[]{:S(2)}, u32[]{:S(2)}) %collective-permute-start.6) | collective-permute-done | bytes 98336 | tf_op jit(solution)/shard_map/ppermute | solution.py:328
  20.8 1.1 %products_far.1 = (f32[12416,128]{1,0:T(8,128)S(1)}, s16[2320,128]{1,0:T(8,128)(2,1)S(1)}) custom-call(s32[8,40]{1,0:T(8,128)S(1)} %bitcast_add_fusion.lists_ref, f32[12416,128]{1,0:T(8,128)S(1)} %products_near.1._, bf16[240,128,128]{2,1,0:T(8,128)(2,1)S(1)} %get-tuple-element.38.vals, ...), custom_call_target="tpu_custom_call", output_to_operand_aliasing={{0}: (1, {})} | custom-call | bytes 9000000 | tf_op jit(solution)/shard_map/products_far/pallas_call | solution.py:33
  22.9 1.1 %collective-permute-done.14.rc_ref = s16[2320,128]{1,0:T(8,128)(2,1)S(1)} collective-permute-done((s16[2320,128]{1,0:T(8,128)(2,1)S(1)}, s16[2320,128]{1,0:T(8,128)(2,1)S(1)}, u32[]{:S(2)}, u32[]{:S(2)}) %collective-permute-start.14) | collective-permute-done | bytes 593952 | tf_op jit(solution)/shard_map/ppermute | solution.py:336
  24.4 1.2 %collective-permute-start.15 = (s16[2320,128]{1,0:T(8,128)(2,1)S(1)}, s16[2320,128]{1,0:T(8,128)(2,1)S(1)}, u32[]{:S(2)}, u32[]{:S(2)}) collective-permute-start(s16[2320,128]{1,0:T(8,128)(2,1)S(1)} %x_first.1), channel_id=1, source_target_pairs={{0,16},{1,17},{2,18},{3,19},{4,20},{5,21},{6,22},{7,23},{8,24},{9,... | collective-permute-start | bytes 1781768 | tf_op jit(solution)/shard_map/ppermute | solution.py:336
  25.8 5.9 %collective-permute-start.8 = (s16[400,128]{1,0:T(8,128)(2,1)S(1)}, s16[400,128]{1,0:T(8,128)(2,1)S(1)}, u32[]{:S(2)}, u32[]{:S(2)}) collective-permute-start(s16[400,128]{1,0:T(8,128)(2,1)S(1)} %get-tuple-element.44), channel_id=1, source_target_pairs={{0,14},{1,15},{2,0},{3,1},{4,2},{5,3},{6,4},{7,5},{8,6},{9,7},{10,... | collective-permute-start | bytes 307208 | tf_op jit(solution)/shard_map/ppermute | solution.py:336
  31.7 2.5 %collective-permute-start.9 = (s16[208,128]{1,0:T(8,128)(2,1)S(1)}, s16[208,128]{1,0:T(8,128)(2,1)S(1)}, u32[]{:S(2)}, u32[]{:S(2)}) collective-permute-start(s16[208,128]{1,0:T(8,128)(2,1)S(1)} %get-tuple-element.45), channel_id=1, source_target_pairs={{0,12},{1,13},{2,14},{3,15},{4,0},{5,1},{6,2},{7,3},{8,4},{9,5},{1... | collective-permute-start | bytes 159752 | tf_op jit(solution)/shard_map/ppermute | solution.py:336
  34.1 2.9 %collective-permute-done.11.refs_1_ = s16[208,128]{1,0:T(8,128)(2,1)S(1)} collective-permute-done((s16[208,128]{1,0:T(8,128)(2,1)S(1)}, s16[208,128]{1,0:T(8,128)(2,1)S(1)}, u32[]{:S(2)}, u32[]{:S(2)}) %collective-permute-start.11) | collective-permute-done | bytes 53280 | tf_op jit(solution)/shard_map/ppermute | solution.py:336
  37.1 2.2 %collective-permute-start.12 = (s16[208,128]{1,0:T(8,128)(2,1)S(1)}, s16[208,128]{1,0:T(8,128)(2,1)S(1)}, u32[]{:S(2)}, u32[]{:S(2)}) collective-permute-start(s16[208,128]{1,0:T(8,128)(2,1)S(1)} %get-tuple-element.48), channel_id=1, source_target_pairs={{0,10},{1,11},{2,12},{3,13},{4,14},{5,15},{6,0},{7,1},{8,2},{9,3},... | collective-permute-start | bytes 159752 | tf_op jit(solution)/shard_map/ppermute | solution.py:336
  39.4 2.2 %collective-permute-start.13 = (s16[208,128]{1,0:T(8,128)(2,1)S(1)}, s16[208,128]{1,0:T(8,128)(2,1)S(1)}, u32[]{:S(2)}, u32[]{:S(2)}) collective-permute-start(s16[208,128]{1,0:T(8,128)(2,1)S(1)} %get-tuple-element.49), channel_id=1, source_target_pairs={{0,2},{1,3},{2,4},{3,5},{4,6},{5,7},{6,8},{7,9},{8,10},{9,11},{10,... | collective-permute-start | bytes 159752 | tf_op jit(solution)/shard_map/ppermute | solution.py:336
  41.8 2.6 %collective-permute-done.12.refs_3_ = s16[208,128]{1,0:T(8,128)(2,1)S(1)} collective-permute-done((s16[208,128]{1,0:T(8,128)(2,1)S(1)}, s16[208,128]{1,0:T(8,128)(2,1)S(1)}, u32[]{:S(2)}, u32[]{:S(2)}) %collective-permute-start.12) | collective-permute-done | bytes 53280 | tf_op jit(solution)/shard_map/ppermute | solution.py:336
  45.3 1.1 %collective-permute-start.17 = (s16[592,128]{1,0:T(8,128)(2,1)S(1)}, s16[592,128]{1,0:T(8,128)(2,1)S(1)}, u32[]{:S(2)}, u32[]{:S(2)}) collective-permute-start(s16[592,128]{1,0:T(8,128)(2,1)S(1)} %get-tuple-element.55), channel_id=1, source_target_pairs={{0,14},{1,15},{2,0},{3,1},{4,2},{5,3},{6,4},{7,5},{8,6},{9,7},{10,... | collective-permute-start | bytes 454664 | tf_op jit(solution)/shard_map/ppermute | solution.py:336
  47.4 2.6 %collective-permute-start.18 = (s16[304,128]{1,0:T(8,128)(2,1)S(1)}, s16[304,128]{1,0:T(8,128)(2,1)S(1)}, u32[]{:S(2)}, u32[]{:S(2)}) collective-permute-start(s16[304,128]{1,0:T(8,128)(2,1)S(1)} %get-tuple-element.56), channel_id=1, source_target_pairs={{0,12},{1,13},{2,14},{3,15},{4,0},{5,1},{6,2},{7,3},{8,4},{9,5},{1... | collective-permute-start | bytes 233480 | tf_op jit(solution)/shard_map/ppermute | solution.py:336
  50.7 1.9 %collective-permute-done.20.up_ref = s16[304,128]{1,0:T(8,128)(2,1)S(1)} collective-permute-done((s16[304,128]{1,0:T(8,128)(2,1)S(1)}, s16[304,128]{1,0:T(8,128)(2,1)S(1)}, u32[]{:S(2)}, u32[]{:S(2)}) %collective-permute-start.20) | collective-permute-done | bytes 77856 | tf_op jit(solution)/shard_map/ppermute | solution.py:336
  52.9 2.4 %collective-permute-start.21 = (s16[304,128]{1,0:T(8,128)(2,1)S(1)}, s16[304,128]{1,0:T(8,128)(2,1)S(1)}, u32[]{:S(2)}, u32[]{:S(2)}) collective-permute-start(s16[304,128]{1,0:T(8,128)(2,1)S(1)} %get-tuple-element.59), channel_id=1, source_target_pairs={{0,10},{1,11},{2,12},{3,13},{4,14},{5,15},{6,0},{7,1},{8,2},{9,3},... | collective-permute-start | bytes 233480 | tf_op jit(solution)/shard_map/ppermute | solution.py:336
  55.3 2.4 %collective-permute-start.22 = (s16[304,128]{1,0:T(8,128)(2,1)S(1)}, s16[304,128]{1,0:T(8,128)(2,1)S(1)}, u32[]{:S(2)}, u32[]{:S(2)}) collective-permute-start(s16[304,128]{1,0:T(8,128)(2,1)S(1)} %get-tuple-element.60), channel_id=1, source_target_pairs={{0,2},{1,3},{2,4},{3,5},{4,6},{5,7},{6,8},{7,9},{8,10},{9,11},{10,... | collective-permute-start | bytes 233480 | tf_op jit(solution)/shard_map/ppermute | solution.py:336
  57.7 3.9 %collective-permute-done.16.rx2_ref = s16[112,128]{1,0:T(8,128)(2,1)S(1)} collective-permute-done((s16[112,128]{1,0:T(8,128)(2,1)S(1)}, s16[112,128]{1,0:T(8,128)(2,1)S(1)}, u32[]{:S(2)}, u32[]{:S(2)}) %collective-permute-start.16) | collective-permute-done | bytes 28704 | tf_op jit(solution)/shard_map/ppermute | solution.py:336
  61.6 1.1 %layer.1 = bf16[384,256]{1,0:T(8,128)(2,1)} custom-call(f32[12416,128]{1,0:T(8,128)S(1)} %get-tuple-element.51.panel.panel_ref, s16[3872,128]{1,0:T(8,128)(2,1)S(1)} %collective-permute-done.7.rc_ref, s16[2320,128]{1,0:T(8,128)(2,1)S(1)} %collective-permute-done.15.rx_ref, f32[96,128]{1,0:T(8,128)S(1)} %get-tuple-element.53.sum_ref, ...), custom_call_target="tpu_custom_call" | custom-call | bytes 4500000 | tf_op jit(solution)/shard_map/layer/pallas_call | solution.py:33
  (39 shorter events, 9.1 us)
Async XLA Ops:
  0.0 7.0 %collective-permute-start = (bf16[384,128]{1,0:T(8,128)(2,1)}, bf16[384,128]{1,0:T(8,128)(2,1)S(1)}, u32[]{:S(2)}, u32[]{:S(2)}) collective-permute-start(bf16[384,128]{1,0:T(8,128)(2,1)} %own_ref.1), channel_id=1, source_target_pairs={{0,32},{32,0},{64,96},{96,64},{128,160},{160,128},{192,224},{224,1... | collective-permute-start | bytes 294920 | tf_op jit(solution)/shard_map/ppermute | solution.py:328
  2.1 7.2 %collective-permute-start.4 = (bf16[384,128]{1,0:T(8,128)(2,1)}, bf16[384,128]{1,0:T(8,128)(2,1)S(1)}, u32[]{:S(2)}, u32[]{:S(2)}) collective-permute-start(bf16[384,128]{1,0:T(8,128)(2,1)} %own_ref.1), channel_id=1, source_target_pairs={{0,64},{32,96},{64,128},{96,160},{128,192},{160,224},{192,0},{224,... | collective-permute-start | bytes 294920 | tf_op jit(solution)/shard_map/ppermute | solution.py:328
  3.7 9.0 %collective-permute-start.1 = (bf16[384,128]{1,0:T(8,128)(2,1)}, bf16[384,128]{1,0:T(8,128)(2,1)S(1)}, u32[]{:S(2)}, u32[]{:S(2)}) collective-permute-start(bf16[384,128]{1,0:T(8,128)(2,1)} %own_ref.1), channel_id=1, source_target_pairs={{0,192},{32,224},{64,0},{96,32},{128,64},{160,96},{192,128},{224,1... | collective-permute-start | bytes 294920 | tf_op jit(solution)/shard_map/ppermute | solution.py:328
  7.0 5.7 %collective-permute-start.3 = (bf16[384,128]{1,0:T(8,128)(2,1)S(1)}, bf16[384,128]{1,0:T(8,128)(2,1)S(1)}, u32[]{:S(2)}, u32[]{:S(2)}) collective-permute-start(bf16[384,128]{1,0:T(8,128)(2,1)S(1)} %collective-permute-done.flipped_ref), channel_id=1, source_target_pairs={{0,192},{32,224},{64,0},{96,32},{128,64},{160,96},{192,128},{224,1... | collective-permute-start | bytes 294920 | tf_op jit(solution)/shard_map/ppermute | solution.py:328
  9.3 5.8 %collective-permute-start.2 = (bf16[384,128]{1,0:T(8,128)(2,1)S(1)}, bf16[384,128]{1,0:T(8,128)(2,1)S(1)}, u32[]{:S(2)}, u32[]{:S(2)}) collective-permute-start(bf16[384,128]{1,0:T(8,128)(2,1)S(1)} %collective-permute-done.flipped_ref), channel_id=1, source_target_pairs={{0,64},{32,96},{64,128},{96,160},{128,192},{160,224},{192,0},{224,... | collective-permute-start | bytes 294920 | tf_op jit(solution)/shard_map/ppermute | solution.py:328
  9.4 6.9 %collective-permute-start.5 = (bf16[384,128]{1,0:T(8,128)(2,1)S(1)}, bf16[384,128]{1,0:T(8,128)(2,1)S(1)}, u32[]{:S(2)}, u32[]{:S(2)}) collective-permute-start(bf16[384,128]{1,0:T(8,128)(2,1)S(1)} %collective-permute-done.4.refs_0_), channel_id=1, source_target_pairs={{0,64},{32,96},{64,128},{96,160},{128,192},{160,224},{192,0},{224,... | collective-permute-start | bytes 294920 | tf_op jit(solution)/shard_map/ppermute | solution.py:328
  16.2 4.6 %collective-permute-start.6 = (bf16[384,128]{1,0:T(8,128)(2,1)S(1)}, bf16[384,128]{1,0:T(8,128)(2,1)S(1)}, u32[]{:S(2)}, u32[]{:S(2)}) collective-permute-start(bf16[384,128]{1,0:T(8,128)(2,1)S(1)} %collective-permute-done.3.refs_3_), channel_id=1, source_target_pairs={{0,192},{32,224},{64,0},{96,32},{128,64},{160,96},{192,128},{224,1... | collective-permute-start | bytes 294920 | tf_op jit(solution)/shard_map/ppermute | solution.py:328
  21.9 2.1 %collective-permute-start.14 = (s16[2320,128]{1,0:T(8,128)(2,1)S(1)}, s16[2320,128]{1,0:T(8,128)(2,1)S(1)}, u32[]{:S(2)}, u32[]{:S(2)}) collective-permute-start(s16[2320,128]{1,0:T(8,128)(2,1)S(1)} %get-tuple-element.52), channel_id=1, source_target_pairs={{0,1},{1,0},{2,3},{3,2},{4,5},{5,4},{6,7},{7,6},{8,9},{9,8},{10,11... | collective-permute-start | bytes 1781768 | tf_op jit(solution)/shard_map/ppermute | solution.py:336
  22.4 3.2 %collective-permute-start.7 = (s16[3872,128]{1,0:T(8,128)(2,1)S(1)}, s16[3872,128]{1,0:T(8,128)(2,1)S(1)}, u32[]{:S(2)}, u32[]{:S(2)}) collective-permute-start(s16[3872,128]{1,0:T(8,128)(2,1)S(1)} %core_rest.1), channel_id=1, source_target_pairs={{0,1},{1,0},{2,3},{3,2},{4,5},{5,4},{6,7},{7,6},{8,9},{9,8},{10,11... | collective-permute-start | bytes 2973704 | tf_op jit(solution)/shard_map/ppermute | solution.py:336
  24.4 20.4 %collective-permute-start.15 = (s16[2320,128]{1,0:T(8,128)(2,1)S(1)}, s16[2320,128]{1,0:T(8,128)(2,1)S(1)}, u32[]{:S(2)}, u32[]{:S(2)}) collective-permute-start(s16[2320,128]{1,0:T(8,128)(2,1)S(1)} %x_first.1), channel_id=1, source_target_pairs={{0,16},{1,17},{2,18},{3,19},{4,20},{5,21},{6,22},{7,23},{8,24},{9,... | collective-permute-start | bytes 1781768 | tf_op jit(solution)/shard_map/ppermute | solution.py:336
  25.8 11.2 %collective-permute-start.8 = (s16[400,128]{1,0:T(8,128)(2,1)S(1)}, s16[400,128]{1,0:T(8,128)(2,1)S(1)}, u32[]{:S(2)}, u32[]{:S(2)}) collective-permute-start(s16[400,128]{1,0:T(8,128)(2,1)S(1)} %get-tuple-element.44), channel_id=1, source_target_pairs={{0,14},{1,15},{2,0},{3,1},{4,2},{5,3},{6,4},{7,5},{8,6},{9,7},{10,... | collective-permute-start | bytes 307208 | tf_op jit(solution)/shard_map/ppermute | solution.py:336
  31.7 5.3 %collective-permute-start.11 = (s16[208,128]{1,0:T(8,128)(2,1)S(1)}, s16[208,128]{1,0:T(8,128)(2,1)S(1)}, u32[]{:S(2)}, u32[]{:S(2)}) collective-permute-start(s16[208,128]{1,0:T(8,128)(2,1)S(1)} %get-tuple-element.47), channel_id=1, source_target_pairs={{0,2},{1,3},{2,4},{3,5},{4,6},{5,7},{6,8},{7,9},{8,10},{9,11},{10,... | collective-permute-start | bytes 159752 | tf_op jit(solution)/shard_map/ppermute | solution.py:336
  31.7 9.9 %collective-permute-start.9 = (s16[208,128]{1,0:T(8,128)(2,1)S(1)}, s16[208,128]{1,0:T(8,128)(2,1)S(1)}, u32[]{:S(2)}, u32[]{:S(2)}) collective-permute-start(s16[208,128]{1,0:T(8,128)(2,1)S(1)} %get-tuple-element.45), channel_id=1, source_target_pairs={{0,12},{1,13},{2,14},{3,15},{4,0},{5,1},{6,2},{7,3},{8,4},{9,5},{1... | collective-permute-start | bytes 159752 | tf_op jit(solution)/shard_map/ppermute | solution.py:336
  34.1 7.7 %collective-permute-start.10 = (s16[208,128]{1,0:T(8,128)(2,1)S(1)}, s16[208,128]{1,0:T(8,128)(2,1)S(1)}, u32[]{:S(2)}, u32[]{:S(2)}) collective-permute-start(s16[208,128]{1,0:T(8,128)(2,1)S(1)} %get-tuple-element.46), channel_id=1, source_target_pairs={{0,6},{1,7},{2,8},{3,9},{4,10},{5,11},{6,12},{7,13},{8,14},{9,15},... | collective-permute-start | bytes 159752 | tf_op jit(solution)/shard_map/ppermute | solution.py:336
  37.1 7.3 %collective-permute-start.12 = (s16[208,128]{1,0:T(8,128)(2,1)S(1)}, s16[208,128]{1,0:T(8,128)(2,1)S(1)}, u32[]{:S(2)}, u32[]{:S(2)}) collective-permute-start(s16[208,128]{1,0:T(8,128)(2,1)S(1)} %get-tuple-element.48), channel_id=1, source_target_pairs={{0,10},{1,11},{2,12},{3,13},{4,14},{5,15},{6,0},{7,1},{8,2},{9,3},... | collective-permute-start | bytes 159752 | tf_op jit(solution)/shard_map/ppermute | solution.py:336
  39.4 5.3 %collective-permute-start.13 = (s16[208,128]{1,0:T(8,128)(2,1)S(1)}, s16[208,128]{1,0:T(8,128)(2,1)S(1)}, u32[]{:S(2)}, u32[]{:S(2)}) collective-permute-start(s16[208,128]{1,0:T(8,128)(2,1)S(1)} %get-tuple-element.49), channel_id=1, source_target_pairs={{0,2},{1,3},{2,4},{3,5},{4,6},{5,7},{6,8},{7,9},{8,10},{9,11},{10,... | collective-permute-start | bytes 159752 | tf_op jit(solution)/shard_map/ppermute | solution.py:336
  44.8 16.8 %copy-start.1 = (bf16[128,256]{1,0:T(8,128)(2,1)S(1)}, bf16[128,256]{1,0:T(8,128)(2,1)}, u32[]{:S(2)}) copy-start(bf16[128,256]{1,0:T(8,128)(2,1)} %refs_5_.1) | copy-start | bytes 196612
  45.3 7.4 %collective-permute-start.17 = (s16[592,128]{1,0:T(8,128)(2,1)S(1)}, s16[592,128]{1,0:T(8,128)(2,1)S(1)}, u32[]{:S(2)}, u32[]{:S(2)}) collective-permute-start(s16[592,128]{1,0:T(8,128)(2,1)S(1)} %get-tuple-element.55), channel_id=1, source_target_pairs={{0,14},{1,15},{2,0},{3,1},{4,2},{5,3},{6,4},{7,5},{8,6},{9,7},{10,... | collective-permute-start | bytes 454664 | tf_op jit(solution)/shard_map/ppermute | solution.py:336
  46.3 6.3 %collective-permute-start.20 = (s16[304,128]{1,0:T(8,128)(2,1)S(1)}, s16[304,128]{1,0:T(8,128)(2,1)S(1)}, u32[]{:S(2)}, u32[]{:S(2)}) collective-permute-start(s16[304,128]{1,0:T(8,128)(2,1)S(1)} %get-tuple-element.58), channel_id=1, source_target_pairs={{0,2},{1,3},{2,4},{3,5},{4,6},{5,7},{6,8},{7,9},{8,10},{9,11},{10,... | collective-permute-start | bytes 233480 | tf_op jit(solution)/shard_map/ppermute | solution.py:336
  47.4 14.2 %collective-permute-start.18 = (s16[304,128]{1,0:T(8,128)(2,1)S(1)}, s16[304,128]{1,0:T(8,128)(2,1)S(1)}, u32[]{:S(2)}, u32[]{:S(2)}) collective-permute-start(s16[304,128]{1,0:T(8,128)(2,1)S(1)} %get-tuple-element.56), channel_id=1, source_target_pairs={{0,12},{1,13},{2,14},{3,15},{4,0},{5,1},{6,2},{7,3},{8,4},{9,5},{1... | collective-permute-start | bytes 233480 | tf_op jit(solution)/shard_map/ppermute | solution.py:336
  49.9 11.7 %collective-permute-start.19 = (s16[304,128]{1,0:T(8,128)(2,1)S(1)}, s16[304,128]{1,0:T(8,128)(2,1)S(1)}, u32[]{:S(2)}, u32[]{:S(2)}) collective-permute-start(s16[304,128]{1,0:T(8,128)(2,1)S(1)} %get-tuple-element.57), channel_id=1, source_target_pairs={{0,6},{1,7},{2,8},{3,9},{4,10},{5,11},{6,12},{7,13},{8,14},{9,15},... | collective-permute-start | bytes 233480 | tf_op jit(solution)/shard_map/ppermute | solution.py:336
  52.9 8.7 %collective-permute-start.21 = (s16[304,128]{1,0:T(8,128)(2,1)S(1)}, s16[304,128]{1,0:T(8,128)(2,1)S(1)}, u32[]{:S(2)}, u32[]{:S(2)}) collective-permute-start(s16[304,128]{1,0:T(8,128)(2,1)S(1)} %get-tuple-element.59), channel_id=1, source_target_pairs={{0,10},{1,11},{2,12},{3,13},{4,14},{5,15},{6,0},{7,1},{8,2},{9,3},... | collective-permute-start | bytes 233480 | tf_op jit(solution)/shard_map/ppermute | solution.py:336
  55.3 6.3 %collective-permute-start.22 = (s16[304,128]{1,0:T(8,128)(2,1)S(1)}, s16[304,128]{1,0:T(8,128)(2,1)S(1)}, u32[]{:S(2)}, u32[]{:S(2)}) collective-permute-start(s16[304,128]{1,0:T(8,128)(2,1)S(1)} %get-tuple-element.60), channel_id=1, source_target_pairs={{0,2},{1,3},{2,4},{3,5},{4,6},{5,7},{6,8},{7,9},{8,10},{9,11},{10,... | collective-permute-start | bytes 233480 | tf_op jit(solution)/shard_map/ppermute | solution.py:336
  57.7 3.9 %collective-permute-start.16 = (s16[112,128]{1,0:T(8,128)(2,1)S(1)}, s16[112,128]{1,0:T(8,128)(2,1)S(1)}, u32[]{:S(2)}, u32[]{:S(2)}) collective-permute-start(s16[112,128]{1,0:T(8,128)(2,1)S(1)} %get-tuple-element.54), channel_id=1, source_target_pairs={{0,16},{1,17},{2,18},{3,19},{4,20},{5,21},{6,22},{7,23},{8,24},{9,... | collective-permute-start | bytes 86024 | tf_op jit(solution)/shard_map/ppermute | solution.py:336
  (1 other events, 0.9 us)

commit v8 on v7

--- a/solution.py
+++ b/solution.py
@@ -304,10 +304,19 @@
     sum_ref[...] = add(mine, *arrivals(SECOND, 0, *arrived))[0]
 
 
-def layer(panel, rc_ref, rx_ref, sum_ref, rx2_ref, *refs):
-    here = Here(panel)
-    *arrived, weight_ref, out_ref = refs
-    first = add(base_value(FIRST, here, rc_ref, rx_ref, 0, here.z), *arrivals(FIRST, 0, *arrived))
+def z_most(panel, rc_ref, rx_ref, down_ref, two_ref, far_ref, sum_ref):
+    here = Here(panel)
+    total = add(
+        base_value(FIRST, here, rc_ref, rx_ref, 0, here.z),
+        read_message(down_ref, 1, FIRST), read_message(two_ref, 0, FIRST), read_message(far_ref, 0, FIRST),
+    )
+    for i, block in enumerate(total):
+        sum_ref[i * FIRST[1] : (i + 1) * FIRST[1], :] = block
+
+
+def layer(most_ref, sum_ref, rx2_ref, three_ref, one_ref, weight_ref, out_ref):
+    first = [most_ref[i * FIRST[1] : (i + 1) * FIRST[1], :] for i in range(FIRST[2])]
+    first = add(first, read_message(three_ref, 0, FIRST), read_message(one_ref, 0, FIRST))
     second = add([sum_ref[...]], read_message(rx2_ref, 0, SECOND))
     weight = weight_ref[...]
     row = 0
@@ -415,9 +424,14 @@
     panel, to_x = lax.optimization_barrier((panel, to_x))
     rx_second = send_rep(to_x, 1, 0, 0)
     first = sum_along_z(FIRST, "first", panel, rc, rx_first)
+    down, two, far, three, one = first
+    most = call(
+        z_most, "first_most", jax.ShapeDtypeStruct((FIRST[1] * FIRST[2], F), jnp.float32), [VMEM] * 6, VMEM,
+        (panel, rc, rx_first, down, two, far), 0.3,
+    )
     return call(
-        layer, "layer", jax.ShapeDtypeStruct((PIECE_ROWS, H), jnp.bfloat16), [VMEM] * 11, VMEM,
-        (panel, rc, rx_first, own_sum, rx_second, *first, weight), 1.5,
+        layer, "layer", jax.ShapeDtypeStruct((PIECE_ROWS, H), jnp.bfloat16), [VMEM] * 6, VMEM,
+        (most, own_sum, rx_second, three, one, weight), 1.0,
     )
 
 

time: 62.9 us -> 62.6 us (level)
  waiting for transfers between devices: 17.8 us -> 16.4 us
  Pallas kernels: 8.91 us -> 9.95 us
    pallas_call x12 -> x13, Pallas kernels: 8.91 us -> 9.95 us  [call(): pl.pallas_call(kernel, out_shape=out_shape, in_specs=in_specs, out_specs=...]
    ppermute x7, waiting for transfers between devices: 4.91 us -> 3.88 us  [send_blk(): return lax.ppermute(array, 'blk', pairs)]
  transfers between devices with their start and end apart: 23 -> 23, of which waited for: 10 -> 13; matrix products, arithmetic and copies ran while one was open for 1% -> 1% of each run, Pallas kernels for 10% -> 12%
where the time goes in v8:
time: 62.6 us; the launch traced here: 62 us
  starting transfers between devices  33.9 us (54%)
  waiting for transfers between devices  16.4 us (26%)
  Pallas kernels  9.95 us (16%)
  local copies, waits for them, and re-layouts  0.9 us (1%)
  other arithmetic  0.77 us (1%)
    ppermute x16, starting transfers between devices, send_rep(): return lax.ppermute(array, 'rep', pairs)  24.7 us
    ppermute x16, waiting for transfers between devices, send_rep(): return lax.ppermute(array, 'rep', pairs)  12.5 us
    pallas_call x13, Pallas kernels, call(): pl.pallas_call(kernel, out_shape=out_shape, in_specs=in_specs, out_specs=...  9.95 us
    ppermute x7, starting transfers between devices, send_blk(): return lax.ppermute(array, 'blk', pairs)  9.23 us
    ppermute x7, waiting for transfers between devices, send_blk(): return lax.ppermute(array, 'blk', pairs)  3.88 us
  transfers between devices with their start and end apart: 23, of which 13 were waited for; matrix products, arithmetic and copies ran while one was open for 1% of the time, Pallas kernels for 12%

profile of v8, /device:TPU:2, one launch (start us, length us, event | category | flops | bytes accessed | tf_op | source)
XLA Modules:
  0.0 62.0 jit_solution(385356655483255905)
XLA Ops:
  0.0 2.1 %collective-permute-start = (bf16[384,128]{1,0:T(8,128)(2,1)}, bf16[384,128]{1,0:T(8,128)(2,1)S(1)}, u32[]{:S(2)}, u32[]{:S(2)}) collective-permute-start(bf16[384,128]{1,0:T(8,128)(2,1)} %own_ref.1), channel_id=1, source_target_pairs={{0,32},{32,0},{64,96},{96,64},{128,160},{160,128},{192,224},{224,1... | collective-permute-start | bytes 294920 | tf_op jit(solution)/shard_map/ppermute | solution.py:337
  2.1 1.6 %collective-permute-start.4 = (bf16[384,128]{1,0:T(8,128)(2,1)}, bf16[384,128]{1,0:T(8,128)(2,1)S(1)}, u32[]{:S(2)}, u32[]{:S(2)}) collective-permute-start(bf16[384,128]{1,0:T(8,128)(2,1)} %own_ref.1), channel_id=1, source_target_pairs={{0,64},{32,96},{64,128},{96,160},{128,192},{160,224},{192,0},{224,... | collective-permute-start | bytes 294920 | tf_op jit(solution)/shard_map/ppermute | solution.py:337
  3.7 1.7 %collective-permute-start.1 = (bf16[384,128]{1,0:T(8,128)(2,1)}, bf16[384,128]{1,0:T(8,128)(2,1)S(1)}, u32[]{:S(2)}, u32[]{:S(2)}) collective-permute-start(bf16[384,128]{1,0:T(8,128)(2,1)} %own_ref.1), channel_id=1, source_target_pairs={{0,192},{32,224},{64,0},{96,32},{128,64},{160,96},{192,128},{224,1... | collective-permute-start | bytes 294920 | tf_op jit(solution)/shard_map/ppermute | solution.py:337
  7.0 2.3 %collective-permute-start.3 = (bf16[384,128]{1,0:T(8,128)(2,1)S(1)}, bf16[384,128]{1,0:T(8,128)(2,1)S(1)}, u32[]{:S(2)}, u32[]{:S(2)}) collective-permute-start(bf16[384,128]{1,0:T(8,128)(2,1)S(1)} %collective-permute-done.flipped_ref), channel_id=1, source_target_pairs={{0,192},{32,224},{64,0},{96,32},{128,64},{160,96},{192,128},{224,1... | collective-permute-start | bytes 294920 | tf_op jit(solution)/shard_map/ppermute | solution.py:337
  9.9 3.2 %products_here.1 = (f32[12416,128]{1,0:T(8,128)S(1)}, bf16[240,128,128]{2,1,0:T(8,128)(2,1)S(1)}) custom-call(s32[8,40]{1,0:T(8,128)S(1)} %bitcast_add_fusion.lists_ref, bf16[384,128]{1,0:T(8,128)(2,1)S(1)} %own_piece.1.own_ref, bf16[384,128]{1,0:T(8,128)(2,1)S(1)} %collective-permute-done.flipped_ref, bf16[320,128,128]{2,1,0:T(8,128)(2,1)} %bitcast.4), custom_call_target="tpu_custom_call" | custom-call | bytes 12000000 | tf_op jit(solution)/shard_map/products_here/pallas_call | solution.py:33
  13.1 2.0 %collective-permute-done.2.refs_2_ = bf16[384,128]{1,0:T(8,128)(2,1)S(1)} collective-permute-done((bf16[384,128]{1,0:T(8,128)(2,1)S(1)}, bf16[384,128]{1,0:T(8,128)(2,1)S(1)}, u32[]{:S(2)}, u32[]{:S(2)}) %collective-permute-start.2) | collective-permute-done | bytes 98336 | tf_op jit(solution)/shard_map/ppermute | solution.py:337
  15.2 1.1 %collective-permute-done.5.refs_4_ = bf16[384,128]{1,0:T(8,128)(2,1)S(1)} collective-permute-done((bf16[384,128]{1,0:T(8,128)(2,1)S(1)}, bf16[384,128]{1,0:T(8,128)(2,1)S(1)}, u32[]{:S(2)}, u32[]{:S(2)}) %collective-permute-start.5) | collective-permute-done | bytes 98336 | tf_op jit(solution)/shard_map/ppermute | solution.py:337
  17.2 2.9 %products_near.1._ = f32[12416,128]{1,0:T(8,128)S(1)} custom-call(s32[8,40]{1,0:T(8,128)S(1)} %bitcast_add_fusion.lists_ref, f32[12416,128]{1,0:T(8,128)S(1)} %get-tuple-element.37._, bf16[240,128,128]{2,1,0:T(8,128)(2,1)S(1)} %get-tuple-element.38.vals, bf16[384,128]{1,0:T(8,128)(2,1)S(1)} %collective-permute-done.4.refs_0_, ...), custom_call_target="tpu_custom_call", output_to_operand_aliasing={{}: (1, {})} | custom-call | bytes 9000000 | tf_op jit(solution)/shard_map/products_near/pallas_call | solution.py:33
  20.8 1.1 %products_far.1 = (f32[12416,128]{1,0:T(8,128)S(1)}, s16[2320,128]{1,0:T(8,128)(2,1)S(1)}) custom-call(s32[8,40]{1,0:T(8,128)S(1)} %bitcast_add_fusion.lists_ref, f32[12416,128]{1,0:T(8,128)S(1)} %products_near.1._, bf16[240,128,128]{2,1,0:T(8,128)(2,1)S(1)} %get-tuple-element.38.vals, ...), custom_call_target="tpu_custom_call", output_to_operand_aliasing={{0}: (1, {})} | custom-call | bytes 9000000 | tf_op jit(solution)/shard_map/products_far/pallas_call | solution.py:33
  22.9 1.1 %collective-permute-done.14.rc_ref = s16[2320,128]{1,0:T(8,128)(2,1)S(1)} collective-permute-done((s16[2320,128]{1,0:T(8,128)(2,1)S(1)}, s16[2320,128]{1,0:T(8,128)(2,1)S(1)}, u32[]{:S(2)}, u32[]{:S(2)}) %collective-permute-start.14) | collective-permute-done | bytes 593952 | tf_op jit(solution)/shard_map/ppermute | solution.py:345
  24.4 1.1 %collective-permute-start.15 = (s16[2320,128]{1,0:T(8,128)(2,1)S(1)}, s16[2320,128]{1,0:T(8,128)(2,1)S(1)}, u32[]{:S(2)}, u32[]{:S(2)}) collective-permute-start(s16[2320,128]{1,0:T(8,128)(2,1)S(1)} %x_first.1), channel_id=1, source_target_pairs={{0,16},{1,17},{2,18},{3,19},{4,20},{5,21},{6,22},{7,23},{8,24},{9,... | collective-permute-start | bytes 1781768 | tf_op jit(solution)/shard_map/ppermute | solution.py:345
  25.7 5.9 %collective-permute-start.8 = (s16[400,128]{1,0:T(8,128)(2,1)S(1)}, s16[400,128]{1,0:T(8,128)(2,1)S(1)}, u32[]{:S(2)}, u32[]{:S(2)}) collective-permute-start(s16[400,128]{1,0:T(8,128)(2,1)S(1)} %get-tuple-element.44), channel_id=1, source_target_pairs={{0,14},{1,15},{2,0},{3,1},{4,2},{5,3},{6,4},{7,5},{8,6},{9,7},{10,... | collective-permute-start | bytes 307208 | tf_op jit(solution)/shard_map/ppermute | solution.py:345
  31.6 2.5 %collective-permute-start.9 = (s16[208,128]{1,0:T(8,128)(2,1)S(1)}, s16[208,128]{1,0:T(8,128)(2,1)S(1)}, u32[]{:S(2)}, u32[]{:S(2)}) collective-permute-start(s16[208,128]{1,0:T(8,128)(2,1)S(1)} %get-tuple-element.45), channel_id=1, source_target_pairs={{0,12},{1,13},{2,14},{3,15},{4,0},{5,1},{6,2},{7,3},{8,4},{9,5},{1... | collective-permute-start | bytes 159752 | tf_op jit(solution)/shard_map/ppermute | solution.py:345
  34.2 2.8 %collective-permute-done.11.refs_1_ = s16[208,128]{1,0:T(8,128)(2,1)S(1)} collective-permute-done((s16[208,128]{1,0:T(8,128)(2,1)S(1)}, s16[208,128]{1,0:T(8,128)(2,1)S(1)}, u32[]{:S(2)}, u32[]{:S(2)}) %collective-permute-start.11) | collective-permute-done | bytes 53280 | tf_op jit(solution)/shard_map/ppermute | solution.py:345
  37.1 2.3 %collective-permute-start.12 = (s16[208,128]{1,0:T(8,128)(2,1)S(1)}, s16[208,128]{1,0:T(8,128)(2,1)S(1)}, u32[]{:S(2)}, u32[]{:S(2)}) collective-permute-start(s16[208,128]{1,0:T(8,128)(2,1)S(1)} %get-tuple-element.48), channel_id=1, source_target_pairs={{0,10},{1,11},{2,12},{3,13},{4,14},{5,15},{6,0},{7,1},{8,2},{9,3},... | collective-permute-start | bytes 159752 | tf_op jit(solution)/shard_map/ppermute | solution.py:345
  39.4 2.2 %collective-permute-start.13 = (s16[208,128]{1,0:T(8,128)(2,1)S(1)}, s16[208,128]{1,0:T(8,128)(2,1)S(1)}, u32[]{:S(2)}, u32[]{:S(2)}) collective-permute-start(s16[208,128]{1,0:T(8,128)(2,1)S(1)} %get-tuple-element.49), channel_id=1, source_target_pairs={{0,2},{1,3},{2,4},{3,5},{4,6},{5,7},{6,8},{7,9},{8,10},{9,11},{10,... | collective-permute-start | bytes 159752 | tf_op jit(solution)/shard_map/ppermute | solution.py:345
  41.9 2.3 %collective-permute-done.12.refs_3_ = s16[208,128]{1,0:T(8,128)(2,1)S(1)} collective-permute-done((s16[208,128]{1,0:T(8,128)(2,1)S(1)}, s16[208,128]{1,0:T(8,128)(2,1)S(1)}, u32[]{:S(2)}, u32[]{:S(2)}) %collective-permute-start.12) | collective-permute-done | bytes 53280 | tf_op jit(solution)/shard_map/ppermute | solution.py:345
  46.3 1.1 %collective-permute-start.20 = (s16[304,128]{1,0:T(8,128)(2,1)S(1)}, s16[304,128]{1,0:T(8,128)(2,1)S(1)}, u32[]{:S(2)}, u32[]{:S(2)}) collective-permute-start(s16[304,128]{1,0:T(8,128)(2,1)S(1)} %get-tuple-element.58), channel_id=1, source_target_pairs={{0,2},{1,3},{2,4},{3,5},{4,6},{5,7},{6,8},{7,9},{8,10},{9,11},{10,... | collective-permute-start | bytes 233480 | tf_op jit(solution)/shard_map/ppermute | solution.py:345
  47.4 2.7 %collective-permute-start.17 = (s16[304,128]{1,0:T(8,128)(2,1)S(1)}, s16[304,128]{1,0:T(8,128)(2,1)S(1)}, u32[]{:S(2)}, u32[]{:S(2)}) collective-permute-start(s16[304,128]{1,0:T(8,128)(2,1)S(1)} %get-tuple-element.54), channel_id=1, source_target_pairs={{0,12},{1,13},{2,14},{3,15},{4,0},{5,1},{6,2},{7,3},{8,4},{9,5},{1... | collective-permute-start | bytes 233480 | tf_op jit(solution)/shard_map/ppermute | solution.py:345
  50.7 1.9 %collective-permute-done.20.up_ref = s16[304,128]{1,0:T(8,128)(2,1)S(1)} collective-permute-done((s16[304,128]{1,0:T(8,128)(2,1)S(1)}, s16[304,128]{1,0:T(8,128)(2,1)S(1)}, u32[]{:S(2)}, u32[]{:S(2)}) %collective-permute-start.20) | collective-permute-done | bytes 77856 | tf_op jit(solution)/shard_map/ppermute | solution.py:345
  52.8 2.6 %collective-permute-start.21 = (s16[304,128]{1,0:T(8,128)(2,1)S(1)}, s16[304,128]{1,0:T(8,128)(2,1)S(1)}, u32[]{:S(2)}, u32[]{:S(2)}) collective-permute-start(s16[304,128]{1,0:T(8,128)(2,1)S(1)} %get-tuple-element.59), channel_id=1, source_target_pairs={{0,10},{1,11},{2,12},{3,13},{4,14},{5,15},{6,0},{7,1},{8,2},{9,3},... | collective-permute-start | bytes 233480 | tf_op jit(solution)/shard_map/ppermute | solution.py:345
  56.3 1.0 %collective-permute-start.19 = (s16[112,128]{1,0:T(8,128)(2,1)S(1)}, s16[112,128]{1,0:T(8,128)(2,1)S(1)}, u32[]{:S(2)}, u32[]{:S(2)}) collective-permute-start(s16[112,128]{1,0:T(8,128)(2,1)S(1)} %get-tuple-element.57), channel_id=1, source_target_pairs={{0,16},{1,17},{2,18},{3,19},{4,20},{5,21},{6,22},{7,23},{8,24},{9,... | collective-permute-start | bytes 86024 | tf_op jit(solution)/shard_map/ppermute | solution.py:345
  57.3 1.7 %collective-permute-done.18.far_ref = s16[304,128]{1,0:T(8,128)(2,1)S(1)} collective-permute-done((s16[304,128]{1,0:T(8,128)(2,1)S(1)}, s16[304,128]{1,0:T(8,128)(2,1)S(1)}, u32[]{:S(2)}, u32[]{:S(2)}) %collective-permute-start.18) | collective-permute-done | bytes 77856 | tf_op jit(solution)/shard_map/ppermute | solution.py:345
  59.2 1.0 %collective-permute-done.19.rx2_ref = s16[112,128]{1,0:T(8,128)(2,1)S(1)} collective-permute-done((s16[112,128]{1,0:T(8,128)(2,1)S(1)}, s16[112,128]{1,0:T(8,128)(2,1)S(1)}, u32[]{:S(2)}, u32[]{:S(2)}) %collective-permute-start.19) | collective-permute-done | bytes 28704 | tf_op jit(solution)/shard_map/ppermute | solution.py:345
  (40 shorter events, 11.8 us)
Async XLA Ops:
  0.0 7.0 %collective-permute-start = (bf16[384,128]{1,0:T(8,128)(2,1)}, bf16[384,128]{1,0:T(8,128)(2,1)S(1)}, u32[]{:S(2)}, u32[]{:S(2)}) collective-permute-start(bf16[384,128]{1,0:T(8,128)(2,1)} %own_ref.1), channel_id=1, source_target_pairs={{0,32},{32,0},{64,96},{96,64},{128,160},{160,128},{192,224},{224,1... | collective-permute-start | bytes 294920 | tf_op jit(solution)/shard_map/ppermute | solution.py:337
  2.1 7.2 %collective-permute-start.4 = (bf16[384,128]{1,0:T(8,128)(2,1)}, bf16[384,128]{1,0:T(8,128)(2,1)S(1)}, u32[]{:S(2)}, u32[]{:S(2)}) collective-permute-start(bf16[384,128]{1,0:T(8,128)(2,1)} %own_ref.1), channel_id=1, source_target_pairs={{0,64},{32,96},{64,128},{96,160},{128,192},{160,224},{192,0},{224,... | collective-permute-start | bytes 294920 | tf_op jit(solution)/shard_map/ppermute | solution.py:337
  3.7 9.4 %collective-permute-start.1 = (bf16[384,128]{1,0:T(8,128)(2,1)}, bf16[384,128]{1,0:T(8,128)(2,1)S(1)}, u32[]{:S(2)}, u32[]{:S(2)}) collective-permute-start(bf16[384,128]{1,0:T(8,128)(2,1)} %own_ref.1), channel_id=1, source_target_pairs={{0,192},{32,224},{64,0},{96,32},{128,64},{160,96},{192,128},{224,1... | collective-permute-start | bytes 294920 | tf_op jit(solution)/shard_map/ppermute | solution.py:337
  7.0 6.1 %collective-permute-start.3 = (bf16[384,128]{1,0:T(8,128)(2,1)S(1)}, bf16[384,128]{1,0:T(8,128)(2,1)S(1)}, u32[]{:S(2)}, u32[]{:S(2)}) collective-permute-start(bf16[384,128]{1,0:T(8,128)(2,1)S(1)} %collective-permute-done.flipped_ref), channel_id=1, source_target_pairs={{0,192},{32,224},{64,0},{96,32},{128,64},{160,96},{192,128},{224,1... | collective-permute-start | bytes 294920 | tf_op jit(solution)/shard_map/ppermute | solution.py:337
  9.3 5.8 %collective-permute-start.2 = (bf16[384,128]{1,0:T(8,128)(2,1)S(1)}, bf16[384,128]{1,0:T(8,128)(2,1)S(1)}, u32[]{:S(2)}, u32[]{:S(2)}) collective-permute-start(bf16[384,128]{1,0:T(8,128)(2,1)S(1)} %collective-permute-done.flipped_ref), channel_id=1, source_target_pairs={{0,64},{32,96},{64,128},{96,160},{128,192},{160,224},{192,0},{224,... | collective-permute-start | bytes 294920 | tf_op jit(solution)/shard_map/ppermute | solution.py:337
  9.4 6.9 %collective-permute-start.5 = (bf16[384,128]{1,0:T(8,128)(2,1)S(1)}, bf16[384,128]{1,0:T(8,128)(2,1)S(1)}, u32[]{:S(2)}, u32[]{:S(2)}) collective-permute-start(bf16[384,128]{1,0:T(8,128)(2,1)S(1)} %collective-permute-done.4.refs_0_), channel_id=1, source_target_pairs={{0,64},{32,96},{64,128},{96,160},{128,192},{160,224},{192,0},{224,... | collective-permute-start | bytes 294920 | tf_op jit(solution)/shard_map/ppermute | solution.py:337
  16.2 4.6 %collective-permute-start.6 = (bf16[384,128]{1,0:T(8,128)(2,1)S(1)}, bf16[384,128]{1,0:T(8,128)(2,1)S(1)}, u32[]{:S(2)}, u32[]{:S(2)}) collective-permute-start(bf16[384,128]{1,0:T(8,128)(2,1)S(1)} %collective-permute-done.3.refs_3_), channel_id=1, source_target_pairs={{0,192},{32,224},{64,0},{96,32},{128,64},{160,96},{192,128},{224,1... | collective-permute-start | bytes 294920 | tf_op jit(solution)/shard_map/ppermute | solution.py:337
  21.9 2.1 %collective-permute-start.14 = (s16[2320,128]{1,0:T(8,128)(2,1)S(1)}, s16[2320,128]{1,0:T(8,128)(2,1)S(1)}, u32[]{:S(2)}, u32[]{:S(2)}) collective-permute-start(s16[2320,128]{1,0:T(8,128)(2,1)S(1)} %get-tuple-element.52), channel_id=1, source_target_pairs={{0,1},{1,0},{2,3},{3,2},{4,5},{5,4},{6,7},{7,6},{8,9},{9,8},{10,11... | collective-permute-start | bytes 1781768 | tf_op jit(solution)/shard_map/ppermute | solution.py:345
  22.4 3.1 %collective-permute-start.7 = (s16[3872,128]{1,0:T(8,128)(2,1)S(1)}, s16[3872,128]{1,0:T(8,128)(2,1)S(1)}, u32[]{:S(2)}, u32[]{:S(2)}) collective-permute-start(s16[3872,128]{1,0:T(8,128)(2,1)S(1)} %core_rest.1), channel_id=1, source_target_pairs={{0,1},{1,0},{2,3},{3,2},{4,5},{5,4},{6,7},{7,6},{8,9},{9,8},{10,11... | collective-permute-start | bytes 2973704 | tf_op jit(solution)/shard_map/ppermute | solution.py:345
  24.4 20.5 %collective-permute-start.15 = (s16[2320,128]{1,0:T(8,128)(2,1)S(1)}, s16[2320,128]{1,0:T(8,128)(2,1)S(1)}, u32[]{:S(2)}, u32[]{:S(2)}) collective-permute-start(s16[2320,128]{1,0:T(8,128)(2,1)S(1)} %x_first.1), channel_id=1, source_target_pairs={{0,16},{1,17},{2,18},{3,19},{4,20},{5,21},{6,22},{7,23},{8,24},{9,... | collective-permute-start | bytes 1781768 | tf_op jit(solution)/shard_map/ppermute | solution.py:345
  25.7 11.3 %collective-permute-start.8 = (s16[400,128]{1,0:T(8,128)(2,1)S(1)}, s16[400,128]{1,0:T(8,128)(2,1)S(1)}, u32[]{:S(2)}, u32[]{:S(2)}) collective-permute-start(s16[400,128]{1,0:T(8,128)(2,1)S(1)} %get-tuple-element.44), channel_id=1, source_target_pairs={{0,14},{1,15},{2,0},{3,1},{4,2},{5,3},{6,4},{7,5},{8,6},{9,7},{10,... | collective-permute-start | bytes 307208 | tf_op jit(solution)/shard_map/ppermute | solution.py:345
  31.6 5.3 %collective-permute-start.11 = (s16[208,128]{1,0:T(8,128)(2,1)S(1)}, s16[208,128]{1,0:T(8,128)(2,1)S(1)}, u32[]{:S(2)}, u32[]{:S(2)}) collective-permute-start(s16[208,128]{1,0:T(8,128)(2,1)S(1)} %get-tuple-element.47), channel_id=1, source_target_pairs={{0,2},{1,3},{2,4},{3,5},{4,6},{5,7},{6,8},{7,9},{8,10},{9,11},{10,... | collective-permute-start | bytes 159752 | tf_op jit(solution)/shard_map/ppermute | solution.py:345
  31.6 9.9 %collective-permute-start.9 = (s16[208,128]{1,0:T(8,128)(2,1)S(1)}, s16[208,128]{1,0:T(8,128)(2,1)S(1)}, u32[]{:S(2)}, u32[]{:S(2)}) collective-permute-start(s16[208,128]{1,0:T(8,128)(2,1)S(1)} %get-tuple-element.45), channel_id=1, source_target_pairs={{0,12},{1,13},{2,14},{3,15},{4,0},{5,1},{6,2},{7,3},{8,4},{9,5},{1... | collective-permute-start | bytes 159752 | tf_op jit(solution)/shard_map/ppermute | solution.py:345
  34.2 7.7 %collective-permute-start.10 = (s16[208,128]{1,0:T(8,128)(2,1)S(1)}, s16[208,128]{1,0:T(8,128)(2,1)S(1)}, u32[]{:S(2)}, u32[]{:S(2)}) collective-permute-start(s16[208,128]{1,0:T(8,128)(2,1)S(1)} %get-tuple-element.46), channel_id=1, source_target_pairs={{0,6},{1,7},{2,8},{3,9},{4,10},{5,11},{6,12},{7,13},{8,14},{9,15},... | collective-permute-start | bytes 159752 | tf_op jit(solution)/shard_map/ppermute | solution.py:345
  37.1 7.1 %collective-permute-start.12 = (s16[208,128]{1,0:T(8,128)(2,1)S(1)}, s16[208,128]{1,0:T(8,128)(2,1)S(1)}, u32[]{:S(2)}, u32[]{:S(2)}) collective-permute-start(s16[208,128]{1,0:T(8,128)(2,1)S(1)} %get-tuple-element.48), channel_id=1, source_target_pairs={{0,10},{1,11},{2,12},{3,13},{4,14},{5,15},{6,0},{7,1},{8,2},{9,3},... | collective-permute-start | bytes 159752 | tf_op jit(solution)/shard_map/ppermute | solution.py:345
  39.4 5.3 %collective-permute-start.13 = (s16[208,128]{1,0:T(8,128)(2,1)S(1)}, s16[208,128]{1,0:T(8,128)(2,1)S(1)}, u32[]{:S(2)}, u32[]{:S(2)}) collective-permute-start(s16[208,128]{1,0:T(8,128)(2,1)S(1)} %get-tuple-element.49), channel_id=1, source_target_pairs={{0,2},{1,3},{2,4},{3,5},{4,6},{5,7},{6,8},{7,9},{8,10},{9,11},{10,... | collective-permute-start | bytes 159752 | tf_op jit(solution)/shard_map/ppermute | solution.py:345
  45.3 7.3 %collective-permute-start.16 = (s16[592,128]{1,0:T(8,128)(2,1)S(1)}, s16[592,128]{1,0:T(8,128)(2,1)S(1)}, u32[]{:S(2)}, u32[]{:S(2)}) collective-permute-start(s16[592,128]{1,0:T(8,128)(2,1)S(1)} %get-tuple-element.53), channel_id=1, source_target_pairs={{0,14},{1,15},{2,0},{3,1},{4,2},{5,3},{6,4},{7,5},{8,6},{9,7},{10,... | collective-permute-start | bytes 454664 | tf_op jit(solution)/shard_map/ppermute | solution.py:345
  46.3 6.3 %collective-permute-start.20 = (s16[304,128]{1,0:T(8,128)(2,1)S(1)}, s16[304,128]{1,0:T(8,128)(2,1)S(1)}, u32[]{:S(2)}, u32[]{:S(2)}) collective-permute-start(s16[304,128]{1,0:T(8,128)(2,1)S(1)} %get-tuple-element.58), channel_id=1, source_target_pairs={{0,2},{1,3},{2,4},{3,5},{4,6},{5,7},{6,8},{7,9},{8,10},{9,11},{10,... | collective-permute-start | bytes 233480 | tf_op jit(solution)/shard_map/ppermute | solution.py:345
  47.4 9.9 %collective-permute-start.17 = (s16[304,128]{1,0:T(8,128)(2,1)S(1)}, s16[304,128]{1,0:T(8,128)(2,1)S(1)}, u32[]{:S(2)}, u32[]{:S(2)}) collective-permute-start(s16[304,128]{1,0:T(8,128)(2,1)S(1)} %get-tuple-element.54), channel_id=1, source_target_pairs={{0,12},{1,13},{2,14},{3,15},{4,0},{5,1},{6,2},{7,3},{8,4},{9,5},{1... | collective-permute-start | bytes 233480 | tf_op jit(solution)/shard_map/ppermute | solution.py:345
  50.1 11.0 %copy-start.1 = (bf16[128,256]{1,0:T(8,128)(2,1)S(1)}, bf16[128,256]{1,0:T(8,128)(2,1)}, u32[]{:S(2)}) copy-start(bf16[128,256]{1,0:T(8,128)(2,1)} %weight_ref.1) | copy-start | bytes 196612
  50.1 9.0 %collective-permute-start.18 = (s16[304,128]{1,0:T(8,128)(2,1)S(1)}, s16[304,128]{1,0:T(8,128)(2,1)S(1)}, u32[]{:S(2)}, u32[]{:S(2)}) collective-permute-start(s16[304,128]{1,0:T(8,128)(2,1)S(1)} %get-tuple-element.55), channel_id=1, source_target_pairs={{0,6},{1,7},{2,8},{3,9},{4,10},{5,11},{6,12},{7,13},{8,14},{9,15},... | collective-permute-start | bytes 233480 | tf_op jit(solution)/shard_map/ppermute | solution.py:345
  52.8 7.7 %collective-permute-start.21 = (s16[304,128]{1,0:T(8,128)(2,1)S(1)}, s16[304,128]{1,0:T(8,128)(2,1)S(1)}, u32[]{:S(2)}, u32[]{:S(2)}) collective-permute-start(s16[304,128]{1,0:T(8,128)(2,1)S(1)} %get-tuple-element.59), channel_id=1, source_target_pairs={{0,10},{1,11},{2,12},{3,13},{4,14},{5,15},{6,0},{7,1},{8,2},{9,3},... | collective-permute-start | bytes 233480 | tf_op jit(solution)/shard_map/ppermute | solution.py:345
  55.4 5.6 %collective-permute-start.22 = (s16[304,128]{1,0:T(8,128)(2,1)S(1)}, s16[304,128]{1,0:T(8,128)(2,1)S(1)}, u32[]{:S(2)}, u32[]{:S(2)}) collective-permute-start(s16[304,128]{1,0:T(8,128)(2,1)S(1)} %get-tuple-element.60), channel_id=1, source_target_pairs={{0,2},{1,3},{2,4},{3,5},{4,6},{5,7},{6,8},{7,9},{8,10},{9,11},{10,... | collective-permute-start | bytes 233480 | tf_op jit(solution)/shard_map/ppermute | solution.py:345
  56.3 3.9 %collective-permute-start.19 = (s16[112,128]{1,0:T(8,128)(2,1)S(1)}, s16[112,128]{1,0:T(8,128)(2,1)S(1)}, u32[]{:S(2)}, u32[]{:S(2)}) collective-permute-start(s16[112,128]{1,0:T(8,128)(2,1)S(1)} %get-tuple-element.57), channel_id=1, source_target_pairs={{0,16},{1,17},{2,18},{3,19},{4,20},{5,21},{6,22},{7,23},{8,24},{9,... | collective-permute-start | bytes 86024 | tf_op jit(solution)/shard_map/ppermute | solution.py:345
  (1 other events, 0.9 us)
